TPU v7x, 256 devices: a whole 4x4x8 slice. The times are simulated.
256 devices in a mesh: qr: 16 (over y, x), pc: 16 (over z, core).
Axes of the slice: x: 4, y: 4, z: 8, core: 2. Of those that a mesh axis runs over, the one named last changes fastest.
Arguments:
- query_pool: bfloat16 [16384, 4096], P(('qr', 'pc')), may hold values from -14 to 14
- passage_pool: bfloat16 [16384, 4096], P(('pc', 'qr')), may hold values from -14 to 14
- proj: bfloat16 [4096, 1024], replicated, may hold values from -0.09375 to 0.09375
- positive: int32 [16384], P(('qr', 'pc')), may hold values from 0 to 16383, as said below
Outputs:
- loss: float32 [], replicated
- grad_query_pool: float32 [16384, 4096], P(('qr', 'pc'))
- grad_passage_pool: float32 [16384, 4096], P(('pc', 'qr'))
Inputs may be any that keep to these rules, and one draw needn't show every extreme that they name: Every passage is the positive of exactly one query.
All inputs are finite; a program needn't handle non-finite values.
Results may differ from a plain program's by a relative error of at most 0.023.
Values may be sent and summed in bfloat16 or wider, within the bound.
No kernel may reach another device: no remote copies, remote signals or barrier semaphores. Data moves between devices by JAX's collectives and lax.ppermute only.
A program may use at most 64 MiB of HBM per device.

v0:
```python
import jax
import jax.numpy as jnp
from jax import lax
from jax.sharding import PartitionSpec as P

logit_scale = 20.0
grad_scale = 128.0
norm_eps = 1e-06


def embed_rows(pool, proj):
    raw_rows = jnp.dot(pool, proj, preferred_element_type=jnp.float32)
    inv_rows = lax.rsqrt(jnp.sum(raw_rows * raw_rows, axis=-1, keepdims=True) + norm_eps)
    return (raw_rows, inv_rows)


def normal_back(raw_rows, inv_rows, incoming):
    unit_rows = raw_rows * inv_rows
    return inv_rows * (incoming - unit_rows * jnp.sum(unit_rows * incoming, axis=-1, keepdims=True))


def body(query_pool, passage_pool, proj, positive):
    qr_size = lax.axis_size("qr")
    qr_index = lax.axis_index("qr")
    pc_index = lax.axis_index("pc")
    own_rows = query_pool.shape[0]
    raw_query, inv_query = embed_rows(query_pool, proj)
    raw_passage, inv_passage = embed_rows(passage_pool, proj)
    query_embed = (raw_query * inv_query).astype(jnp.bfloat16)
    passage_embed = (raw_passage * inv_passage).astype(jnp.bfloat16)
    query_tile, positive_tile = (
        lax.all_gather(query_embed, "pc", axis=0, tiled=True),
        lax.all_gather(positive, "pc", axis=0, tiled=True),
    )
    passage_tile = lax.all_gather(passage_embed, "qr", axis=0, tiled=True)
    tile_rows = query_tile.shape[0]
    tile_cols = passage_tile.shape[0]
    logits = logit_scale * lax.dot_general(
        query_tile, passage_tile, (((1,), (1,)), ((), ())), preferred_element_type=jnp.float32
    )
    shifted = jnp.exp(logits - logit_scale)
    row_part = jnp.sum(shifted, axis=1)
    column_part = jnp.sum(shifted, axis=0)
    row_sum = lax.psum(row_part, "pc")
    column_sum = lax.psum(column_part, "qr")
    row_lse = logit_scale + jnp.log(row_sum)
    column_lse = logit_scale + jnp.log(column_sum)
    local_column = positive_tile - pc_index * tile_cols
    inside = (local_column >= 0) & (local_column < tile_cols)
    picked = jnp.take_along_axis(logits, jnp.clip(local_column, 0, tile_cols - 1)[:, None], axis=1)[
        :, 0
    ]
    positive_sum = jnp.sum(jnp.where(inside, picked, 0.0))
    row_share = lax.dynamic_slice_in_dim(row_lse, pc_index * own_rows, own_rows)
    column_share = lax.dynamic_slice_in_dim(column_lse, qr_index * own_rows, own_rows)
    local_term = jnp.sum(row_share) + jnp.sum(column_share) - 2.0 * positive_sum
    loss = lax.psum(local_term, ("qr", "pc")) / (2.0 * tile_rows * qr_size)
    onehot = (lax.broadcasted_iota(jnp.int32, logits.shape, 1) == local_column[:, None]).astype(
        jnp.float32
    )
    grad_tile = grad_scale * (
        0.5 * (jnp.exp(logits - row_lse[:, None]) + jnp.exp(logits - column_lse[None, :])) - onehot
    )
    grad_tile = grad_tile.astype(jnp.bfloat16)
    query_partial = logit_scale * jnp.dot(
        grad_tile, passage_tile, preferred_element_type=jnp.float32
    )
    passage_partial = logit_scale * lax.dot_general(
        grad_tile, query_tile, (((0,), (0,)), ((), ())), preferred_element_type=jnp.float32
    )
    grad_query_embed = lax.psum_scatter(
        query_partial.astype(jnp.bfloat16), "pc", scatter_dimension=0, tiled=True
    ).astype(jnp.float32)
    grad_passage_embed = lax.psum_scatter(
        passage_partial.astype(jnp.bfloat16), "qr", scatter_dimension=0, tiled=True
    ).astype(jnp.float32)
    grad_raw_query = normal_back(raw_query, inv_query, grad_query_embed).astype(jnp.bfloat16)
    grad_raw_passage = normal_back(raw_passage, inv_passage, grad_passage_embed).astype(
        jnp.bfloat16
    )
    grad_query_pool = lax.dot_general(
        grad_raw_query, proj, (((1,), (1,)), ((), ())), preferred_element_type=jnp.float32
    )
    grad_passage_pool = lax.dot_general(
        grad_raw_passage, proj, (((1,), (1,)), ((), ())), preferred_element_type=jnp.float32
    )
    return (loss, grad_query_pool, grad_passage_pool)


def solution(mesh):
    in_specs = (P(("qr", "pc"), None), P(("pc", "qr"), None), P(), P(("qr", "pc")))
    out_specs = (P(), P(("qr", "pc"), None), P(("pc", "qr"), None))
    return jax.shard_map(body, mesh=mesh, in_specs=in_specs, out_specs=out_specs, check_vma=False)
```

profile of v0, /device:TPU:2, one launch (start us, length us, event | category | flops | bytes accessed | tf_op | source)
XLA Modules:
  0.0 346.2 jit_solution(9601942360084313286)
XLA Ops:
  7.2 0.0 all-gather.3.cloned.1.call-start
  7.2 1.0 copy-done
  8.2 5.1 %multiply_reduce_fusion.1 = (f32[64]{0:T(128)S(1)}, f32[64,1024]{1,0:T(8,128)S(1)}) fusion(bf16[64,4096]{1,0:T(8,128)(2,1)S(1)} %copy-done, bf16[4096,1024]{1,0:T(8,128)(2,1)} %param.6), kind=kOutput, calls=%fused_computation.20 | convolution fusion | flops 537001920 | bytes 9175296 | tf_op jit(solution)/shard_map/dot_general | solution.py:12
  13.3 0.8 multiply_convert_fusion.4
  14.1 0.0 all-gather.5.cloned.1.call-start
  14.1 5.1 %multiply_reduce_fusion = (f32[64]{0:T(128)S(1)}, f32[64,1024]{1,0:T(8,128)S(1)}) fusion(bf16[64,4096]{1,0:T(8,128)(2,1)S(1)} %copy-done.1, bf16[4096,1024]{1,0:T(8,128)(2,1)} %param.6), kind=kOutput, calls=%fused_computation.19 | convolution fusion | flops 537001920 | bytes 9175296 | tf_op jit(solution)/shard_map/dot_general | solution.py:12
  19.2 0.8 multiply_convert_fusion.3
  20.0 0.0 all-gather.5.cloned.1.call-update
  20.0 0.0 reduce-scatter.5.cloned.1.call-start
  20.1 0.6 dynamic-slice
  21.3 0.2 dynamic-update-slice
  21.6 16.5 %all-reduce = s32[1024]{0:T(1024)S(1)} all-reduce(s32[1024]{0:T(1024)S(1)} %dynamic-update-slice), channel_id=1, replica_groups=mesh['qr'=16,'pc'=16] {'pc'}, use_global_device_ids=true, to_apply=%add | all-reduce | flops 1024 | bytes 8192
  38.1 18.7 %all-gather.3.cloned.1.call-done = bf16[1024,1024]{1,0:T(8,128)(2,1)} async-done(((bf16[64,1024]{1,0:T(8,128)(2,1)}), bf16[1024,1024]{1,0:T(8,128)(2,1)}) %all-gather.3.cloned.1.call-update) | async-done | bytes 2097168 | tf_op jit(solution)/shard_map/all_gather | solution.py:32
  56.7 51.1 %all-gather.5.cloned.1.call-done = bf16[1024,1024]{1,0:T(8,128)(2,1)} async-done(((bf16[64,1024]{1,0:T(8,128)(2,1)}), bf16[1024,1024]{1,0:T(8,128)(2,1)}) %all-gather.5.cloned.1.call-update) | async-done | bytes 2097168 | tf_op jit(solution)/shard_map/all_gather | solution.py:35
  107.9 6.8 %fusion = (f32[1024]{0:T(1024)S(1)}, f32[1024]{0:T(1024)S(1)}, f32[1024,1024]{1,0:T(8,128)}) fusion(bf16[1024,1024]{1,0:T(8,128)(2,1)} %all-gather.3.cloned.1.call-done, bf16[1024,1024]{1,0:T(8,128)(2,1)} %all-gather.5.cloned.1.call-done), kind=kOutput, calls=%fused_computation.6 | convolution fusion | flops 2151675904 | bytes 8396800 | tf_op jit(solution)/shard_map/dot_general | solution.py:38
  114.7 36.3 %psum.22 = f32[1024]{0:T(1024)S(1)} all-reduce(f32[1024]{0:T(1024)S(1)} %get-tuple-element.3), channel_id=1, replica_groups=mesh['qr'=16,'pc'=16] {'qr'}, use_global_device_ids=true, to_apply=%region_6.7 | all-reduce | flops 1024 | bytes 8192 | tf_op jit(solution)/shard_map/psum | solution.py:45
  151.0 23.6 %psum.21 = f32[1024]{0:T(1024)S(1)} all-reduce(f32[1024]{0:T(1024)S(1)} %get-tuple-element.4), channel_id=1, replica_groups=mesh['qr'=16,'pc'=16] {'pc'}, use_global_device_ids=true, to_apply=%region_3.0 | all-reduce | flops 1024 | bytes 8192 | tf_op jit(solution)/shard_map/psum | solution.py:44
  174.5 3.8 %multiply_convert_fusion.2 = bf16[1024,1024]{1,0:T(8,128)(2,1)S(1)} fusion(f32[1024,1024]{1,0:T(8,128)} %get-tuple-element.11, s32[1024]{0:T(1024)S(1)} %get-tuple-element.6, f32[1024]{0:T(1024)S(1)} %log_add_fusion, f32[1024]{0:T(1024)S(1)} %log_add_fusion.1), kind=kLoop, calls=%fused_computation.3 | loop fusion | flops 9437184 | bytes 6303744 | tf_op jit(solution)/shard_map/convert_element_type | solution.py:64
  178.4 5.3 %multiply_convert_fusion = bf16[1024,1024]{1,0:T(8,128)(2,1)} fusion(bf16[1024,1024]{1,0:T(8,128)(2,1)S(1)} %multiply_convert_fusion.2, bf16[1024,1024]{1,0:T(8,128)(2,1)} %all-gather.3.cloned.1.call-done), kind=kOutput, calls=%fused_computation.1 | convolution fusion | flops 2149580800 | bytes 6291456 | tf_op jit(solution)/shard_map/dot_general | solution.py:68
  183.7 0.0 reduce-scatter.3.cloned.1.call-start
  183.8 5.3 %multiply_convert_fusion.1 = bf16[1024,1024]{1,0:T(8,128)(2,1)} fusion(bf16[1024,1024]{1,0:T(8,128)(2,1)S(1)} %multiply_convert_fusion.2, bf16[1024,1024]{1,0:T(8,128)(2,1)} %all-gather.5.cloned.1.call-done), kind=kOutput, calls=%fused_computation.2 | convolution fusion | flops 2149580800 | bytes 6291456 | tf_op jit(solution)/shard_map/dot_general | solution.py:65
  189.2 16.9 %gather_fusion = f32[1024]{0:T(1024)S(1)} fusion(f32[1024,1024]{1,0:T(8,128)} %get-tuple-element.11, s32[1024]{0:T(1024)S(1)} %bitcast.17), kind=kCustom, calls=%fused_computation | custom fusion | bytes 16384 | tf_op jit(solution)/shard_map/jit(take_along_axis)/gather | solution.py:50
  206.1 0.7 dynamic-slice_reduce_fusion
  206.8 0.7 dynamic-slice_reduce_fusion.1
  207.4 0.6 select_reduce_fusion
  210.0 75.0 %psum.23 = f32[]{:T(128)} all-reduce(f32[]{:T(128)S(6)} %sub.40), channel_id=1, replica_groups=mesh['qr'=16,'pc'=16] {'qr','pc'}, use_global_device_ids=true, to_apply=%region_9.10 | all-reduce | flops 1 | bytes 8 | tf_op jit(solution)/shard_map/psum | solution.py:57
  285.6 0.0 reduce-scatter.5.cloned.1.call-done
  285.7 1.1 fusion.5
  286.8 36.4 %reduce-scatter.3.cloned.1.call-done = bf16[64,1024]{1,0:T(8,128)(2,1)} async-done(((bf16[1024,1024]{1,0:T(8,128)(2,1)}), bf16[64,1024]{1,0:T(8,128)(2,1)}) %reduce-scatter.3.cloned.1.call-update) | async-done | bytes 131088 | tf_op jit(solution)/shard_map/reduce_scatter | solution.py:71
  323.2 1.1 fusion.2
  324.3 7.1 %fusion.10 = f32[64,4096]{1,0:T(8,128)} fusion(bf16[4096,1024]{1,0:T(8,128)(2,1)} %param.6, bf16[64,1024]{1,0:T(8,128)(2,1)} %reduce-scatter.3.cloned.1.call-done, f32[64,1024]{1,0:T(8,128)S(1)} %get-tuple-element.8, f32[64]{0:T(128)S(1)} %fusion.2, f32[64]{0:T(128)S(1)} %add_rsqrt_fusion.1), kind=kOutput, calls=%fused_computation.24 | convolution fusion | flops 537264128 | bytes 9830912 | tf_op jit(solution)/shard_map/dot_general | solution.py:81
  331.5 7.0 %fusion.8 = f32[64,4096]{1,0:T(8,128)} fusion(bf16[4096,1024]{1,0:T(8,128)(2,1)} %param.6, bf16[64,1024]{1,0:T(8,128)(2,1)S(1)} %copy-done.2, f32[64,1024]{1,0:T(8,128)S(1)} %get-tuple-element.10, f32[64]{0:T(128)S(1)} %fusion.5, f32[64]{0:T(128)S(1)} %add_rsqrt_fusion), kind=kOutput, calls=%fused_computation.23 | convolution fusion | flops 537264128 | bytes 9830912 | tf_op jit(solution)/shard_map/dot_general | solution.py:84
  (21 shorter events, 0.2 us)
Async XLA Ops:
  7.2 1.0 copy-start
  7.2 7.0 %copy-start.1 = (bf16[64,4096]{1,0:T(8,128)(2,1)S(1)}, bf16[64,4096]{1,0:T(8,128)(2,1)}, u32[]{:S(2)}) copy-start(bf16[64,4096]{1,0:T(8,128)(2,1)} %param.5) | copy-start | bytes 1572868
  7.2 49.5 %all-gather.3.cloned.1.call-start = ((), (), s32[]{:S(2)}) async-start(), calls=%async_computation.2 | async-start | bytes 2228224 | tf_op jit(solution)/shard_map/all_gather | solution.py:32
  14.1 6.0 %copy-start.4 = (u32[256]{0:T(256)S(1)}, u32[256]{0:T(256)}, u32[]{:S(2)}) copy-start(u32[256]{0:T(256)} %constant.66) | copy-start | bytes 3076
  14.1 7.2 %copy-start.3 = (s32[64]{0:T(128)S(1)}, s32[64]{0:T(128)}, u32[]{:S(2)}) copy-start(s32[64]{0:T(128)} %param.7) | copy-start | bytes 772
  14.1 93.8 %all-gather.5.cloned.1.call-start = ((), (), s32[]{:S(2)}) async-start(), calls=%async_computation.3 | async-start | bytes 2228224 | tf_op jit(solution)/shard_map/all_gather | solution.py:35
  20.0 265.7 %reduce-scatter.5.cloned.1.call-start = ((), (), s32[]{:S(2)}) async-start(), calls=%async_computation.5 | async-start | bytes 2228224 | tf_op jit(solution)/shard_map/reduce_scatter | solution.py:74
  183.7 139.5 %reduce-scatter.3.cloned.1.call-start = ((), (), s32[]{:S(2)}) async-start(), calls=%async_computation.4 | async-start | bytes 2228224 | tf_op jit(solution)/shard_map/reduce_scatter | solution.py:71
  324.3 7.2 %copy-start.2 = (bf16[64,1024]{1,0:T(8,128)(2,1)S(1)}, bf16[64,1024]{1,0:T(8,128)(2,1)}, u32[]{:S(2)}) copy-start(bf16[64,1024]{1,0:T(8,128)(2,1)} %reduce-scatter.5.cloned.1.call-done) | copy-start | bytes 393220
Sparse Core Ops, SparseCore 0:
  14.2 42.4 all-gather.2
  59.7 48.0 all-gather.4
  183.8 77.6 reduce-scatter.4
  264.1 59.0 reduce-scatter.2
where the time goes:
time: 347 us; the launch traced here: 346 us
  blocking collectives  151 us (44%)
  waiting for transfers between devices  106 us (31%)
  matrix products  41.7 us (12%)
  local copies, waits for them, and re-layouts  18.8 us (5%)
  between operations  18.3 us (5%)
  other arithmetic  9.57 us (3%)
    psum x1, blocking collectives, body(): loss = lax.psum(local_term, ('qr', 'pc')) / (2.0 * tile_rows * qr_size)  75 us
    all_gather x1, waiting for transfers between devices, body(): passage_tile = lax.all_gather(passage_embed, 'qr', axis=0, tiled=True)  51.1 us
    reduce_scatter x1, waiting for transfers between devices, body(): lax.psum_scatter(query_partial.astype(jnp.bfloat16), 'pc', scatter_dimens...  36.4 us
    psum x1, blocking collectives, body(): column_sum = lax.psum(column_part, 'qr')  36.3 us
    psum x1, blocking collectives, body(): row_sum = lax.psum(row_part, 'pc')  23.6 us
    all_gather x1, waiting for transfers between devices, body(): lax.all_gather(query_embed, 'pc', axis=0, tiled=True)  18.7 us
    gather x1, local copies, waits for them, and re-layouts, body(): jnp.take_along_axis(logits, jnp.clip(local_column, 0, tile_cols - 1)[:, N...  16.9 us
    unnamed x1, blocking collectives  16.5 us
  transfers between devices with their start and end apart: 4, of which 3 were waited for; matrix products, arithmetic and copies ran while one was open for 9% of the time, Pallas kernels for 0%

commit v1 on v0

v1 whole, which is shorter than its diff:
```python
import jax
import jax.numpy as jnp
from jax import lax
from jax.sharding import Mesh, PartitionSpec as P

logit_scale = 20.0
grad_scale = 128.0
norm_eps = 1e-06

NY, NX, NZ, NC = 4, 4, 8, 2
QR = ("y", "x")
PC = ("z", "c")
f32 = jnp.float32
bf16 = jnp.bfloat16


def shift(value, axis, size, step):
    return lax.ppermute(value, axis, [(i, (i + step) % size) for i in range(size)])


def swap(value, axis, size, bit):
    return lax.ppermute(value, axis, [(i, i ^ bit) for i in range(size)])


pc_steps = (("c", NC, 1), ("z", NZ, 1), ("z", NZ, 2), ("z", NZ, 4))
qr_steps = (("x", NX, 1), ("x", NX, 2), ("y", NY, 1), ("y", NY, 2))


def embed_rows(pool, proj):
    raw_rows = jnp.dot(pool, proj, preferred_element_type=f32)
    inv_rows = lax.rsqrt(jnp.sum(raw_rows * raw_rows, axis=-1, keepdims=True) + norm_eps)
    return (raw_rows, inv_rows)


def normal_back(raw_rows, inv_rows, incoming):
    unit_rows = raw_rows * inv_rows
    return inv_rows * (incoming - unit_rows * jnp.sum(unit_rows * incoming, axis=-1, keepdims=True))


def scatter_z(blocks, z_index):
    def block(k):
        return lax.dynamic_index_in_dim(blocks, (z_index + k) % NZ, 0, keepdims=False)

    far = block(NZ // 2)
    half = far.shape[0] // 2
    down = shift(far[:half], "z", NZ, -1)
    up = shift(far[half:], "z", NZ, 1)
    down = jnp.concatenate([down.astype(f32), jnp.zeros(down.shape, f32)], axis=0)
    up = jnp.concatenate([jnp.zeros(up.shape, f32), up.astype(f32)], axis=0)
    for k in range(NZ // 2 - 1, 0, -1):
        down = shift((block(NZ - k).astype(f32) + down).astype(bf16), "z", NZ, -1).astype(f32)
        up = shift((block(k).astype(f32) + up).astype(bf16), "z", NZ, 1).astype(f32)
    return block(0).astype(f32) + down + up


def body(query_pool, passage_pool, proj, positive):
    z_index = lax.axis_index("z")
    c_index = lax.axis_index("c")
    pc_index = z_index * NC + c_index
    own_rows = query_pool.shape[0]
    raw_query, inv_query = embed_rows(query_pool, proj)
    query_embed = (raw_query * inv_query).astype(bf16)
    query_tile = lax.all_gather(query_embed, PC, axis=0, tiled=True)
    raw_passage, inv_passage = embed_rows(passage_pool, proj)
    passage_embed = (raw_passage * inv_passage).astype(bf16)
    passage_tile = lax.all_to_all(jnp.tile(passage_embed, (NY * NX, 1)), QR, 0, 0, tiled=True)
    positive_tile = lax.all_gather(positive, PC, axis=0, tiled=True)
    tile_rows = query_tile.shape[0]
    tile_cols = passage_tile.shape[0]
    width = query_tile.shape[1]
    logits = logit_scale * lax.dot_general(
        query_tile, passage_tile, (((1,), (1,)), ((), ())), preferred_element_type=f32
    )
    shifted = jnp.exp(logits - logit_scale)
    row_sum = jnp.sum(shifted, axis=1)
    column_sum = jnp.sum(shifted, axis=0)
    for pc_step, qr_step in zip(pc_steps, qr_steps):
        row_sum = row_sum + swap(row_sum, *pc_step)
        column_sum = column_sum + swap(column_sum, *qr_step)
    row_lse = logit_scale + jnp.log(row_sum)
    column_lse = logit_scale + jnp.log(column_sum)
    local_column = positive_tile - pc_index * tile_cols
    onehot = lax.broadcasted_iota(jnp.int32, logits.shape, 1) == local_column[:, None]
    positive_sum = jnp.sum(jnp.where(onehot, logits, 0.0))
    loss = (
        jnp.sum(row_lse) / (NZ * NC) + jnp.sum(column_lse) / (NY * NX) - 2.0 * positive_sum
    ).reshape(1)
    for step in pc_steps + qr_steps:
        loss = loss + swap(loss, *step)
    loss = loss[0] / (2.0 * tile_rows * NY * NX)
    grad_tile = grad_scale * (
        0.5 * (jnp.exp(logits - row_lse[:, None]) + jnp.exp(logits - column_lse[None, :]))
        - onehot.astype(f32)
    )
    grad_tile = grad_tile.astype(bf16)
    query_partial = (
        logit_scale * jnp.dot(grad_tile, passage_tile, preferred_element_type=f32)
    ).astype(bf16)
    passage_partial = (
        logit_scale
        * lax.dot_general(
            grad_tile, query_tile, (((0,), (0,)), ((), ())), preferred_element_type=f32
        )
    ).astype(bf16)
    passage_terms = lax.all_to_all(passage_partial, QR, 0, 0, tiled=True)
    grad_passage_embed = jnp.sum(
        passage_terms.reshape(NY * NX, own_rows, width).astype(f32), axis=0
    )
    query_parts = query_partial.reshape(NZ, NC, own_rows, width)
    other = swap(lax.dynamic_index_in_dim(query_parts, 1 - c_index, 1, keepdims=False), "c", NC, 1)
    own = lax.dynamic_index_in_dim(query_parts, c_index, 1, keepdims=False)
    blocks = (own.astype(f32) + other.astype(f32)).astype(bf16)
    grad_query_embed = scatter_z(blocks, z_index)
    grad_raw_query = normal_back(raw_query, inv_query, grad_query_embed).astype(bf16)
    grad_raw_passage = normal_back(raw_passage, inv_passage, grad_passage_embed).astype(bf16)
    grad_query_pool = lax.dot_general(
        grad_raw_query, proj, (((1,), (1,)), ((), ())), preferred_element_type=f32
    )
    grad_passage_pool = lax.dot_general(
        grad_raw_passage, proj, (((1,), (1,)), ((), ())), preferred_element_type=f32
    )
    return (loss, grad_query_pool, grad_passage_pool)


def solution(mesh):
    fine = Mesh(mesh.devices.reshape(NY, NX, NZ, NC), ("y", "x", "z", "c"))
    in_specs = (
        P(("y", "x", "z", "c"), None),
        P(("z", "c", "y", "x"), None),
        P(),
        P(("y", "x", "z", "c")),
    )
    out_specs = (P(), P(("y", "x", "z", "c"), None), P(("z", "c", "y", "x"), None))
    return jax.shard_map(
        body, mesh=fine, in_specs=in_specs, out_specs=out_specs, check_vma=False
    )
```

time: 347 us -> 208 us (0.60)
  blocking collectives: 151 us -> 16.4 us
  starting transfers between devices: 0.16 us -> 65.1 us
  waiting for transfers between devices: 106 us -> 44.6 us
  local copies, waits for them, and re-layouts: 18.8 us -> 5.5 us
  between operations: 18.3 us -> 22.8 us
  other arithmetic: 9.57 us -> 13.8 us
    psum x3 -> x0, blocking collectives: 135 us -> none  [the longest x1 75 us: body(): loss = lax.psum(local_term, ('qr', 'pc')) / (2.0 * tile_rows * qr_size)]
    all_gather x2 -> x1, waiting for transfers between devices: 69.8 us -> 1.31 us  [body(): query_tile = lax.all_gather(query_embed, PC, axis=0, tiled=True)]
    ppermute x0 -> x25, starting transfers between devices: none -> 51.7 us  [the longest x17 40.6 us: swap(): return lax.ppermute(value, axis, [(i, i ^ bit) for i in range(size)])]
    reduce_scatter x2 -> x0, waiting for transfers between devices: 36.4 us -> none  [the longest x1 36.4 us: body(): lax.psum_scatter(query_partial.astype(jnp.bfloat16), 'pc', scatter_dimens...]
    ppermute x0 -> x25, waiting for transfers between devices: none -> 34 us  [the longest x17 19.4 us: swap(): return lax.ppermute(value, axis, [(i, i ^ bit) for i in range(size)])]
    gather x1 -> x0, local copies, waits for them, and re-layouts: 16.9 us -> none  [body(): jnp.take_along_axis(logits, jnp.clip(local_column, 0, tile_cols - 1)[:, N...]
    all_to_all x0 -> x2, starting transfers between devices: none -> 13.4 us  [the longest x1 7.48 us: body(): lax.all_to_all(jnp.tile(passage_embed, (NY * NX, 1)), QR, 0, 0, tiled=True)]
    all_to_all x0 -> x2, waiting for transfers between devices: none -> 9.23 us  [the longest x1 9.22 us: body(): lax.all_to_all(jnp.tile(passage_embed, (NY * NX, 1)), QR, 0, 0, tiled=True)]
  transfers between devices with their start and end apart: 4 -> 28, of which waited for: 3 -> 19; matrix products, arithmetic and copies ran while one was open for 9% -> 13% of each run, Pallas kernels for 0% -> 0%
where the time goes in v1:
time: 208 us
  starting transfers between devices  65.1 us (31%)
  waiting for transfers between devices  44.6 us (21%)
  matrix products  39.7 us (19%)
  between operations  22.8 us (11%)
  blocking collectives  16.4 us (8%)
  other arithmetic  13.8 us (7%)
  local copies, waits for them, and re-layouts  5.5 us (3%)
    ppermute x17, starting transfers between devices, swap(): return lax.ppermute(value, axis, [(i, i ^ bit) for i in range(size)])  40.6 us
    ppermute x17, waiting for transfers between devices, swap(): return lax.ppermute(value, axis, [(i, i ^ bit) for i in range(size)])  19.4 us
    unnamed x1, blocking collectives  16.4 us
    ppermute x8, waiting for transfers between devices, shift(): lax.ppermute(value, axis, [(i, (i + step) % size) for i in range(size)])  14.7 us
    ppermute x8, starting transfers between devices, shift(): lax.ppermute(value, axis, [(i, (i + step) % size) for i in range(size)])  11.1 us
    dot_general x2, matrix products, embed_rows(): raw_rows = jnp.dot(pool, proj, preferred_element_type=f32)  10.1 us
    all_to_all x1, waiting for transfers between devices, body(): lax.all_to_all(jnp.tile(passage_embed, (NY * NX, 1)), QR, 0, 0, tiled=True)  9.22 us
    all_to_all x1, starting transfers between devices, body(): lax.all_to_all(jnp.tile(passage_embed, (NY * NX, 1)), QR, 0, 0, tiled=True)  7.48 us
  transfers between devices with their start and end apart: 28, of which 19 were waited for; matrix products, arithmetic and copies ran while one was open for 13% of the time, Pallas kernels for 0%

profile of v1, /device:TPU:2, one launch (start us, length us, event | category | flops | bytes accessed | tf_op | source)
XLA Modules:
  0.0 207.8 jit_solution(14063545679672824924)
XLA Ops:
  8.2 5.1 %multiply_reduce_fusion.3 = (f32[64]{0:T(128)S(1)}, f32[64,1024]{1,0:T(8,128)S(1)}) fusion(bf16[64,4096]{1,0:T(8,128)(2,1)S(1)} %copy-done, bf16[4096,1024]{1,0:T(8,128)(2,1)} %param.6), kind=kOutput, calls=%fused_computation.31 | convolution fusion | flops 537001920 | bytes 9175296 | tf_op jit(solution)/shard_map/dot_general | solution.py:30
  14.1 5.1 %multiply_reduce_fusion.2 = (f32[64]{0:T(128)S(1)}, f32[64,1024]{1,0:T(8,128)S(1)}) fusion(bf16[64,4096]{1,0:T(8,128)(2,1)S(1)} %copy-done.4, bf16[4096,1024]{1,0:T(8,128)(2,1)} %param.6), kind=kOutput, calls=%fused_computation.30 | convolution fusion | flops 537001920 | bytes 9175296 | tf_op jit(solution)/shard_map/dot_general | solution.py:30
  20.9 7.5 %all-to-all-start = ((bf16[16,64,1024]{2,1,0:T(8,128)(2,1)}), bf16[16,64,1024]{2,1,0:T(8,128)(2,1)S(1)}, u32[]{:S(2)}, u32[]{:S(2)}) async-start(bf16[16,64,1024]{2,1,0:T(8,128)(2,1)} %tile.2), calls=%async_computation | async-start | bytes 4194304 | tf_op jit(solution)/shard_map/all_to_all | solution.py:66
  29.9 16.4 %all-reduce.2 = s32[1024]{0:T(1024)S(1)} all-reduce(s32[1024]{0:T(1024)S(1)} %dynamic-update-slice), channel_id=1, replica_groups=mesh['y'=4,'x'=4,'z'=8,'c'=2] {'z','c'}, use_global_device_ids=true, to_apply=%add.2 | all-reduce | flops 1024 | bytes 8192
  46.2 9.2 %all-to-all-done = bf16[16,64,1024]{2,1,0:T(8,128)(2,1)S(1)} async-done(((bf16[16,64,1024]{2,1,0:T(8,128)(2,1)}), bf16[16,64,1024]{2,1,0:T(8,128)(2,1)S(1)}, u32[]{:S(2)}, u32[]{:S(2)}) %all-to-all-start) | async-done | bytes 2097184 | tf_op jit(solution)/shard_map/all_to_all | solution.py:66
  56.8 7.1 %select_reduce_fusion = (f32[]{:T(128)}, f32[1024]{0:T(1024)S(1)}, f32[1024]{0:T(1024)S(1)}, f32[1024,1024]{1,0:T(8,128)}) fusion(s32[1024]{0:T(1024)S(1)} %broadcast_subtract_fusion, bf16[1024,1024]{1,0:T(8,128)(2,1)} %all-gather.2.cloned.1.call-done, bf16[1024,1024]{1,0:T(8,128)(2,1)S(1)} %bitcast.57), kind=kOutput, calls=%fused_computation.4 | convolution fusion | flops 2154821632 | bytes 8400900 | tf_op jit(solution)/shard_map/dot_general | solution.py:71
  64.1 3.1 %collective-permute-start.4 = (f32[1024]{0:T(1024)S(1)}, f32[1024]{0:T(1024)S(1)}, u32[]{:S(2)}, u32[]{:S(2)}) collective-permute-start(f32[1024]{0:T(1024)S(1)} %get-tuple-element.4), channel_id=1, source_target_pairs={{0,16},{16,0},{32,48},{48,32},{1,17},{17,1},{33,49},{49,33},{2,18}... | collective-permute-start | bytes 12296 | tf_op jit(solution)/shard_map/ppermute | solution.py:22
  70.8 3.3 %collective-permute-start.2 = (f32[1024]{0:T(1024)S(1)}, f32[1024]{0:T(1024)S(1)}, u32[]{:S(2)}, u32[]{:S(2)}) collective-permute-start(f32[1024]{0:T(1024)S(1)} %add.194), channel_id=1, source_target_pairs={{0,4},{2,6},{4,0},{6,2},{8,12},{10,14},{12,8},{14,10},{1,5},{3,7},... | collective-permute-start | bytes 12296 | tf_op jit(solution)/shard_map/ppermute | solution.py:22
  75.7 6.9 %collective-permute-start.3 = (f32[1024]{0:T(1024)S(1)}, f32[1024]{0:T(1024)S(1)}, u32[]{:S(2)}, u32[]{:S(2)}) collective-permute-start(f32[1024]{0:T(1024)S(1)} %add.195), channel_id=1, source_target_pairs={{0,8},{2,10},{4,12},{6,14},{8,0},{10,2},{12,4},{14,6},{1,9},{3,11}... | collective-permute-start | bytes 12296 | tf_op jit(solution)/shard_map/ppermute | solution.py:22
  84.8 2.8 %collective-permute-done.7 = f32[1024]{0:T(1024)S(1)} collective-permute-done((f32[1024]{0:T(1024)S(1)}, f32[1024]{0:T(1024)S(1)}, u32[]{:S(2)}, u32[]{:S(2)}) %collective-permute-start.7) | collective-permute-done | bytes 4128 | tf_op jit(solution)/shard_map/ppermute | solution.py:22
  88.3 3.8 %multiply_convert_fusion.2 = bf16[1024,1024]{1,0:T(8,128)(2,1)S(1)} fusion(f32[1024,1024]{1,0:T(8,128)} %get-tuple-element.18, f32[1024]{0:T(1024)S(1)} %get-tuple-element.7, f32[1024]{0:T(1024)S(1)} %get-tuple-element.9, s32[1024]{0:T(1024)S(1)} %broadcast_subtract_fusion), kind=kLoop, calls=%fused_computation.3 | loop fusion | flops 10485760 | bytes 6303744 | tf_op jit(solution)/shard_map/convert_element_type | solution.py:95
  92.1 2.3 %multiply_convert_fusion.1 = bf16[1024,1024]{1,0:T(8,128)(2,1)S(1)} fusion(bf16[1024,1024]{1,0:T(8,128)(2,1)S(1)} %multiply_convert_fusion.2, bf16[1024,1024]{1,0:T(8,128)(2,1)S(1)} %bitcast.58), kind=kOutput, calls=%fused_computation.2 | convolution fusion | flops 2149580800 | bytes 6291456 | tf_op jit(solution)/shard_map/dot_general | solution.py:97
  96.0 2.6 %collective-permute-done.16 = bf16[8,64,1024]{2,1,0:T(8,128)(2,1)S(1)} collective-permute-done((bf16[8,64,1024]{2,1,0:T(8,128)(2,1)S(1)}, bf16[8,64,1024]{2,1,0:T(8,128)(2,1)S(1)}, u32[]{:S(2)}, u32[]{:S(2)}) %collective-permute-start.16) | collective-permute-done | bytes 1048608 | tf_op jit(solution)/shard_map/ppermute | solution.py:22
  102.0 2.6 %collective-permute-done.17 = bf16[32,1024]{1,0:T(8,128)(2,1)S(1)} collective-permute-done((bf16[32,1024]{1,0:T(8,128)(2,1)S(1)}, bf16[32,1024]{1,0:T(8,128)(2,1)S(1)}, u32[]{:S(2)}, u32[]{:S(2)}) %collective-permute-start.17) | collective-permute-done | bytes 65568 | tf_op jit(solution)/shard_map/ppermute | solution.py:18
  104.7 2.9 %collective-permute-start.18 = (bf16[64,1024]{1,0:T(8,128)(2,1)S(1)}, bf16[64,1024]{1,0:T(8,128)(2,1)S(1)}, u32[]{:S(2)}, u32[]{:S(2)}) collective-permute-start(bf16[64,1024]{1,0:T(8,128)(2,1)S(1)} %fusion.6), channel_id=1, source_target_pairs={{0,14},{2,0},{4,2},{6,4},{8,6},{10,8},{12,10},{14,12},{1,15},{3,1}... | collective-permute-start | bytes 393224 | tf_op jit(solution)/shard_map/ppermute | solution.py:18
  107.6 6.0 %multiply_convert_fusion = bf16[1024,1024]{1,0:T(8,128)(2,1)} fusion(bf16[1024,1024]{1,0:T(8,128)(2,1)} %copy-done.3, bf16[1024,1024]{1,0:T(8,128)(2,1)} %all-gather.2.cloned.1.call-done), kind=kOutput, calls=%fused_computation.1 | convolution fusion | flops 2149580800 | bytes 6291456 | tf_op jit(solution)/shard_map/dot_general | solution.py:101
  113.6 5.9 %all-to-all-start.1 = ((bf16[16,64,1024]{2,1,0:T(8,128)(2,1)}), bf16[16,64,1024]{2,1,0:T(8,128)(2,1)S(1)}, u32[]{:S(2)}, u32[]{:S(2)}) async-start(bf16[16,64,1024]{2,1,0:T(8,128)(2,1)} %bitcast.56), calls=%async_computation.1 | async-start | bytes 4194304 | tf_op jit(solution)/shard_map/all_to_all | solution.py:105
  120.5 2.0 collective-permute-start.21
  122.5 3.5 %collective-permute-done.21 = bf16[32,1024]{1,0:T(8,128)(2,1)S(1)} collective-permute-done((bf16[32,1024]{1,0:T(8,128)(2,1)S(1)}, bf16[32,1024]{1,0:T(8,128)(2,1)S(1)}, u32[]{:S(2)}, u32[]{:S(2)}) %collective-permute-start.21) | collective-permute-done | bytes 65568 | tf_op jit(solution)/shard_map/ppermute | solution.py:18
  129.1 5.5 %collective-permute-done.22 = bf16[64,1024]{1,0:T(8,128)(2,1)S(1)} collective-permute-done((bf16[64,1024]{1,0:T(8,128)(2,1)S(1)}, bf16[64,1024]{1,0:T(8,128)(2,1)S(1)}, u32[]{:S(2)}, u32[]{:S(2)}) %collective-permute-start.22) | collective-permute-done | bytes 131104 | tf_op jit(solution)/shard_map/ppermute | solution.py:18
  135.6 3.2 %collective-permute-start.20 = (bf16[64,1024]{1,0:T(8,128)(2,1)}, bf16[64,1024]{1,0:T(8,128)(2,1)S(1)}, u32[]{:S(2)}, u32[]{:S(2)}) collective-permute-start(bf16[64,1024]{1,0:T(8,128)(2,1)} %get-tuple-element.10), channel_id=1, source_target_pairs={{0,14},{2,0},{4,2},{6,4},{8,6},{10,8},{12,10},{14,12},{1,15},{3,1}... | collective-permute-start | bytes 393224 | tf_op jit(solution)/shard_map/ppermute | solution.py:18
  138.8 3.0 %collective-permute-done.23 = bf16[64,1024]{1,0:T(8,128)(2,1)} collective-permute-done((bf16[64,1024]{1,0:T(8,128)(2,1)S(1)}, bf16[64,1024]{1,0:T(8,128)(2,1)}, u32[]{:S(2)}, u32[]{:S(2)}) %collective-permute-start.23) | collective-permute-done | bytes 131104 | tf_op jit(solution)/shard_map/ppermute | solution.py:18
  148.2 2.2 %collective-permute-done.9 = f32[1]{0:T(128)} collective-permute-done((f32[1]{0:T(128)}, f32[1]{0:T(128)}, u32[]{:S(2)}, u32[]{:S(2)}) %collective-permute-start.9) | collective-permute-done | bytes 36 | tf_op jit(solution)/shard_map/ppermute | solution.py:22
  151.0 3.4 %collective-permute-start.10 = (f32[1]{0:T(128)}, f32[1]{0:T(128)}, u32[]{:S(2)}, u32[]{:S(2)}) collective-permute-start(f32[1]{0:T(128)} %add.206), channel_id=1, source_target_pairs={{0,4},{2,6},{4,0},{6,2},{8,12},{10,14},{12,8},{14,10},{1,5},{3,7},... | collective-permute-start | bytes 20 | tf_op jit(solution)/shard_map/ppermute | solution.py:22
  156.1 4.3 %collective-permute-start.11 = (f32[1]{0:T(128)}, f32[1]{0:T(128)}, u32[]{:S(2)}, u32[]{:S(2)}) collective-permute-start(f32[1]{0:T(128)} %add.207), channel_id=1, source_target_pairs={{0,8},{2,10},{4,12},{6,14},{8,0},{10,2},{12,4},{14,6},{1,9},{3,11}... | collective-permute-start | bytes 20 | tf_op jit(solution)/shard_map/ppermute | solution.py:22
  160.4 3.2 %collective-permute-done.11 = f32[1]{0:T(128)} collective-permute-done((f32[1]{0:T(128)}, f32[1]{0:T(128)}, u32[]{:S(2)}, u32[]{:S(2)}) %collective-permute-start.11) | collective-permute-done | bytes 36 | tf_op jit(solution)/shard_map/ppermute | solution.py:22
  165.7 2.1 %collective-permute-done.12 = f32[1]{0:T(128)} collective-permute-done((f32[1]{0:T(128)}, f32[1]{0:T(128)}, u32[]{:S(2)}, u32[]{:S(2)}) %collective-permute-start.12) | collective-permute-done | bytes 36 | tf_op jit(solution)/shard_map/ppermute | solution.py:22
  168.4 3.5 %collective-permute-start.13 = (f32[1]{0:T(128)}, f32[1]{0:T(128)}, u32[]{:S(2)}, u32[]{:S(2)}) collective-permute-start(f32[1]{0:T(128)} %add.209), channel_id=1, source_target_pairs={{0,32},{16,48},{32,0},{48,16},{1,33},{17,49},{33,1},{49,17},{2,34}... | collective-permute-start | bytes 20 | tf_op jit(solution)/shard_map/ppermute | solution.py:22
  174.1 2.8 %collective-permute-start.14 = (f32[1]{0:T(128)}, f32[1]{0:T(128)}, u32[]{:S(2)}, u32[]{:S(2)}) collective-permute-start(f32[1]{0:T(128)} %add.210), channel_id=1, source_target_pairs={{0,64},{64,0},{128,192},{192,128},{1,65},{65,1},{129,193},{193,129... | collective-permute-start | bytes 20 | tf_op jit(solution)/shard_map/ppermute | solution.py:22
  178.3 4.4 %collective-permute-start.15 = (f32[1]{0:T(128)}, f32[1]{0:T(128)}, u32[]{:S(2)}, u32[]{:S(2)}) collective-permute-start(f32[1]{0:T(128)} %add.211), channel_id=1, source_target_pairs={{0,128},{64,192},{128,0},{192,64},{1,129},{65,193},{129,1},{193,65... | collective-permute-start | bytes 20 | tf_op jit(solution)/shard_map/ppermute | solution.py:22
  185.1 7.1 %fusion.10 = f32[64,4096]{1,0:T(8,128)} fusion(bf16[4096,1024]{1,0:T(8,128)(2,1)} %param.6, f32[64,1024]{1,0:T(8,128)S(1)} %get-tuple-element.15, bf16[64,1024]{1,0:T(8,128)(2,1)S(1)} %collective-permute-done.24, bf16[64,1024]{1,0:T(8,128)(2,1)S(1)} %collective-permute-done.20, f32[64]{0:T(128)S(1)} %multiply_reduce_fusion.1, f32[64]{0:T(128)S(1)} %add_rsqrt_fusion.1, ...), kind=kOutput, calls=%fused_computation.34 | convolution fusion | flops 537526272 | bytes 10093060 | tf_op jit(solution)/shard_map/dot_general | solution.py:116
  192.8 7.0 %fusion.11 = f32[64,4096]{1,0:T(8,128)} fusion(bf16[4096,1024]{1,0:T(8,128)(2,1)} %param.6, f32[64,1024]{1,0:T(8,128)S(1)} %convert_reduce_fusion, f32[64,1024]{1,0:T(8,128)S(1)} %get-tuple-element.17, f32[64]{0:T(128)S(1)} %multiply_reduce_fusion, f32[64]{0:T(128)S(1)} %add_rsqrt_fusion), kind=kOutput, calls=%fused_computation.35 | convolution fusion | flops 537198592 | bytes 9961984 | tf_op jit(solution)/shard_map/dot_general | solution.py:119
  (78 shorter events, 35.2 us)
Async XLA Ops:
  7.2 6.9 %copy-start.4 = (bf16[64,4096]{1,0:T(8,128)(2,1)S(1)}, bf16[64,4096]{1,0:T(8,128)(2,1)}, u32[]{:S(2)}) copy-start(bf16[64,4096]{1,0:T(8,128)(2,1)} %param.5) | copy-start | bytes 1572868
  7.2 49.6 %all-gather.2.cloned.1.call-start = ((), (), s32[]{:S(2)}) async-start(), calls=%async_computation.2 | async-start | bytes 2228224 | tf_op jit(solution)/shard_map/all_gather | solution.py:63
  19.1 9.2 %copy-start.7 = (u32[256]{0:T(256)S(1)}, u32[256]{0:T(256)}, u32[]{:S(2)}) copy-start(u32[256]{0:T(256)} %constant.124) | copy-start | bytes 3076
  19.1 10.5 %copy-start.6 = (s32[64]{0:T(128)S(1)}, s32[64]{0:T(128)}, u32[]{:S(2)}) copy-start(s32[64]{0:T(128)} %param.7) | copy-start | bytes 772
  20.9 34.6 %all-to-all-start = ((bf16[16,64,1024]{2,1,0:T(8,128)(2,1)}), bf16[16,64,1024]{2,1,0:T(8,128)(2,1)S(1)}, u32[]{:S(2)}, u32[]{:S(2)}) async-start(bf16[16,64,1024]{2,1,0:T(8,128)(2,1)} %tile.2), calls=%async_computation | async-start | bytes 4194304 | tf_op jit(solution)/shard_map/all_to_all | solution.py:66
  63.9 3.3 %collective-permute-start = (f32[1024]{0:T(1024)S(1)}, f32[1024]{0:T(1024)S(1)}, u32[]{:S(2)}, u32[]{:S(2)}) collective-permute-start(f32[1024]{0:T(1024)S(1)} %get-tuple-element.5), channel_id=1, source_target_pairs={{0,1},{1,0},{2,3},{3,2},{4,5},{5,4},{6,7},{7,6},{8,9},{9,8},{10,11... | collective-permute-start | bytes 12296 | tf_op jit(solution)/shard_map/ppermute | solution.py:22
  64.1 5.0 %collective-permute-start.4 = (f32[1024]{0:T(1024)S(1)}, f32[1024]{0:T(1024)S(1)}, u32[]{:S(2)}, u32[]{:S(2)}) collective-permute-start(f32[1024]{0:T(1024)S(1)} %get-tuple-element.4), channel_id=1, source_target_pairs={{0,16},{16,0},{32,48},{48,32},{1,17},{17,1},{33,49},{49,33},{2,18}... | collective-permute-start | bytes 12296 | tf_op jit(solution)/shard_map/ppermute | solution.py:22
  67.2 3.6 %collective-permute-start.1 = (f32[1024]{0:T(1024)S(1)}, f32[1024]{0:T(1024)S(1)}, u32[]{:S(2)}, u32[]{:S(2)}) collective-permute-start(f32[1024]{0:T(1024)S(1)} %add.193), channel_id=1, source_target_pairs={{0,2},{2,0},{4,6},{6,4},{8,10},{10,8},{12,14},{14,12},{1,3},{3,1},... | collective-permute-start | bytes 12296 | tf_op jit(solution)/shard_map/ppermute | solution.py:22
  69.2 5.1 %collective-permute-start.5 = (f32[1024]{0:T(1024)S(1)}, f32[1024]{0:T(1024)S(1)}, u32[]{:S(2)}, u32[]{:S(2)}) collective-permute-start(f32[1024]{0:T(1024)S(1)} %add.198), channel_id=1, source_target_pairs={{0,32},{16,48},{32,0},{48,16},{1,33},{17,49},{33,1},{49,17},{2,34}... | collective-permute-start | bytes 12296 | tf_op jit(solution)/shard_map/ppermute | solution.py:22
  70.8 4.9 %collective-permute-start.2 = (f32[1024]{0:T(1024)S(1)}, f32[1024]{0:T(1024)S(1)}, u32[]{:S(2)}, u32[]{:S(2)}) collective-permute-start(f32[1024]{0:T(1024)S(1)} %add.194), channel_id=1, source_target_pairs={{0,4},{2,6},{4,0},{6,2},{8,12},{10,14},{12,8},{14,10},{1,5},{3,7},... | collective-permute-start | bytes 12296 | tf_op jit(solution)/shard_map/ppermute | solution.py:22
  74.3 8.3 %collective-permute-start.6 = (f32[1024]{0:T(1024)S(1)}, f32[1024]{0:T(1024)S(1)}, u32[]{:S(2)}, u32[]{:S(2)}) collective-permute-start(f32[1024]{0:T(1024)S(1)} %add.199), channel_id=1, source_target_pairs={{0,64},{64,0},{128,192},{192,128},{1,65},{65,1},{129,193},{193,129... | collective-permute-start | bytes 12296 | tf_op jit(solution)/shard_map/ppermute | solution.py:22
  75.7 8.5 %collective-permute-start.3 = (f32[1024]{0:T(1024)S(1)}, f32[1024]{0:T(1024)S(1)}, u32[]{:S(2)}, u32[]{:S(2)}) collective-permute-start(f32[1024]{0:T(1024)S(1)} %add.195), channel_id=1, source_target_pairs={{0,8},{2,10},{4,12},{6,14},{8,0},{10,2},{12,4},{14,6},{1,9},{3,11}... | collective-permute-start | bytes 12296 | tf_op jit(solution)/shard_map/ppermute | solution.py:22
  82.6 5.1 %collective-permute-start.7 = (f32[1024]{0:T(1024)S(1)}, f32[1024]{0:T(1024)S(1)}, u32[]{:S(2)}, u32[]{:S(2)}) collective-permute-start(f32[1024]{0:T(1024)S(1)} %add.200), channel_id=1, source_target_pairs={{0,128},{64,192},{128,0},{192,64},{1,129},{65,193},{129,1},{193,65... | collective-permute-start | bytes 12296 | tf_op jit(solution)/shard_map/ppermute | solution.py:22
  95.9 2.7 %collective-permute-start.16 = (bf16[8,64,1024]{2,1,0:T(8,128)(2,1)S(1)}, bf16[8,64,1024]{2,1,0:T(8,128)(2,1)S(1)}, u32[]{:S(2)}, u32[]{:S(2)}) collective-permute-start(bf16[8,64,1024]{2,1,0:T(8,128)(2,1)S(1)} %dynamic-slice_bitcast_fusion), channel_id=1, source_target_pairs={{0,1},{1,0},{2,3},{3,2},{4,5},{5,4},{6,7},{7,6},{8,9},{9,8},{10,11... | collective-permute-start | bytes 3145736 | tf_op jit(solution)/shard_map/ppermute | solution.py:22
  100.3 13.3 %copy-start.1 = (bf16[8,64,1024]{2,1,0:T(8,128)(2,1)}, bf16[8,64,1024]{2,1,0:T(8,128)(2,1)S(1)}, u32[]{:S(2)}) copy-start(bf16[8,64,1024]{2,1,0:T(8,128)(2,1)S(1)} %fusion.2) | copy-start | bytes 3145732
  100.3 4.3 %collective-permute-start.17 = (bf16[32,1024]{1,0:T(8,128)(2,1)S(1)}, bf16[32,1024]{1,0:T(8,128)(2,1)S(1)}, u32[]{:S(2)}, u32[]{:S(2)}) collective-permute-start(bf16[32,1024]{1,0:T(8,128)(2,1)S(1)} %get-tuple-element.12), channel_id=1, source_target_pairs={{0,14},{2,0},{4,2},{6,4},{8,6},{10,8},{12,10},{14,12},{1,15},{3,1}... | collective-permute-start | bytes 196616 | tf_op jit(solution)/shard_map/ppermute | solution.py:18
  104.7 14.8 %collective-permute-start.18 = (bf16[64,1024]{1,0:T(8,128)(2,1)S(1)}, bf16[64,1024]{1,0:T(8,128)(2,1)S(1)}, u32[]{:S(2)}, u32[]{:S(2)}) collective-permute-start(bf16[64,1024]{1,0:T(8,128)(2,1)S(1)} %fusion.6), channel_id=1, source_target_pairs={{0,14},{2,0},{4,2},{6,4},{8,6},{10,8},{12,10},{14,12},{1,15},{3,1}... | collective-permute-start | bytes 393224 | tf_op jit(solution)/shard_map/ppermute | solution.py:18
  113.6 78.7 %all-to-all-start.1 = ((bf16[16,64,1024]{2,1,0:T(8,128)(2,1)}), bf16[16,64,1024]{2,1,0:T(8,128)(2,1)S(1)}, u32[]{:S(2)}, u32[]{:S(2)}) async-start(bf16[16,64,1024]{2,1,0:T(8,128)(2,1)} %bitcast.56), calls=%async_computation.1 | async-start | bytes 4194304 | tf_op jit(solution)/shard_map/all_to_all | solution.py:105
  120.4 6.3 %collective-permute-start.19 = (bf16[64,1024]{1,0:T(8,128)(2,1)S(1)}, bf16[64,1024]{1,0:T(8,128)(2,1)S(1)}, u32[]{:S(2)}, u32[]{:S(2)}) collective-permute-start(bf16[64,1024]{1,0:T(8,128)(2,1)S(1)} %fusion.7), channel_id=1, source_target_pairs={{0,14},{2,0},{4,2},{6,4},{8,6},{10,8},{12,10},{14,12},{1,15},{3,1}... | collective-permute-start | bytes 393224 | tf_op jit(solution)/shard_map/ppermute | solution.py:18
  120.5 5.6 %collective-permute-start.21 = (bf16[32,1024]{1,0:T(8,128)(2,1)S(1)}, bf16[32,1024]{1,0:T(8,128)(2,1)S(1)}, u32[]{:S(2)}, u32[]{:S(2)}) collective-permute-start(bf16[32,1024]{1,0:T(8,128)(2,1)S(1)} %get-tuple-element.13), channel_id=1, source_target_pairs={{0,2},{2,4},{4,6},{6,8},{8,10},{10,12},{12,14},{14,0},{1,3},{3,5},... | collective-permute-start | bytes 196616 | tf_op jit(solution)/shard_map/ppermute | solution.py:18
  128.4 6.2 %collective-permute-start.22 = (bf16[64,1024]{1,0:T(8,128)(2,1)S(1)}, bf16[64,1024]{1,0:T(8,128)(2,1)S(1)}, u32[]{:S(2)}, u32[]{:S(2)}) collective-permute-start(bf16[64,1024]{1,0:T(8,128)(2,1)S(1)} %get-tuple-element.11), channel_id=1, source_target_pairs={{0,2},{2,4},{4,6},{6,8},{8,10},{10,12},{12,14},{14,0},{1,3},{3,5},... | collective-permute-start | bytes 393224 | tf_op jit(solution)/shard_map/ppermute | solution.py:18
  135.5 6.4 %collective-permute-start.23 = (bf16[64,1024]{1,0:T(8,128)(2,1)S(1)}, bf16[64,1024]{1,0:T(8,128)(2,1)}, u32[]{:S(2)}, u32[]{:S(2)}) collective-permute-start(bf16[64,1024]{1,0:T(8,128)(2,1)S(1)} %fusion.4), channel_id=1, source_target_pairs={{0,2},{2,4},{4,6},{6,8},{8,10},{10,12},{12,14},{14,0},{1,3},{3,5},... | collective-permute-start | bytes 393224 | tf_op jit(solution)/shard_map/ppermute | solution.py:18
  135.6 48.4 %collective-permute-start.20 = (bf16[64,1024]{1,0:T(8,128)(2,1)}, bf16[64,1024]{1,0:T(8,128)(2,1)S(1)}, u32[]{:S(2)}, u32[]{:S(2)}) collective-permute-start(bf16[64,1024]{1,0:T(8,128)(2,1)} %get-tuple-element.10), channel_id=1, source_target_pairs={{0,14},{2,0},{4,2},{6,4},{8,6},{10,8},{12,10},{14,12},{1,15},{3,1}... | collective-permute-start | bytes 393224 | tf_op jit(solution)/shard_map/ppermute | solution.py:18
  142.8 41.1 %collective-permute-start.24 = (bf16[64,1024]{1,0:T(8,128)(2,1)S(1)}, bf16[64,1024]{1,0:T(8,128)(2,1)S(1)}, u32[]{:S(2)}, u32[]{:S(2)}) collective-permute-start(bf16[64,1024]{1,0:T(8,128)(2,1)S(1)} %fusion.5), channel_id=1, source_target_pairs={{0,2},{2,4},{4,6},{6,8},{8,10},{10,12},{12,14},{14,0},{1,3},{3,5},... | collective-permute-start | bytes 393224 | tf_op jit(solution)/shard_map/ppermute | solution.py:18
  145.0 1.2 collective-permute-start.8
  146.8 3.6 %collective-permute-start.9 = (f32[1]{0:T(128)}, f32[1]{0:T(128)}, u32[]{:S(2)}, u32[]{:S(2)}) collective-permute-start(f32[1]{0:T(128)} %add.205), channel_id=1, source_target_pairs={{0,2},{2,0},{4,6},{6,4},{8,10},{10,8},{12,14},{14,12},{1,3},{3,1},... | collective-permute-start | bytes 20 | tf_op jit(solution)/shard_map/ppermute | solution.py:22
  151.0 4.5 %collective-permute-start.10 = (f32[1]{0:T(128)}, f32[1]{0:T(128)}, u32[]{:S(2)}, u32[]{:S(2)}) collective-permute-start(f32[1]{0:T(128)} %add.206), channel_id=1, source_target_pairs={{0,4},{2,6},{4,0},{6,2},{8,12},{10,14},{12,8},{14,10},{1,5},{3,7},... | collective-permute-start | bytes 20 | tf_op jit(solution)/shard_map/ppermute | solution.py:22
  156.1 7.5 %collective-permute-start.11 = (f32[1]{0:T(128)}, f32[1]{0:T(128)}, u32[]{:S(2)}, u32[]{:S(2)}) collective-permute-start(f32[1]{0:T(128)} %add.207), channel_id=1, source_target_pairs={{0,8},{2,10},{4,12},{6,14},{8,0},{10,2},{12,4},{14,6},{1,9},{3,11}... | collective-permute-start | bytes 20 | tf_op jit(solution)/shard_map/ppermute | solution.py:22
  164.2 3.6 %collective-permute-start.12 = (f32[1]{0:T(128)}, f32[1]{0:T(128)}, u32[]{:S(2)}, u32[]{:S(2)}) collective-permute-start(f32[1]{0:T(128)} %add.208), channel_id=1, source_target_pairs={{0,16},{16,0},{32,48},{48,32},{1,17},{17,1},{33,49},{49,33},{2,18}... | collective-permute-start | bytes 20 | tf_op jit(solution)/shard_map/ppermute | solution.py:22
  168.4 5.1 %collective-permute-start.13 = (f32[1]{0:T(128)}, f32[1]{0:T(128)}, u32[]{:S(2)}, u32[]{:S(2)}) collective-permute-start(f32[1]{0:T(128)} %add.209), channel_id=1, source_target_pairs={{0,32},{16,48},{32,0},{48,16},{1,33},{17,49},{33,1},{49,17},{2,34}... | collective-permute-start | bytes 20 | tf_op jit(solution)/shard_map/ppermute | solution.py:22
  174.1 3.6 %collective-permute-start.14 = (f32[1]{0:T(128)}, f32[1]{0:T(128)}, u32[]{:S(2)}, u32[]{:S(2)}) collective-permute-start(f32[1]{0:T(128)} %add.210), channel_id=1, source_target_pairs={{0,64},{64,0},{128,192},{192,128},{1,65},{65,1},{129,193},{193,129... | collective-permute-start | bytes 20 | tf_op jit(solution)/shard_map/ppermute | solution.py:22
  178.3 5.1 %collective-permute-start.15 = (f32[1]{0:T(128)}, f32[1]{0:T(128)}, u32[]{:S(2)}, u32[]{:S(2)}) collective-permute-start(f32[1]{0:T(128)} %add.211), channel_id=1, source_target_pairs={{0,128},{64,192},{128,0},{192,64},{1,129},{65,193},{129,1},{193,65... | collective-permute-start | bytes 20 | tf_op jit(solution)/shard_map/ppermute | solution.py:22
  (4 other events, 5.4 us)
Sparse Core Ops, SparseCore 0:
  14.2 42.5 all-gather.1

commit v2 on v1

v2 whole, which is shorter than its diff:
```python
import functools

import jax
import jax.numpy as jnp
from jax import lax
from jax.experimental import pallas as pl
from jax.experimental.pallas import tpu as pltpu
from jax.sharding import Mesh, PartitionSpec as P

logit_scale = 20.0
grad_scale = 128.0
norm_eps = 1e-06
log2_e = 1.4426950408889634

NY, NX, NZ, NC = 4, 4, 8, 2
QR = ("y", "x")
PC = ("z", "c")
f32 = jnp.float32
bf16 = jnp.bfloat16
LANES = 128
HBM = pl.BlockSpec(memory_space=pltpu.HBM)
VMEM = pl.BlockSpec(memory_space=pltpu.VMEM)
SMEM = pl.BlockSpec(memory_space=pltpu.SMEM)
params = pltpu.CompilerParams(vmem_limit_bytes=32 * 1024 * 1024)
NT = (((1,), (1,)), ((), ()))
TN = (((0,), (0,)), ((), ()))


def shift(value, axis, size, step):
    return lax.ppermute(value, axis, [(i, (i + step) % size) for i in range(size)])


def swap(value, axis, size, bit):
    return lax.ppermute(value, axis, [(i, i ^ bit) for i in range(size)])


pc_steps = (("c", NC, 1), ("z", NZ, 1), ("z", NZ, 2), ("z", NZ, 4))
qr_steps = (("x", NX, 1), ("x", NX, 2), ("y", NY, 1), ("y", NY, 2))


def sds(shape, dtype):
    return jax.ShapeDtypeStruct(shape, dtype)


def fixed(shape):
    return pl.BlockSpec(shape, lambda *i: (0,) * len(shape))


def embed_kernel(
    query_ref,
    passage_ref,
    proj_ref,
    positive_ref,
    message_ref,
    copies_ref,
    unit_ref,
    inv_ref,
    pools,
    weights,
    spread,
    in_sems,
    out_sems,
):
    rows, depth = query_ref.shape
    width = proj_ref.shape[1]
    steps = in_sems.shape[0] - 2
    chunk = depth // steps
    loads = [
        pltpu.make_async_copy(query_ref, pools.at[:rows], in_sems.at[0]),
        pltpu.make_async_copy(passage_ref, pools.at[rows:], in_sems.at[1]),
    ]
    for k in range(steps):
        part = pl.ds(k * chunk, chunk)
        loads.append(pltpu.make_async_copy(proj_ref.at[part], weights.at[part], in_sems.at[k + 2]))
    for load in loads:
        load.start()
    loads[0].wait()
    loads[1].wait()
    raw = jnp.zeros((2 * rows, width), f32)
    for k in range(steps):
        loads[k + 2].wait()
        part = pl.ds(k * chunk, chunk)
        raw = raw + jnp.dot(pools[:, part], weights[part, :], preferred_element_type=f32)
    inv = lax.rsqrt(jnp.sum(raw * raw, axis=-1, keepdims=True) + norm_eps)
    unit = raw * inv
    embed = unit.astype(bf16)
    spread[...] = embed[rows:]
    stores = []
    for k in range(copies_ref.shape[0] // rows):
        part = pl.ds(k * rows, rows)
        stores.append(pltpu.make_async_copy(spread, copies_ref.at[part], out_sems.at[k]))
    for store in stores:
        store.start()
    unit_ref[...] = unit
    inv_ref[...] = jnp.broadcast_to(inv, inv_ref.shape)
    message_ref[:, :width] = embed[:rows]
    square = (rows, rows)
    line = jnp.broadcast_to(positive_ref[...].astype(f32), square)
    on = lax.broadcasted_iota(jnp.int32, square, 0) == lax.broadcasted_iota(jnp.int32, square, 1)
    index = jnp.sum(jnp.where(on, line, 0.0), axis=1, keepdims=True)
    high = jnp.floor(index * (1.0 / LANES))
    low = index - high * LANES
    lane = lax.broadcasted_iota(jnp.int32, (rows, LANES), 1)
    message_ref[:, width:] = jnp.where(lane == 0, high, jnp.where(lane == 1, low, 0.0)).astype(bf16)
    for store in stores:
        store.wait()


def embed(query_pool, passage_pool, proj, positive):
    rows, depth = query_pool.shape
    width = proj.shape[1]
    copies = NY * NX
    steps = 8
    return pl.pallas_call(
        embed_kernel,
        in_specs=[HBM, HBM, HBM, VMEM],
        out_specs=[VMEM, HBM, VMEM, VMEM],
        out_shape=[
            sds((rows, width + LANES), bf16),
            sds((copies * rows, width), bf16),
            sds((2 * rows, width), f32),
            sds((2 * rows, LANES), f32),
        ],
        scratch_shapes=[
            pltpu.VMEM((2 * rows, depth), bf16),
            pltpu.VMEM((depth, width), bf16),
            pltpu.VMEM((rows, width), bf16),
            pltpu.SemaphoreType.DMA((steps + 2,)),
            pltpu.SemaphoreType.DMA((copies,)),
        ],
        compiler_params=params,
        name="embed",
    )(query_pool, passage_pool, proj, positive)


def positive_column(query_ref, width, place_ref, columns):
    parts = query_ref[:, width:].astype(f32)
    index = parts[:, 0:1] * LANES + parts[:, 1:2]
    first = (place_ref[0] * NC + place_ref[1]) * columns
    return index.astype(jnp.int32) - first


def line_of(place_ref, k):
    z = lax.rem(place_ref[0] + k % NZ, NZ)
    c = place_ref[1] if k < NZ else 1 - place_ref[1]
    return pl.ds(c * NZ + z, 1)


def logits_kernel(place_ref, *refs):
    pieces = refs[: NZ * NC]
    passage_ref, exp_ref, query_ref, kept_ref, row_ref, col_ref, row_acc, in_sems = refs[NZ * NC :]
    own = pieces[0].shape[0]
    columns, width = passage_ref.shape
    rows = query_ref.shape[0]
    steps = in_sems.shape[0] - NZ * NC
    chunk = columns // steps
    loads = []
    for k, piece in enumerate(pieces):
        loads.append(pltpu.make_async_copy(piece, query_ref.at[pl.ds(k * own, own)], in_sems.at[k]))
    for k in range(steps):
        part = pl.ds(k * chunk, chunk)
        sem = in_sems.at[NZ * NC + k]
        loads.append(pltpu.make_async_copy(passage_ref.at[part], kept_ref.at[part], sem))
    for load in loads:
        load.start()
    for load in loads[: NZ * NC]:
        load.wait()
    positive = positive_column(query_ref, width, place_ref, columns)
    row_part = jnp.zeros((rows, LANES), f32)
    picked = jnp.zeros((1, chunk), f32)
    for k in range(steps):
        loads[NZ * NC + k].wait()
        part = pl.ds(k * chunk, chunk)
        dots = lax.dot_general(
            query_ref[:, :width], kept_ref[part, :], NT, preferred_element_type=f32
        )
        shifted = jnp.exp2(dots * (logit_scale * log2_e) - logit_scale * log2_e)
        exp_ref[:, part] = shifted
        col_ref[:, part] = jnp.sum(shifted, axis=0, keepdims=True)
        for n in range(chunk // LANES):
            row_part = row_part + shifted[:, n * LANES : (n + 1) * LANES]
        column = lax.broadcasted_iota(jnp.int32, (rows, chunk), 1) + k * chunk
        found = jnp.where(column == positive, dots, 0.0)
        picked = picked + jnp.sum(found, axis=0, keepdims=True)
    total = logit_scale * jnp.sum(picked, axis=1, keepdims=True)
    row_acc[...] = row_part
    lane = lax.broadcasted_iota(jnp.int32, (1, LANES), 1)
    for k in range(0, NZ * NC, 2):
        turned = row_acc[k * own : (k + 2) * own, :].T
        line = jnp.sum(turned, axis=0, keepdims=True)
        row_ref[line_of(place_ref, k), :] = jnp.where(lane < own, line, total)
        line = pltpu.roll(line, own, 1)
        row_ref[line_of(place_ref, k + 1), :] = jnp.where(lane < own, line, total)


def tile_logits(place, pieces, passage_tile):
    own, wide = pieces[0].shape
    columns, width = passage_tile.shape
    rows = own * len(pieces)
    steps = 4
    return pl.pallas_call(
        logits_kernel,
        in_specs=[SMEM] + [HBM] * (len(pieces) + 1),
        out_specs=[VMEM] * 5,
        out_shape=[
            sds((rows, columns), f32),
            sds((rows, wide), bf16),
            sds((columns, width), bf16),
            sds((len(pieces), LANES), f32),
            sds((1, columns), f32),
        ],
        scratch_shapes=[
            pltpu.VMEM((rows, LANES), f32),
            pltpu.SemaphoreType.DMA((len(pieces) + steps,)),
        ],
        compiler_params=params,
        name="logits",
    )(place, *pieces, passage_tile)


def grads_kernel(
    place_ref,
    exp_ref,
    row_ref,
    col_ref,
    query_ref,
    passage_ref,
    part_ref,
    own_ref,
    other_ref,
    col_loss_ref,
    grad,
    row_scale,
    parts,
    sems,
):
    columns, width = passage_ref.shape
    rows = query_ref.shape[0]
    own = rows // (NZ * NC)
    steps = sems.shape[0]
    chunk = columns // steps
    half = 0.5 * grad_scale
    lane = lax.broadcasted_iota(jnp.int32, (1, LANES), 1)
    row_total = logit_scale * rows - 2.0 * row_ref[0:1, own : own + 1]
    for k in range(0, NZ * NC, 2):
        first, second = row_ref[line_of(place_ref, k), :], row_ref[line_of(place_ref, k + 1), :]
        line = jnp.where(lane < own, first, pltpu.roll(second, own, 1))
        row_total = row_total + jnp.sum(jnp.log(line), axis=1, keepdims=True)
        turned = jnp.broadcast_to(half / line, (LANES, LANES)).T
        row_scale[k * own : (k + 2) * own, :] = turned
    col_total = jnp.sum(jnp.log(col_ref[...]), axis=1, keepdims=True) + logit_scale * columns
    col_loss_ref[...] = jnp.broadcast_to(col_total, (1, LANES))
    high = row_total.astype(bf16).astype(f32)
    middle = (row_total - high).astype(bf16).astype(f32)
    low = row_total - high - middle
    extra = jnp.where(lane == 0, high, jnp.where(lane == 1, middle, jnp.where(lane == 2, low, 0.0)))
    extra = jnp.broadcast_to(extra, (chunk, LANES)).astype(bf16)
    positive = positive_column(query_ref, width, place_ref, columns)
    stores = []
    for k in range(steps):
        part = pl.ds(k * chunk, chunk)
        scale = jnp.concatenate([row_scale[...]] * (chunk // LANES), axis=1)
        scale = scale + half / col_ref[:, part]
        column = lax.broadcasted_iota(jnp.int32, (rows, chunk), 1) + k * chunk
        hit = jnp.where(column == positive, grad_scale, 0.0)
        tile = (exp_ref[:, part] * scale - hit).astype(bf16)
        grad[:, part] = tile
        term = lax.dot_general(tile, query_ref[:, :width], TN, preferred_element_type=f32)
        parts[part, :width] = (logit_scale * term).astype(bf16)
        parts[part, width:] = extra
        stores.append(pltpu.make_async_copy(parts.at[part], part_ref.at[part], sems.at[k]))
        stores[-1].start()
    for k, out_ref in enumerate((own_ref, other_ref)):
        part = pl.ds(k * NZ * own, NZ * own)
        term = jnp.dot(grad[part, :], passage_ref[...], preferred_element_type=f32)
        out_ref[...] = (logit_scale * term).astype(bf16).reshape(out_ref.shape)
    for store in stores:
        store.wait()


def tile_grads(place, shifted, row_sum, column_sum, query_tile, passage_tile):
    rows, wide = query_tile.shape
    columns, width = passage_tile.shape
    own = rows // (NZ * NC)
    steps = 4
    return pl.pallas_call(
        grads_kernel,
        in_specs=[SMEM] + [VMEM] * 5,
        out_specs=[HBM, VMEM, VMEM, VMEM],
        out_shape=[
            sds((columns, wide), bf16),
            sds((NZ, own, width), bf16),
            sds((NZ, own, width), bf16),
            sds((1, LANES), f32),
        ],
        scratch_shapes=[
            pltpu.VMEM((rows, columns), bf16),
            pltpu.VMEM((rows, LANES), f32),
            pltpu.VMEM((columns, wide), bf16),
            pltpu.SemaphoreType.DMA((steps,)),
        ],
        compiler_params=params,
        name="grads",
    )(place, shifted, row_sum, column_sum, query_tile, passage_tile)


def ring_step(own, other, turns, loss, came_loss):
    _, height, width = own.shape
    operands, in_specs, kept = [], [], []
    for block, came in turns:
        spec = pl.BlockSpec((1, height, width), lambda i, block=block: (block, 0, 0))
        operands += [own, other]
        in_specs += [spec, spec]
        kept.append(came is not None)
        if came is not None:
            operands.append(came)
            in_specs.append(fixed((height, width)))
    operands += [loss, came_loss]
    in_specs += [fixed((1, LANES))] * 2

    def kernel(*refs):
        refs = list(refs)
        outs = refs[len(operands) :]
        for out, there in zip(outs, kept):
            total = refs.pop(0)[0].astype(f32) + refs.pop(0)[0].astype(f32)
            if there:
                total = total + refs.pop(0)[...].astype(f32)
            out[...] = total.astype(out.dtype)
        outs[-1][...] = refs[0][...] + refs[1][...]

    count = len(turns)
    return pl.pallas_call(
        kernel,
        grid=(1,),
        in_specs=in_specs,
        out_specs=[fixed((height, width))] * count + [fixed((1, LANES))],
        out_shape=[sds((height, width), bf16)] * count + [sds((1, LANES), f32)],
        compiler_params=params,
        name="ring",
    )(*operands)


def final_kernel(
    count,
    base_ref,
    down_ref,
    up_ref,
    loss_ref,
    unit_ref,
    inv_ref,
    proj_ref,
    terms_ref,
    total_ref,
    query_ref,
    passage_ref,
    terms,
    raw,
    outs,
    in_sems,
    out_sems,
):
    rows, width = down_ref.shape
    steps = out_sems.shape[0] // 2
    chunk = proj_ref.shape[0] // steps
    loads = []
    blocks = in_sems.shape[0]
    height = terms_ref.shape[0] // blocks
    for k in range(blocks):
        part = pl.ds(k * height, height)
        loads.append(pltpu.make_async_copy(terms_ref.at[part], terms.at[part], in_sems.at[k]))
        loads[-1].start()

    def back(k, incoming):
        unit = unit_ref[k * rows : (k + 1) * rows, :]
        inv = inv_ref[k * rows : (k + 1) * rows, :1]
        along = jnp.sum(unit * incoming, axis=-1, keepdims=True)
        raw[k * rows : (k + 1) * rows, :] = (inv * (incoming - unit * along)).astype(bf16)

    back(0, base_ref[...].astype(f32) + down_ref[...].astype(f32) + up_ref[...].astype(f32))
    passage = jnp.zeros((rows, width), f32)
    total = loss_ref[:, :1]
    for k in range(blocks):
        loads[k].wait()
        for n in range(k * height, (k + 1) * height, rows):
            passage = passage + terms[n : n + rows, :width].astype(f32)
            extra = terms[n : n + 16, width:].astype(f32)[:1]
            total = total + jnp.sum(extra, axis=1, keepdims=True)
    total_ref[...] = total * (1.0 / count)
    back(1, passage)
    stores = []
    for k in range(steps):
        part = pl.ds(k * chunk, chunk)
        outs[:, part] = lax.dot_general(raw[...], proj_ref[part, :], NT, preferred_element_type=f32)
        for n, out_ref in enumerate((query_ref, passage_ref)):
            source = outs.at[pl.ds(n * rows, rows), part]
            store = pltpu.make_async_copy(source, out_ref.at[:, part], out_sems.at[2 * k + n])
            store.start()
            stores.append(store)
    for store in stores:
        store.wait()


def final(count, base, down, up, loss, unit, inv, proj, terms):
    rows, width = down.shape
    depth = proj.shape[0]
    steps = 4
    return pl.pallas_call(
        functools.partial(final_kernel, count),
        in_specs=[VMEM] * 7 + [HBM],
        out_specs=[VMEM, HBM, HBM],
        out_shape=[sds((1, 1), f32)] + [sds((rows, depth), f32)] * 2,
        scratch_shapes=[
            pltpu.VMEM(terms.shape, bf16),
            pltpu.VMEM((2 * rows, width), bf16),
            pltpu.VMEM((2 * rows, depth), f32),
            pltpu.SemaphoreType.DMA((4,)),
            pltpu.SemaphoreType.DMA((2 * steps,)),
        ],
        compiler_params=params,
        name="final",
    )(base, down, up, loss, unit, inv, proj, terms)


def gather_queries(message):
    pieces = {0: message}
    down = up = message
    for k in range(1, NZ // 2 + 1):
        down = shift(down, "z", NZ, -1)
        pieces[k] = down
        if k < NZ // 2:
            up = shift(up, "z", NZ, 1)
            pieces[NZ - k] = up
    own = [pieces[k] for k in range(NZ)]
    return own + [swap(piece, "c", NC, 1) for piece in own]


def body(query_pool, passage_pool, proj, positive):
    place = jnp.stack([lax.axis_index("z"), lax.axis_index("c")]).astype(jnp.int32)
    message, copies, unit, inv = embed(query_pool, passage_pool, proj, positive[None])
    passage_tile = lax.all_to_all(copies, QR, 0, 0, tiled=True)
    pieces = gather_queries(message)
    shifted, query_tile, passage_tile, row_sum, column_sum = tile_logits(
        place, pieces, passage_tile
    )
    for pc_step, qr_step in zip(pc_steps, qr_steps):
        row_sum = row_sum + swap(row_sum, *pc_step)
        column_sum = column_sum + swap(column_sum, *qr_step)
    partial, own, other, loss = tile_grads(
        place, shifted, row_sum, column_sum, query_tile, passage_tile
    )
    terms = lax.all_to_all(partial, QR, 0, 0, tiled=True)
    other = swap(other, "c", NC, 1)
    down, loss = ring_step(own, other, [(4, None)], loss, swap(loss, *pc_steps[0]))
    came = shift(down, "z", NZ, -1)
    turns = [(5, came), (3, None)]
    down, up, loss = ring_step(own, other, turns, loss, swap(loss, *pc_steps[1]))
    came = shift(down, "z", NZ, -1), shift(up, "z", NZ, 1)
    turns = [(6, came[0]), (2, came[1])]
    down, up, loss = ring_step(own, other, turns, loss, swap(loss, *pc_steps[2]))
    came = shift(down, "z", NZ, -1), shift(up, "z", NZ, 1)
    turns = [(7, came[0]), (1, came[1]), (0, None)]
    down, up, base, loss = ring_step(own, other, turns, loss, swap(loss, *pc_steps[3]))
    down, up = shift(down, "z", NZ, -1), shift(up, "z", NZ, 1)
    count = 2.0 * column_sum.shape[1] * NZ * NC
    total, grad_query_pool, grad_passage_pool = final(
        count, base, down, up, loss, unit, inv, proj, terms
    )
    return (total.reshape(()), grad_query_pool, grad_passage_pool)


def solution(mesh):
    fine = Mesh(mesh.devices.reshape(NY, NX, NZ, NC), ("y", "x", "z", "c"))
    in_specs = (
        P(("y", "x", "z", "c"), None),
        P(("z", "c", "y", "x"), None),
        P(),
        P(("y", "x", "z", "c")),
    )
    out_specs = (P(), P(("y", "x", "z", "c"), None), P(("z", "c", "y", "x"), None))
    return jax.shard_map(
        body, mesh=fine, in_specs=in_specs, out_specs=out_specs, check_vma=False
    )
```

time: 208 us -> 149 us (0.72)
  matrix products: 39.7 us -> 0 us
  Pallas kernels: 0 us -> 27.7 us
  between operations: 22.8 us -> 0.96 us
  blocking collectives: 16.4 us -> 0 us
  other arithmetic: 13.8 us -> 0.11 us
  local copies, waits for them, and re-layouts: 5.5 us -> 16.5 us
  waiting for transfers between devices: 44.6 us -> 40.9 us
  starting transfers between devices: 65.1 us -> 62.6 us
    dot_general x7 -> x0, matrix products: 39.7 us -> none  [the longest x2 10.1 us: embed_rows(): raw_rows = jnp.dot(pool, proj, preferred_element_type=f32)]
    pallas_call x0 -> x8, Pallas kernels: none -> 27.7 us  [the longest x1 9.09 us: tile_logits(): pl.pallas_call(logits_kernel, in_specs=[SMEM] + [HBM] * (len(pieces) + 1)...]
    ppermute x17 -> x21, starting transfers between devices: 40.6 us -> 22.9 us  [swap(): return lax.ppermute(value, axis, [(i, i ^ bit) for i in range(size)])]
    unnamed x1 -> x0, blocking collectives: 16.4 us -> none
    ppermute x8 -> x14, starting transfers between devices: 11.1 us -> 25.7 us  [shift(): lax.ppermute(value, axis, [(i, (i + step) % size) for i in range(size)])]
    unnamed x19 -> x24, local copies, waits for them, and re-layouts: 3.81 us -> 16.5 us
    convert_element_type x9 -> x0, other arithmetic: 10.8 us -> none  [the longest x1 3.8 us: body(): grad_tile = grad_tile.astype(bf16)]
    all_to_all x2, waiting for transfers between devices: 9.23 us -> 0.01 us  [the longest x1 0.01 us: body(): terms = lax.all_to_all(partial, QR, 0, 0, tiled=True)]
  transfers between devices with their start and end apart: 28 -> 37, of which waited for: 19 -> 18; matrix products, arithmetic and copies ran while one was open for 13% -> 0% of each run, Pallas kernels for 0% -> 0%
where the time goes in v2:
time: 149 us
  starting transfers between devices  62.6 us (42%)
  waiting for transfers between devices  40.9 us (27%)
  Pallas kernels  27.7 us (19%)
  local copies, waits for them, and re-layouts  16.5 us (11%)
    ppermute x14, starting transfers between devices, shift(): lax.ppermute(value, axis, [(i, (i + step) % size) for i in range(size)])  25.7 us
    ppermute x21, waiting for transfers between devices, swap(): return lax.ppermute(value, axis, [(i, i ^ bit) for i in range(size)])  23.4 us
    ppermute x21, starting transfers between devices, swap(): return lax.ppermute(value, axis, [(i, i ^ bit) for i in range(size)])  22.9 us
    ppermute x14, waiting for transfers between devices, shift(): lax.ppermute(value, axis, [(i, (i + step) % size) for i in range(size)])  17.5 us
    unnamed x24, local copies, waits for them, and re-layouts  16.5 us
    pallas_call x1, Pallas kernels, tile_logits(): pl.pallas_call(logits_kernel, in_specs=[SMEM] + [HBM] * (len(pieces) + 1)...  9.09 us
    all_to_all x1, starting transfers between devices, body(): passage_tile = lax.all_to_all(copies, QR, 0, 0, tiled=True)  7.48 us
    pallas_call x1, Pallas kernels, tile_grads(): pl.pallas_call(grads_kernel, in_specs=[SMEM] + [VMEM] * 5, out_specs=[HBM...  7.47 us
  transfers between devices with their start and end apart: 37, of which 18 were waited for; matrix products, arithmetic and copies ran while one was open for 0% of the time, Pallas kernels for 0%

profile of v2, /device:TPU:2, one launch (start us, length us, event | category | flops | bytes accessed | tf_op | source)
XLA Modules:
  0.0 148.7 jit_solution(565904583015379356)
XLA Ops:
  0.6 3.4 %copy-done = bf16[4096,1024]{1,0:T(8,128)(2,1)S(1)} copy-done((bf16[4096,1024]{1,0:T(8,128)(2,1)S(1)}, bf16[4096,1024]{1,0:T(8,128)(2,1)}, u32[]{:S(2)}) %copy-start) | copy-done | bytes 8388632
  6.8 5.6 %embed.1 = (bf16[64,1152]{1,0:T(8,128)(2,1)S(1)}, bf16[1024,1024]{1,0:T(8,128)(2,1)S(1)}, f32[128,1024]{1,0:T(8,128)S(1)}, f32[128,128]{1,0:T(8,128)S(1)}) custom-call(bf16[64,4096]{1,0:T(8,128)(2,1)S(1)} %copy-done.4, bf16[64,4096]{1,0:T(8,128)(2,1)S(1)} %copy-done.5, bf16[4096,1024]{1,0:T(8,128)(2,1)S(1)} %copy-done, s32[1,64]{1,0:T(1,128)S(1)} %bitcast.12), custom_call_target="tpu_custom_call" | custom-call | tf_op jit(solution)/shard_map/embed/pallas_call | solution.py:114
  15.1 7.5 %all-to-all-start = ((bf16[16,64,1024]{2,1,0:T(8,128)(2,1)}), bf16[16,64,1024]{2,1,0:T(8,128)(2,1)S(1)}, u32[]{:S(2)}, u32[]{:S(2)}) async-start(bf16[16,64,1024]{2,1,0:T(8,128)(2,1)} %bitcast.11), calls=%async_computation | async-start | bytes 4194304 | tf_op jit(solution)/shard_map/all_to_all | solution.py:440
  22.6 5.9 %collective-permute-start = (bf16[64,1152]{1,0:T(8,128)(2,1)S(1)}, bf16[64,1152]{1,0:T(8,128)(2,1)S(1)}, u32[]{:S(2)}, u32[]{:S(2)}) collective-permute-start(bf16[64,1152]{1,0:T(8,128)(2,1)S(1)} %get-tuple-element.31.refs_0_), channel_id=1, source_target_pairs={{0,14},{2,0},{4,2},{6,4},{8,6},{10,8},{12,10},{14,12},{1,15},{3,1}... | collective-permute-start | bytes 442376 | tf_op jit(solution)/shard_map/ppermute | solution.py:30
  28.4 2.7 %collective-permute-done.refs_1_ = bf16[64,1152]{1,0:T(8,128)(2,1)S(1)} collective-permute-done((bf16[64,1152]{1,0:T(8,128)(2,1)S(1)}, bf16[64,1152]{1,0:T(8,128)(2,1)S(1)}, u32[]{:S(2)}, u32[]{:S(2)}) %collective-permute-start) | collective-permute-done | bytes 147488 | tf_op jit(solution)/shard_map/ppermute | solution.py:30
  31.1 3.7 %collective-permute-start.1 = (bf16[64,1152]{1,0:T(8,128)(2,1)S(1)}, bf16[64,1152]{1,0:T(8,128)(2,1)S(1)}, u32[]{:S(2)}, u32[]{:S(2)}) collective-permute-start(bf16[64,1152]{1,0:T(8,128)(2,1)S(1)} %collective-permute-done.refs_1_), channel_id=1, source_target_pairs={{0,14},{2,0},{4,2},{6,4},{8,6},{10,8},{12,10},{14,12},{1,15},{3,1}... | collective-permute-start | bytes 442376 | tf_op jit(solution)/shard_map/ppermute | solution.py:30
  34.8 2.7 %collective-permute-done.1.refs_2_ = bf16[64,1152]{1,0:T(8,128)(2,1)S(1)} collective-permute-done((bf16[64,1152]{1,0:T(8,128)(2,1)S(1)}, bf16[64,1152]{1,0:T(8,128)(2,1)S(1)}, u32[]{:S(2)}, u32[]{:S(2)}) %collective-permute-start.1) | collective-permute-done | bytes 147488 | tf_op jit(solution)/shard_map/ppermute | solution.py:30
  37.4 3.7 %collective-permute-start.2 = (bf16[64,1152]{1,0:T(8,128)(2,1)S(1)}, bf16[64,1152]{1,0:T(8,128)(2,1)S(1)}, u32[]{:S(2)}, u32[]{:S(2)}) collective-permute-start(bf16[64,1152]{1,0:T(8,128)(2,1)S(1)} %collective-permute-done.1.refs_2_), channel_id=1, source_target_pairs={{0,14},{2,0},{4,2},{6,4},{8,6},{10,8},{12,10},{14,12},{1,15},{3,1}... | collective-permute-start | bytes 442376 | tf_op jit(solution)/shard_map/ppermute | solution.py:30
  41.7 2.1 %collective-permute-done.2.refs_3_ = bf16[64,1152]{1,0:T(8,128)(2,1)S(1)} collective-permute-done((bf16[64,1152]{1,0:T(8,128)(2,1)S(1)}, bf16[64,1152]{1,0:T(8,128)(2,1)S(1)}, u32[]{:S(2)}, u32[]{:S(2)}) %collective-permute-start.2) | collective-permute-done | bytes 147488 | tf_op jit(solution)/shard_map/ppermute | solution.py:30
  43.8 3.7 %collective-permute-start.3 = (bf16[64,1152]{1,0:T(8,128)(2,1)S(1)}, bf16[64,1152]{1,0:T(8,128)(2,1)}, u32[]{:S(2)}, u32[]{:S(2)}) collective-permute-start(bf16[64,1152]{1,0:T(8,128)(2,1)S(1)} %collective-permute-done.2.refs_3_), channel_id=1, source_target_pairs={{0,14},{2,0},{4,2},{6,4},{8,6},{10,8},{12,10},{14,12},{1,15},{3,1}... | collective-permute-start | bytes 442376 | tf_op jit(solution)/shard_map/ppermute | solution.py:30
  51.9 9.1 %logits.1 = (f32[1024,1024]{1,0:T(8,128)S(1)}, bf16[1024,1152]{1,0:T(8,128)(2,1)S(1)}, bf16[1024,1024]{1,0:T(8,128)(2,1)S(1)}, f32[16,128]{1,0:T(8,128)S(1)}, f32[1,1024]{1,0:T(1,128)S(1)}) custom-call(s32[2]{0:T(128)S(1)} %pad_add_fusion.place_ref, bf16[64,1152]{1,0:T(8,128)(2,1)S(1)} %get-tuple-element.31.refs_0_, ...), custom_call_target="tpu_custom_call" | custom-call | tf_op jit(solution)/shard_map/logits/pallas_call | solution.py:201
  62.2 4.4 %collective-permute-start.19 = (f32[1,1024]{1,0:T(1,128)S(1)}, f32[1,1024]{1,0:T(1,128)S(1)}, u32[]{:S(2)}, u32[]{:S(2)}) collective-permute-start(f32[1,1024]{1,0:T(1,128)S(1)} %get-tuple-element.35), channel_id=1, source_target_pairs={{0,16},{16,0},{32,48},{48,32},{1,17},{17,1},{33,49},{49,33},{2,18}... | collective-permute-start | bytes 12296 | tf_op jit(solution)/shard_map/ppermute | solution.py:34
  66.6 3.3 %collective-permute-start.17 = (f32[16,128]{1,0:T(8,128)S(1)}, f32[16,128]{1,0:T(8,128)S(1)}, u32[]{:S(2)}, u32[]{:S(2)}) collective-permute-start(f32[16,128]{1,0:T(8,128)S(1)} %add.25), channel_id=1, source_target_pairs={{0,4},{2,6},{4,0},{6,2},{8,12},{10,14},{12,8},{14,10},{1,5},{3,7},... | collective-permute-start | bytes 24584 | tf_op jit(solution)/shard_map/ppermute | solution.py:34
  70.3 4.8 %collective-permute-done.20 = f32[1,1024]{1,0:T(1,128)S(1)} collective-permute-done((f32[1,1024]{1,0:T(1,128)S(1)}, f32[1,1024]{1,0:T(1,128)S(1)}, u32[]{:S(2)}, u32[]{:S(2)}) %collective-permute-start.20) | collective-permute-done | bytes 4128 | tf_op jit(solution)/shard_map/ppermute | solution.py:34
  75.7 4.5 %collective-permute-start.18 = (f32[16,128]{1,0:T(8,128)S(1)}, f32[16,128]{1,0:T(8,128)S(1)}, u32[]{:S(2)}, u32[]{:S(2)}) collective-permute-start(f32[16,128]{1,0:T(8,128)S(1)} %add.26), channel_id=1, source_target_pairs={{0,8},{2,10},{4,12},{6,14},{8,0},{10,2},{12,4},{14,6},{1,9},{3,11}... | collective-permute-start | bytes 24584 | tf_op jit(solution)/shard_map/ppermute | solution.py:34
  80.3 2.5 %collective-permute-start.22 = (f32[1,1024]{1,0:T(1,128)S(1)}, f32[1,1024]{1,0:T(1,128)S(1)}, u32[]{:S(2)}, u32[]{:S(2)}) collective-permute-start(f32[1,1024]{1,0:T(1,128)S(1)} %add.30), channel_id=1, source_target_pairs={{0,128},{64,192},{128,0},{192,64},{1,129},{65,193},{129,1},{193,65... | collective-permute-start | bytes 12296 | tf_op jit(solution)/shard_map/ppermute | solution.py:34
  82.8 2.7 %collective-permute-done.22 = f32[1,1024]{1,0:T(1,128)S(1)} collective-permute-done((f32[1,1024]{1,0:T(1,128)S(1)}, f32[1,1024]{1,0:T(1,128)S(1)}, u32[]{:S(2)}, u32[]{:S(2)}) %collective-permute-start.22) | collective-permute-done | bytes 4128 | tf_op jit(solution)/shard_map/ppermute | solution.py:34
  85.5 7.5 %grads.1 = (bf16[1024,1152]{1,0:T(8,128)(2,1)S(1)}, bf16[8,64,1024]{2,1,0:T(8,128)(2,1)S(1)}, bf16[8,64,1024]{2,1,0:T(8,128)(2,1)S(1)}, f32[1,128]{1,0:T(1,128)S(1)}) custom-call(s32[2]{0:T(128)S(1)} %pad_add_fusion.place_ref, f32[1024,1024]{1,0:T(8,128)S(1)} %get-tuple-element.33.exp_ref, f32[16,128]{1,0:T(8,128)S(1)} %add.27.row_ref, ...), custom_call_target="tpu_custom_call" | custom-call | tf_op jit(solution)/shard_map/grads/pallas_call | solution.py:286
  95.4 6.5 %all-to-all-start.1 = ((bf16[16,64,1152]{2,1,0:T(8,128)(2,1)}), bf16[16,64,1152]{2,1,0:T(8,128)(2,1)S(1)}, u32[]{:S(2)}, u32[]{:S(2)}) async-start(bf16[16,64,1152]{2,1,0:T(8,128)(2,1)} %bitcast.10), calls=%async_computation.1 | async-start | bytes 4718592 | tf_op jit(solution)/shard_map/all_to_all | solution.py:451
  102.4 1.8 %collective-permute-done.24.refs_3_ = f32[1,128]{1,0:T(1,128)S(1)} collective-permute-done((f32[1,128]{1,0:T(1,128)S(1)}, f32[1,128]{1,0:T(1,128)S(1)}, u32[]{:S(2)}, u32[]{:S(2)}) %collective-permute-start.24) | collective-permute-done | bytes 544 | tf_op jit(solution)/shard_map/ppermute | solution.py:34
  106.9 3.6 %collective-permute-done.26.refs_6_ = f32[1,128]{1,0:T(1,128)S(1)} collective-permute-done((f32[1,128]{1,0:T(1,128)S(1)}, f32[1,128]{1,0:T(1,128)S(1)}, u32[]{:S(2)}, u32[]{:S(2)}) %collective-permute-start.26) | collective-permute-done | bytes 544 | tf_op jit(solution)/shard_map/ppermute | solution.py:34
  110.6 2.5 %collective-permute-start.27 = (bf16[64,1024]{1,0:T(8,128)(2,1)S(1)}, bf16[64,1024]{1,0:T(8,128)(2,1)S(1)}, u32[]{:S(2)}, u32[]{:S(2)}) collective-permute-start(bf16[64,1024]{1,0:T(8,128)(2,1)S(1)} %get-tuple-element.43), channel_id=1, source_target_pairs={{0,14},{2,0},{4,2},{6,4},{8,6},{10,8},{12,10},{14,12},{1,15},{3,1}... | collective-permute-start | bytes 393224 | tf_op jit(solution)/shard_map/ppermute | solution.py:30
  114.3 3.2 %collective-permute-done.29.refs_7_ = f32[1,128]{1,0:T(1,128)S(1)} collective-permute-done((f32[1,128]{1,0:T(1,128)S(1)}, f32[1,128]{1,0:T(1,128)S(1)}, u32[]{:S(2)}, u32[]{:S(2)}) %collective-permute-start.29) | collective-permute-done | bytes 544 | tf_op jit(solution)/shard_map/ppermute | solution.py:34
  117.5 1.7 %collective-permute-done.28.refs_5_ = bf16[64,1024]{1,0:T(8,128)(2,1)S(1)} collective-permute-done((bf16[64,1024]{1,0:T(8,128)(2,1)S(1)}, bf16[64,1024]{1,0:T(8,128)(2,1)S(1)}, u32[]{:S(2)}, u32[]{:S(2)}) %collective-permute-start.28) | collective-permute-done | bytes 131104 | tf_op jit(solution)/shard_map/ppermute | solution.py:30
  119.4 1.6 %collective-permute-start.30 = (bf16[64,1024]{1,0:T(8,128)(2,1)S(1)}, bf16[64,1024]{1,0:T(8,128)(2,1)S(1)}, u32[]{:S(2)}, u32[]{:S(2)}) collective-permute-start(bf16[64,1024]{1,0:T(8,128)(2,1)S(1)} %get-tuple-element.46), channel_id=1, source_target_pairs={{0,14},{2,0},{4,2},{6,4},{8,6},{10,8},{12,10},{14,12},{1,15},{3,1}... | collective-permute-start | bytes 393224 | tf_op jit(solution)/shard_map/ppermute | solution.py:30
  121.5 3.3 %collective-permute-start.32 = (f32[1,128]{1,0:T(1,128)S(1)}, f32[1,128]{1,0:T(1,128)S(1)}, u32[]{:S(2)}, u32[]{:S(2)}) collective-permute-start(f32[1,128]{1,0:T(1,128)S(1)} %get-tuple-element.48.refs_8_), channel_id=1, source_target_pairs={{0,8},{2,10},{4,12},{6,14},{8,0},{10,2},{12,4},{14,6},{1,9},{3,11}... | collective-permute-start | bytes 1544 | tf_op jit(solution)/shard_map/ppermute | solution.py:34
  124.7 4.2 %collective-permute-done.32.refs_9_ = f32[1,128]{1,0:T(1,128)S(1)} collective-permute-done((f32[1,128]{1,0:T(1,128)S(1)}, f32[1,128]{1,0:T(1,128)S(1)}, u32[]{:S(2)}, u32[]{:S(2)}) %collective-permute-start.32) | collective-permute-done | bytes 544 | tf_op jit(solution)/shard_map/ppermute | solution.py:34
  129.1 2.8 %collective-permute-start.33 = (bf16[64,1024]{1,0:T(8,128)(2,1)S(1)}, bf16[64,1024]{1,0:T(8,128)(2,1)S(1)}, u32[]{:S(2)}, u32[]{:S(2)}) collective-permute-start(bf16[64,1024]{1,0:T(8,128)(2,1)S(1)} %get-tuple-element.50), channel_id=1, source_target_pairs={{0,14},{2,0},{4,2},{6,4},{8,6},{10,8},{12,10},{14,12},{1,15},{3,1}... | collective-permute-start | bytes 393224 | tf_op jit(solution)/shard_map/ppermute | solution.py:30
  131.9 2.5 %collective-permute-done.33.down_ref = bf16[64,1024]{1,0:T(8,128)(2,1)S(1)} collective-permute-done((bf16[64,1024]{1,0:T(8,128)(2,1)S(1)}, bf16[64,1024]{1,0:T(8,128)(2,1)S(1)}, u32[]{:S(2)}, u32[]{:S(2)}) %collective-permute-start.33) | collective-permute-done | bytes 131104 | tf_op jit(solution)/shard_map/ppermute | solution.py:30
  134.4 3.7 %collective-permute-done.34.up_ref = bf16[64,1024]{1,0:T(8,128)(2,1)S(1)} collective-permute-done((bf16[64,1024]{1,0:T(8,128)(2,1)S(1)}, bf16[64,1024]{1,0:T(8,128)(2,1)S(1)}, u32[]{:S(2)}, u32[]{:S(2)}) %collective-permute-start.34) | collective-permute-done | bytes 131104 | tf_op jit(solution)/shard_map/ppermute | solution.py:30
  138.0 3.4 %copy-done.1 = bf16[4096,1024]{1,0:T(8,128)(2,1)S(1)} copy-done((bf16[4096,1024]{1,0:T(8,128)(2,1)S(1)}, bf16[4096,1024]{1,0:T(8,128)(2,1)}, u32[]{:S(2)}) %copy-start.1) | copy-done | bytes 8388632
  143.3 5.3 %final.1 = (f32[1,1]{1,0:T(1,128)}, f32[64,4096]{1,0:T(8,128)}, f32[64,4096]{1,0:T(8,128)}) custom-call(bf16[64,1024]{1,0:T(8,128)(2,1)S(1)} %get-tuple-element.49.base_ref, bf16[64,1024]{1,0:T(8,128)(2,1)S(1)} %collective-permute-done.33.down_ref, bf16[64,1024]{1,0:T(8,128)(2,1)S(1)} %collective-permute-done.34.up_ref, ...), custom_call_target="tpu_custom_call" | custom-call | tf_op jit(solution)/shard_map/final/pallas_call | solution.py:407
  (83 shorter events, 22.3 us)
Async XLA Ops:
  15.1 36.8 %all-to-all-start = ((bf16[16,64,1024]{2,1,0:T(8,128)(2,1)}), bf16[16,64,1024]{2,1,0:T(8,128)(2,1)S(1)}, u32[]{:S(2)}, u32[]{:S(2)}) async-start(bf16[16,64,1024]{2,1,0:T(8,128)(2,1)} %bitcast.11), calls=%async_computation | async-start | bytes 4194304 | tf_op jit(solution)/shard_map/all_to_all | solution.py:440
  22.6 8.5 %collective-permute-start = (bf16[64,1152]{1,0:T(8,128)(2,1)S(1)}, bf16[64,1152]{1,0:T(8,128)(2,1)S(1)}, u32[]{:S(2)}, u32[]{:S(2)}) collective-permute-start(bf16[64,1152]{1,0:T(8,128)(2,1)S(1)} %get-tuple-element.31.refs_0_), channel_id=1, source_target_pairs={{0,14},{2,0},{4,2},{6,4},{8,6},{10,8},{12,10},{14,12},{1,15},{3,1}... | collective-permute-start | bytes 442376 | tf_op jit(solution)/shard_map/ppermute | solution.py:30
  28.4 6.4 %collective-permute-start.4 = (bf16[64,1152]{1,0:T(8,128)(2,1)S(1)}, bf16[64,1152]{1,0:T(8,128)(2,1)S(1)}, u32[]{:S(2)}, u32[]{:S(2)}) collective-permute-start(bf16[64,1152]{1,0:T(8,128)(2,1)S(1)} %get-tuple-element.31.refs_0_), channel_id=1, source_target_pairs={{0,2},{2,4},{4,6},{6,8},{8,10},{10,12},{12,14},{14,0},{1,3},{3,5},... | collective-permute-start | bytes 442376 | tf_op jit(solution)/shard_map/ppermute | solution.py:30
  31.1 6.4 %collective-permute-start.1 = (bf16[64,1152]{1,0:T(8,128)(2,1)S(1)}, bf16[64,1152]{1,0:T(8,128)(2,1)S(1)}, u32[]{:S(2)}, u32[]{:S(2)}) collective-permute-start(bf16[64,1152]{1,0:T(8,128)(2,1)S(1)} %collective-permute-done.refs_1_), channel_id=1, source_target_pairs={{0,14},{2,0},{4,2},{6,4},{8,6},{10,8},{12,10},{14,12},{1,15},{3,1}... | collective-permute-start | bytes 442376 | tf_op jit(solution)/shard_map/ppermute | solution.py:30
  34.8 6.9 %collective-permute-start.5 = (bf16[64,1152]{1,0:T(8,128)(2,1)S(1)}, bf16[64,1152]{1,0:T(8,128)(2,1)S(1)}, u32[]{:S(2)}, u32[]{:S(2)}) collective-permute-start(bf16[64,1152]{1,0:T(8,128)(2,1)S(1)} %collective-permute-done.4.refs_7_), channel_id=1, source_target_pairs={{0,2},{2,4},{4,6},{6,8},{8,10},{10,12},{12,14},{14,0},{1,3},{3,5},... | collective-permute-start | bytes 442376 | tf_op jit(solution)/shard_map/ppermute | solution.py:30
  37.4 6.4 %collective-permute-start.2 = (bf16[64,1152]{1,0:T(8,128)(2,1)S(1)}, bf16[64,1152]{1,0:T(8,128)(2,1)S(1)}, u32[]{:S(2)}, u32[]{:S(2)}) collective-permute-start(bf16[64,1152]{1,0:T(8,128)(2,1)S(1)} %collective-permute-done.1.refs_2_), channel_id=1, source_target_pairs={{0,14},{2,0},{4,2},{6,4},{8,6},{10,8},{12,10},{14,12},{1,15},{3,1}... | collective-permute-start | bytes 442376 | tf_op jit(solution)/shard_map/ppermute | solution.py:30
  41.1 6.4 %collective-permute-start.7 = (bf16[64,1152]{1,0:T(8,128)(2,1)S(1)}, bf16[64,1152]{1,0:T(8,128)(2,1)S(1)}, u32[]{:S(2)}, u32[]{:S(2)}) collective-permute-start(bf16[64,1152]{1,0:T(8,128)(2,1)S(1)} %get-tuple-element.31.refs_0_), channel_id=1, source_target_pairs={{0,1},{1,0},{2,3},{3,2},{4,5},{5,4},{6,7},{7,6},{8,9},{9,8},{10,11... | collective-permute-start | bytes 442376 | tf_op jit(solution)/shard_map/ppermute | solution.py:34
  41.1 6.4 %collective-permute-start.14 = (bf16[64,1152]{1,0:T(8,128)(2,1)S(1)}, bf16[64,1152]{1,0:T(8,128)(2,1)S(1)}, u32[]{:S(2)}, u32[]{:S(2)}) collective-permute-start(bf16[64,1152]{1,0:T(8,128)(2,1)S(1)} %collective-permute-done.4.refs_7_), channel_id=1, source_target_pairs={{0,1},{1,0},{2,3},{3,2},{4,5},{5,4},{6,7},{7,6},{8,9},{9,8},{10,11... | collective-permute-start | bytes 442376 | tf_op jit(solution)/shard_map/ppermute | solution.py:34
  41.6 6.4 %collective-permute-start.8 = (bf16[64,1152]{1,0:T(8,128)(2,1)S(1)}, bf16[64,1152]{1,0:T(8,128)(2,1)S(1)}, u32[]{:S(2)}, u32[]{:S(2)}) collective-permute-start(bf16[64,1152]{1,0:T(8,128)(2,1)S(1)} %collective-permute-done.refs_1_), channel_id=1, source_target_pairs={{0,1},{1,0},{2,3},{3,2},{4,5},{5,4},{6,7},{7,6},{8,9},{9,8},{10,11... | collective-permute-start | bytes 442376 | tf_op jit(solution)/shard_map/ppermute | solution.py:34
  41.6 7.6 %collective-permute-start.6 = (bf16[64,1152]{1,0:T(8,128)(2,1)S(1)}, bf16[64,1152]{1,0:T(8,128)(2,1)}, u32[]{:S(2)}, u32[]{:S(2)}) collective-permute-start(bf16[64,1152]{1,0:T(8,128)(2,1)S(1)} %collective-permute-done.5.refs_6_), channel_id=1, source_target_pairs={{0,2},{2,4},{4,6},{6,8},{8,10},{10,12},{12,14},{14,0},{1,3},{3,5},... | collective-permute-start | bytes 442376 | tf_op jit(solution)/shard_map/ppermute | solution.py:30
  43.8 6.4 %collective-permute-start.3 = (bf16[64,1152]{1,0:T(8,128)(2,1)S(1)}, bf16[64,1152]{1,0:T(8,128)(2,1)}, u32[]{:S(2)}, u32[]{:S(2)}) collective-permute-start(bf16[64,1152]{1,0:T(8,128)(2,1)S(1)} %collective-permute-done.2.refs_3_), channel_id=1, source_target_pairs={{0,14},{2,0},{4,2},{6,4},{8,6},{10,8},{12,10},{14,12},{1,15},{3,1}... | collective-permute-start | bytes 442376 | tf_op jit(solution)/shard_map/ppermute | solution.py:30
  47.5 2.8 %collective-permute-start.13 = (bf16[64,1152]{1,0:T(8,128)(2,1)S(1)}, bf16[64,1152]{1,0:T(8,128)(2,1)}, u32[]{:S(2)}, u32[]{:S(2)}) collective-permute-start(bf16[64,1152]{1,0:T(8,128)(2,1)S(1)} %collective-permute-done.5.refs_6_), channel_id=1, source_target_pairs={{0,1},{1,0},{2,3},{3,2},{4,5},{5,4},{6,7},{7,6},{8,9},{9,8},{10,11... | collective-permute-start | bytes 442376 | tf_op jit(solution)/shard_map/ppermute | solution.py:34
  48.0 2.9 %collective-permute-start.10 = (bf16[64,1152]{1,0:T(8,128)(2,1)S(1)}, bf16[64,1152]{1,0:T(8,128)(2,1)}, u32[]{:S(2)}, u32[]{:S(2)}) collective-permute-start(bf16[64,1152]{1,0:T(8,128)(2,1)S(1)} %collective-permute-done.2.refs_3_), channel_id=1, source_target_pairs={{0,1},{1,0},{2,3},{3,2},{4,5},{5,4},{6,7},{7,6},{8,9},{9,8},{10,11... | collective-permute-start | bytes 442376 | tf_op jit(solution)/shard_map/ppermute | solution.py:34
  62.2 4.4 %collective-permute-start.16 = (f32[16,128]{1,0:T(8,128)S(1)}, f32[16,128]{1,0:T(8,128)S(1)}, u32[]{:S(2)}, u32[]{:S(2)}) collective-permute-start(f32[16,128]{1,0:T(8,128)S(1)} %add.24), channel_id=1, source_target_pairs={{0,2},{2,0},{4,6},{6,4},{8,10},{10,8},{12,14},{14,12},{1,3},{3,1},... | collective-permute-start | bytes 24584 | tf_op jit(solution)/shard_map/ppermute | solution.py:34
  62.2 7.6 %collective-permute-start.19 = (f32[1,1024]{1,0:T(1,128)S(1)}, f32[1,1024]{1,0:T(1,128)S(1)}, u32[]{:S(2)}, u32[]{:S(2)}) collective-permute-start(f32[1,1024]{1,0:T(1,128)S(1)} %get-tuple-element.35), channel_id=1, source_target_pairs={{0,16},{16,0},{32,48},{48,32},{1,17},{17,1},{33,49},{49,33},{2,18}... | collective-permute-start | bytes 12296 | tf_op jit(solution)/shard_map/ppermute | solution.py:34
  66.6 9.1 %collective-permute-start.17 = (f32[16,128]{1,0:T(8,128)S(1)}, f32[16,128]{1,0:T(8,128)S(1)}, u32[]{:S(2)}, u32[]{:S(2)}) collective-permute-start(f32[16,128]{1,0:T(8,128)S(1)} %add.25), channel_id=1, source_target_pairs={{0,4},{2,6},{4,0},{6,2},{8,12},{10,14},{12,8},{14,10},{1,5},{3,7},... | collective-permute-start | bytes 24584 | tf_op jit(solution)/shard_map/ppermute | solution.py:34
  69.9 5.2 %collective-permute-start.20 = (f32[1,1024]{1,0:T(1,128)S(1)}, f32[1,1024]{1,0:T(1,128)S(1)}, u32[]{:S(2)}, u32[]{:S(2)}) collective-permute-start(f32[1,1024]{1,0:T(1,128)S(1)} %add.28), channel_id=1, source_target_pairs={{0,32},{16,48},{32,0},{48,16},{1,33},{17,49},{33,1},{49,17},{2,34}... | collective-permute-start | bytes 12296 | tf_op jit(solution)/shard_map/ppermute | solution.py:34
  75.1 5.2 %collective-permute-start.21 = (f32[1,1024]{1,0:T(1,128)S(1)}, f32[1,1024]{1,0:T(1,128)S(1)}, u32[]{:S(2)}, u32[]{:S(2)}) collective-permute-start(f32[1,1024]{1,0:T(1,128)S(1)} %add.29), channel_id=1, source_target_pairs={{0,64},{64,0},{128,192},{192,128},{1,65},{65,1},{129,193},{193,129... | collective-permute-start | bytes 12296 | tf_op jit(solution)/shard_map/ppermute | solution.py:34
  75.7 9.8 %collective-permute-start.18 = (f32[16,128]{1,0:T(8,128)S(1)}, f32[16,128]{1,0:T(8,128)S(1)}, u32[]{:S(2)}, u32[]{:S(2)}) collective-permute-start(f32[16,128]{1,0:T(8,128)S(1)} %add.26), channel_id=1, source_target_pairs={{0,8},{2,10},{4,12},{6,14},{8,0},{10,2},{12,4},{14,6},{1,9},{3,11}... | collective-permute-start | bytes 24584 | tf_op jit(solution)/shard_map/ppermute | solution.py:34
  80.3 5.2 %collective-permute-start.22 = (f32[1,1024]{1,0:T(1,128)S(1)}, f32[1,1024]{1,0:T(1,128)S(1)}, u32[]{:S(2)}, u32[]{:S(2)}) collective-permute-start(f32[1,1024]{1,0:T(1,128)S(1)} %add.30), channel_id=1, source_target_pairs={{0,128},{64,192},{128,0},{192,64},{1,129},{65,193},{129,1},{193,65... | collective-permute-start | bytes 12296 | tf_op jit(solution)/shard_map/ppermute | solution.py:34
  95.4 42.7 %all-to-all-start.1 = ((bf16[16,64,1152]{2,1,0:T(8,128)(2,1)}), bf16[16,64,1152]{2,1,0:T(8,128)(2,1)S(1)}, u32[]{:S(2)}, u32[]{:S(2)}) async-start(bf16[16,64,1152]{2,1,0:T(8,128)(2,1)} %bitcast.10), calls=%async_computation.1 | async-start | bytes 4718592 | tf_op jit(solution)/shard_map/all_to_all | solution.py:451
  101.9 2.9 %collective-permute-start.23 = (bf16[8,64,1024]{2,1,0:T(8,128)(2,1)}, bf16[8,64,1024]{2,1,0:T(8,128)(2,1)S(1)}, u32[]{:S(2)}, u32[]{:S(2)}) collective-permute-start(bf16[8,64,1024]{2,1,0:T(8,128)(2,1)} %copy-done.11), channel_id=1, source_target_pairs={{0,1},{1,0},{2,3},{3,2},{4,5},{5,4},{6,7},{7,6},{8,9},{9,8},{10,11... | collective-permute-start | bytes 3145736 | tf_op jit(solution)/shard_map/ppermute | solution.py:34
  104.8 5.7 %collective-permute-start.25 = (bf16[64,1024]{1,0:T(8,128)(2,1)S(1)}, bf16[64,1024]{1,0:T(8,128)(2,1)S(1)}, u32[]{:S(2)}, u32[]{:S(2)}) collective-permute-start(bf16[64,1024]{1,0:T(8,128)(2,1)S(1)} %get-tuple-element.41), channel_id=1, source_target_pairs={{0,14},{2,0},{4,2},{6,4},{8,6},{10,8},{12,10},{14,12},{1,15},{3,1}... | collective-permute-start | bytes 393224 | tf_op jit(solution)/shard_map/ppermute | solution.py:30
  106.2 4.3 %collective-permute-start.26 = (f32[1,128]{1,0:T(1,128)S(1)}, f32[1,128]{1,0:T(1,128)S(1)}, u32[]{:S(2)}, u32[]{:S(2)}) collective-permute-start(f32[1,128]{1,0:T(1,128)S(1)} %get-tuple-element.42.refs_5_), channel_id=1, source_target_pairs={{0,2},{2,0},{4,6},{6,4},{8,10},{10,8},{12,14},{14,12},{1,3},{3,1},... | collective-permute-start | bytes 1544 | tf_op jit(solution)/shard_map/ppermute | solution.py:34
  110.6 7.0 %collective-permute-start.27 = (bf16[64,1024]{1,0:T(8,128)(2,1)S(1)}, bf16[64,1024]{1,0:T(8,128)(2,1)S(1)}, u32[]{:S(2)}, u32[]{:S(2)}) collective-permute-start(bf16[64,1024]{1,0:T(8,128)(2,1)S(1)} %get-tuple-element.43), channel_id=1, source_target_pairs={{0,14},{2,0},{4,2},{6,4},{8,6},{10,8},{12,10},{14,12},{1,15},{3,1}... | collective-permute-start | bytes 393224 | tf_op jit(solution)/shard_map/ppermute | solution.py:30
  113.1 6.2 %collective-permute-start.28 = (bf16[64,1024]{1,0:T(8,128)(2,1)S(1)}, bf16[64,1024]{1,0:T(8,128)(2,1)S(1)}, u32[]{:S(2)}, u32[]{:S(2)}) collective-permute-start(bf16[64,1024]{1,0:T(8,128)(2,1)S(1)} %get-tuple-element.44), channel_id=1, source_target_pairs={{0,2},{2,4},{4,6},{6,8},{8,10},{10,12},{12,14},{14,0},{1,3},{3,5},... | collective-permute-start | bytes 393224 | tf_op jit(solution)/shard_map/ppermute | solution.py:30
  113.1 4.4 %collective-permute-start.29 = (f32[1,128]{1,0:T(1,128)S(1)}, f32[1,128]{1,0:T(1,128)S(1)}, u32[]{:S(2)}, u32[]{:S(2)}) collective-permute-start(f32[1,128]{1,0:T(1,128)S(1)} %get-tuple-element.45.refs_6_), channel_id=1, source_target_pairs={{0,4},{2,6},{4,0},{6,2},{8,12},{10,14},{12,8},{14,10},{1,5},{3,7},... | collective-permute-start | bytes 1544 | tf_op jit(solution)/shard_map/ppermute | solution.py:34
  119.4 9.6 %collective-permute-start.30 = (bf16[64,1024]{1,0:T(8,128)(2,1)S(1)}, bf16[64,1024]{1,0:T(8,128)(2,1)S(1)}, u32[]{:S(2)}, u32[]{:S(2)}) collective-permute-start(bf16[64,1024]{1,0:T(8,128)(2,1)S(1)} %get-tuple-element.46), channel_id=1, source_target_pairs={{0,14},{2,0},{4,2},{6,4},{8,6},{10,8},{12,10},{14,12},{1,15},{3,1}... | collective-permute-start | bytes 393224 | tf_op jit(solution)/shard_map/ppermute | solution.py:30
  120.9 8.0 %collective-permute-start.31 = (bf16[64,1024]{1,0:T(8,128)(2,1)S(1)}, bf16[64,1024]{1,0:T(8,128)(2,1)S(1)}, u32[]{:S(2)}, u32[]{:S(2)}) collective-permute-start(bf16[64,1024]{1,0:T(8,128)(2,1)S(1)} %get-tuple-element.47), channel_id=1, source_target_pairs={{0,2},{2,4},{4,6},{6,8},{8,10},{10,12},{12,14},{14,0},{1,3},{3,5},... | collective-permute-start | bytes 393224 | tf_op jit(solution)/shard_map/ppermute | solution.py:30
  121.5 7.4 %collective-permute-start.32 = (f32[1,128]{1,0:T(1,128)S(1)}, f32[1,128]{1,0:T(1,128)S(1)}, u32[]{:S(2)}, u32[]{:S(2)}) collective-permute-start(f32[1,128]{1,0:T(1,128)S(1)} %get-tuple-element.48.refs_8_), channel_id=1, source_target_pairs={{0,8},{2,10},{4,12},{6,14},{8,0},{10,2},{12,4},{14,6},{1,9},{3,11}... | collective-permute-start | bytes 1544 | tf_op jit(solution)/shard_map/ppermute | solution.py:34
  129.1 5.3 %collective-permute-start.33 = (bf16[64,1024]{1,0:T(8,128)(2,1)S(1)}, bf16[64,1024]{1,0:T(8,128)(2,1)S(1)}, u32[]{:S(2)}, u32[]{:S(2)}) collective-permute-start(bf16[64,1024]{1,0:T(8,128)(2,1)S(1)} %get-tuple-element.50), channel_id=1, source_target_pairs={{0,14},{2,0},{4,2},{6,4},{8,6},{10,8},{12,10},{14,12},{1,15},{3,1}... | collective-permute-start | bytes 393224 | tf_op jit(solution)/shard_map/ppermute | solution.py:30
  131.8 6.2 %collective-permute-start.34 = (bf16[64,1024]{1,0:T(8,128)(2,1)S(1)}, bf16[64,1024]{1,0:T(8,128)(2,1)S(1)}, u32[]{:S(2)}, u32[]{:S(2)}) collective-permute-start(bf16[64,1024]{1,0:T(8,128)(2,1)S(1)} %get-tuple-element.51), channel_id=1, source_target_pairs={{0,2},{2,4},{4,6},{6,8},{8,10},{10,12},{12,14},{14,0},{1,3},{3,5},... | collective-permute-start | bytes 393224 | tf_op jit(solution)/shard_map/ppermute | solution.py:30
  (17 other events, 26.2 us)

commit v3 on v2

v3 whole, which is shorter than its diff:
```python
import functools

import jax
import jax.numpy as jnp
from jax import lax
from jax.experimental import pallas as pl
from jax.experimental.pallas import tpu as pltpu
from jax.sharding import Mesh, PartitionSpec as P

logit_scale = 20.0
grad_scale = 128.0
norm_eps = 1e-06
log2_e = 1.4426950408889634

NY, NX, NZ, NC = 4, 4, 8, 2
QR = ("y", "x")
PC = ("z", "c")
f32 = jnp.float32
bf16 = jnp.bfloat16
LANES = 128
EXTRA = 16
HBM = pl.BlockSpec(memory_space=pltpu.HBM)
VMEM = pl.BlockSpec(memory_space=pltpu.VMEM)
params = pltpu.CompilerParams(vmem_limit_bytes=24 * 1024 * 1024)
NT = (((1,), (1,)), ((), ()))
TN = (((0,), (0,)), ((), ()))


def shift(value, axis, size, step):
    return lax.ppermute(value, axis, [(i, (i + step) % size) for i in range(size)])


def swap(value, axis, size, bit):
    return lax.ppermute(value, axis, [(i, i ^ bit) for i in range(size)])


pc_steps = (("c", NC, 1), ("z", NZ, 1), ("z", NZ, 2), ("z", NZ, 4))
qr_steps = (("x", NX, 1), ("x", NX, 2), ("y", NY, 1), ("y", NY, 2))


def sds(shape, dtype):
    return jax.ShapeDtypeStruct(shape, dtype)


def in_hbm(value):
    return pltpu.with_memory_space_constraint(value, pltpu.HBM)


def in_vmem(value):
    return pltpu.with_memory_space_constraint(value, pltpu.VMEM)


def fixed(shape):
    return pl.BlockSpec(shape, lambda *i: (0,) * len(shape))


def embed_kernel(
    query_ref,
    passage_ref,
    proj_ref,
    positive_ref,
    message_ref,
    copies_ref,
    state_ref,
    weights,
    pools,
    indices,
    spread,
    state,
    in_sems,
    out_sems,
):
    rows, depth = query_ref.shape
    width = proj_ref.shape[1]
    steps = in_sems.shape[0] - 3
    chunk = depth // steps
    loads = [
        pltpu.make_async_copy(query_ref, pools.at[:rows], in_sems.at[0]),
        pltpu.make_async_copy(passage_ref, pools.at[rows:], in_sems.at[1]),
    ]
    for k in range(steps):
        part = pl.ds(k * chunk, chunk)
        loads.append(pltpu.make_async_copy(proj_ref.at[part], weights.at[part], in_sems.at[k + 2]))
    loads.append(pltpu.make_async_copy(positive_ref, indices, in_sems.at[steps + 2]))
    for load in loads:
        load.start()
    loads[0].wait()
    loads[1].wait()
    raw = jnp.zeros((2 * rows, width), f32)
    for k in range(steps):
        loads[k + 2].wait()
        part = pl.ds(k * chunk, chunk)
        raw = raw + jnp.dot(pools[:, part], weights[part, :], preferred_element_type=f32)
    inv = lax.rsqrt(jnp.sum(raw * raw, axis=-1, keepdims=True) + norm_eps)
    unit = raw * inv
    embed = unit.astype(bf16)
    spread[...] = embed[rows:]
    stores = []
    for k in range(copies_ref.shape[0] // rows):
        part = pl.ds(k * rows, rows)
        stores.append(pltpu.make_async_copy(spread, copies_ref.at[part], out_sems.at[k]))
    for store in stores:
        store.start()
    state[:, :width] = unit
    state[:, width:] = jnp.broadcast_to(inv, (2 * rows, LANES))
    stores.append(pltpu.make_async_copy(state, state_ref, out_sems.at[len(stores)]))
    stores[-1].start()
    message_ref[:, :width] = embed[:rows]
    loads[-1].wait()
    square = (rows, rows)
    line = jnp.broadcast_to(indices[...].astype(f32), square)
    on = lax.broadcasted_iota(jnp.int32, square, 0) == lax.broadcasted_iota(jnp.int32, square, 1)
    index = jnp.sum(jnp.where(on, line, 0.0), axis=1, keepdims=True)
    high = jnp.floor(index * (1.0 / LANES))
    low = index - high * LANES
    lane = lax.broadcasted_iota(jnp.int32, (rows, LANES), 1)
    message_ref[:, width:] = jnp.where(lane == 0, high, jnp.where(lane == 1, low, 0.0)).astype(bf16)
    for store in stores:
        store.wait()


def embed(query_pool, passage_pool, proj, positive):
    rows, depth = query_pool.shape
    width = proj.shape[1]
    copies = NY * NX
    steps = 8
    return pl.pallas_call(
        embed_kernel,
        in_specs=[HBM] * 4,
        out_specs=[VMEM, HBM, HBM],
        out_shape=[
            sds((rows, width + LANES), bf16),
            pltpu.HBM((copies * rows, width), bf16),
            pltpu.HBM((2 * rows, width + LANES), f32),
        ],
        scratch_shapes=[
            pltpu.VMEM((depth, width), bf16),
            pltpu.VMEM((2 * rows, depth), bf16),
            pltpu.VMEM((1, rows), jnp.int32),
            pltpu.VMEM((rows, width), bf16),
            pltpu.VMEM((2 * rows, width + LANES), f32),
            pltpu.SemaphoreType.DMA((steps + 3,)),
            pltpu.SemaphoreType.DMA((copies + 1,)),
        ],
        compiler_params=params,
        name="embed",
    )(*map(in_hbm, (query_pool, passage_pool, proj, positive)))


def positive_column(query_ref, part, width, columns):
    words = query_ref[part, width:].astype(f32)
    index = words[:, 0:1] * LANES + words[:, 1:2]
    first = (lax.axis_index("z") * NC + lax.axis_index("c")) * columns
    return index.astype(jnp.int32) - first


def line_of(k):
    z = lax.rem(lax.axis_index("z") + k % NZ, NZ)
    c = lax.axis_index("c")
    return pl.ds((c if k < NZ else 1 - c) * NZ + z, 1)


def logits_kernel(*refs):
    pieces = refs[: NZ * NC]
    passage_ref, exp_ref, query_ref, row_ref, col_ref, row_acc, in_sems = refs[NZ * NC :]
    own = pieces[0].shape[0]
    columns, width = passage_ref.shape
    rows = query_ref.shape[0]
    loads = []
    for k, piece in enumerate(pieces):
        loads.append(pltpu.make_async_copy(piece, query_ref.at[pl.ds(k * own, own)], in_sems.at[k]))
        loads[-1].start()
    steps = 2
    each = rows // steps
    picked = jnp.zeros((1, columns), f32)
    col_sum = jnp.zeros((1, columns), f32)
    for k in range(steps):
        for load in loads[k * each // own : (k + 1) * each // own]:
            load.wait()
        part = pl.ds(k * each, each)
        positive = positive_column(query_ref, part, width, columns)
        dots = lax.dot_general(
            query_ref[part, :width], passage_ref[...], NT, preferred_element_type=f32
        )
        shifted = jnp.exp2(dots * (logit_scale * log2_e) - logit_scale * log2_e)
        exp_ref[part, :] = shifted
        col_sum = col_sum + jnp.sum(shifted, axis=0, keepdims=True)
        row_part = shifted[:, :LANES]
        for n in range(1, columns // LANES):
            row_part = row_part + shifted[:, n * LANES : (n + 1) * LANES]
        row_acc[part, :] = row_part
        column = lax.broadcasted_iota(jnp.int32, (each, columns), 1)
        found = jnp.where(column == positive, dots, 0.0)
        picked = picked + jnp.sum(found, axis=0, keepdims=True)
    col_ref[...] = col_sum
    total = logit_scale * jnp.sum(picked, axis=1, keepdims=True)
    lane = lax.broadcasted_iota(jnp.int32, (1, LANES), 1)
    for k in range(0, NZ * NC, 2):
        turned = row_acc[k * own : (k + 2) * own, :].T
        line = jnp.sum(turned, axis=0, keepdims=True)
        row_ref[line_of(k), :] = jnp.where(lane < own, line, total)
        line = pltpu.roll(line, own, 1)
        row_ref[line_of(k + 1), :] = jnp.where(lane < own, line, total)


def tile_logits(pieces, passage_tile):
    own, wide = pieces[0].shape
    columns, width = passage_tile.shape
    rows = own * len(pieces)
    return pl.pallas_call(
        logits_kernel,
        in_specs=[HBM] * len(pieces) + [VMEM],
        out_specs=[VMEM] * 4,
        out_shape=[
            pltpu.VMEM((rows, columns), f32),
            pltpu.VMEM((rows, wide), bf16),
            sds((len(pieces), LANES), f32),
            sds((1, columns), f32),
        ],
        scratch_shapes=[
            pltpu.VMEM((rows, LANES), f32),
            pltpu.SemaphoreType.DMA((len(pieces),)),
        ],
        compiler_params=params,
        name="logits",
    )(*map(in_hbm, pieces), in_vmem(passage_tile))


def in_thirds(value, shape):
    high = value.astype(bf16).astype(f32)
    middle = (value - high).astype(bf16).astype(f32)
    low = value - high - middle
    lane = lax.broadcasted_iota(jnp.int32, shape, 1)
    parts = jnp.where(lane == 1, middle, jnp.where(lane == 2, low, 0.0))
    return jnp.where(lane == 0, high, parts).astype(bf16)


def as_tiles(out_ref, block, extra):
    rows, width = block.shape
    for m in range(width // LANES):
        out_ref[m * rows : (m + 1) * rows, :] = block[:, m * LANES : (m + 1) * LANES]
    out_ref[width // LANES * rows :, :] = extra


def grads_kernel(
    exp_ref,
    row_ref,
    col_ref,
    query_ref,
    passage_ref,
    part_ref,
    own_ref,
    other_ref,
    grad,
    row_scale,
    parts,
    sems,
):
    columns, width = passage_ref.shape
    rows = query_ref.shape[0]
    own = rows // (NZ * NC)
    steps = sems.shape[0]
    chunk = columns // steps
    half = 0.5 * grad_scale
    lane = lax.broadcasted_iota(jnp.int32, (1, LANES), 1)
    row_total = logit_scale * rows - 2.0 * row_ref[0:1, own : own + 1]
    for k in range(0, NZ * NC, 2):
        first, second = row_ref[line_of(k), :], row_ref[line_of(k + 1), :]
        line = jnp.where(lane < own, first, pltpu.roll(second, own, 1))
        row_total = row_total + jnp.sum(jnp.log(line), axis=1, keepdims=True)
        turned = jnp.broadcast_to(half / line, (LANES, LANES)).T
        row_scale[k * own : (k + 2) * own, :] = turned
    col_total = jnp.sum(jnp.log(col_ref[...]), axis=1, keepdims=True) + logit_scale * columns
    row_extra = in_thirds(jnp.broadcast_to(row_total, (EXTRA, 1)), (EXTRA, LANES))
    col_extra = in_thirds(jnp.broadcast_to(col_total, (EXTRA, 1)), (EXTRA, LANES))
    positive = positive_column(query_ref, pl.ds(0, rows), width, columns)
    stores = []
    for k in range(steps):
        part = pl.ds(k * chunk, chunk)
        scale = jnp.concatenate([row_scale[...]] * (chunk // LANES), axis=1)
        scale = scale + half / col_ref[:, part]
        column = lax.broadcasted_iota(jnp.int32, (rows, chunk), 1) + k * chunk
        hit = jnp.where(column == positive, grad_scale, 0.0)
        tile = (exp_ref[:, part] * scale - hit).astype(bf16)
        grad[:, part] = tile
        term = lax.dot_general(tile, query_ref[:, :width], TN, preferred_element_type=f32)
        term = (logit_scale * term).astype(bf16)
        blocks = pl.ds(k * chunk // own, chunk // own)
        for n in range(chunk // own):
            as_tiles(parts.at[k * chunk // own + n], term[n * own : (n + 1) * own, :], row_extra)
        stores.append(pltpu.make_async_copy(parts.at[blocks], part_ref.at[blocks], sems.at[k]))
        stores[-1].start()
    for k, out_ref in enumerate((own_ref, other_ref)):
        part = pl.ds(k * NZ * own, NZ * own)
        term = jnp.dot(grad[part, :], passage_ref[...], preferred_element_type=f32)
        term = (logit_scale * term).astype(bf16)
        for n in range(NZ):
            as_tiles(out_ref.at[n], term[n * own : (n + 1) * own, :], col_extra)
    for store in stores:
        store.wait()


def tile_grads(shifted, row_sum, column_sum, query_tile, passage_tile):
    rows, wide = query_tile.shape
    columns, width = passage_tile.shape
    own = rows // (NZ * NC)
    block = (own * width // LANES + EXTRA, LANES)
    steps = 4
    return pl.pallas_call(
        grads_kernel,
        in_specs=[VMEM] * 5,
        out_specs=[HBM, VMEM, VMEM],
        out_shape=[
            pltpu.HBM((columns // own, *block), bf16),
            sds((NZ, *block), bf16),
            sds((NZ, *block), bf16),
        ],
        scratch_shapes=[
            pltpu.VMEM((rows, columns), bf16),
            pltpu.VMEM((rows, LANES), f32),
            pltpu.VMEM((columns // own, *block), bf16),
            pltpu.SemaphoreType.DMA((steps,)),
        ],
        compiler_params=params,
        name="grads",
    )(in_vmem(shifted), row_sum, column_sum, in_vmem(query_tile), in_vmem(passage_tile))


def ring_step(own, other, turns):
    _, height, width = own.shape
    operands, in_specs, kept = [], [], []
    for block, came in turns:
        spec = pl.BlockSpec((1, height, width), lambda i, block=block: (block, 0, 0))
        operands += [own, other]
        in_specs += [spec, spec]
        kept.append(came is not None)
        if came is not None:
            operands.append(came)
            in_specs.append(fixed((height, width)))

    def kernel(*refs):
        refs = list(refs)
        outs = refs[len(operands) :]
        for out, there in zip(outs, kept):
            total = refs.pop(0)[0].astype(f32) + refs.pop(0)[0].astype(f32)
            if there:
                total = total + refs.pop(0)[...].astype(f32)
            out[: height - EXTRA, :] = total[: height - EXTRA].astype(bf16)
            extra = jnp.sum(total[height - EXTRA :], axis=1, keepdims=True)
            out[height - EXTRA :, :] = in_thirds(extra, (EXTRA, LANES))

    count = len(turns)
    return pl.pallas_call(
        kernel,
        grid=(1,),
        in_specs=in_specs,
        out_specs=[fixed((height, width))] * count,
        out_shape=[sds((height, width), bf16)] * count,
        compiler_params=params,
        cost_estimate=pl.CostEstimate(flops=1, bytes_accessed=1, transcendentals=0),
        name="ring",
    )(*operands)


def final_kernel(
    count,
    own_ref,
    other_ref,
    down_ref,
    up_ref,
    proj_ref,
    state_ref,
    terms_ref,
    total_ref,
    query_ref,
    passage_ref,
    weights,
    state,
    terms,
    raw,
    outs,
    in_sems,
    out_sems,
):
    width = proj_ref.shape[1]
    spread = width // LANES
    rows = (down_ref.shape[0] - EXTRA) // spread
    steps = out_sems.shape[0] // 2
    chunk = proj_ref.shape[0] // steps
    groups = in_sems.shape[0] - 1 - steps
    each = terms_ref.shape[0] // groups
    loads = [pltpu.make_async_copy(state_ref, state, in_sems.at[0])]
    for k in range(groups):
        part = pl.ds(k * each, each)
        loads.append(pltpu.make_async_copy(terms_ref.at[part], terms.at[part], in_sems.at[k + 1]))
    for k in range(steps):
        part = pl.ds(k * chunk, chunk)
        sem = in_sems.at[k + 1 + groups]
        loads.append(pltpu.make_async_copy(proj_ref.at[part], weights.at[part], sem))
    for load in loads:
        load.start()

    def back(k, tiles):
        parts = [tiles[m * rows : (m + 1) * rows] for m in range(spread)]
        incoming = jnp.concatenate(parts, axis=1)
        unit = state[k * rows : (k + 1) * rows, :width]
        inv = state[k * rows : (k + 1) * rows, width : width + 1]
        along = jnp.sum(unit * incoming, axis=-1, keepdims=True)
        raw[k * rows : (k + 1) * rows, :] = (inv * (incoming - unit * along)).astype(bf16)
        return jnp.sum(tiles[spread * rows : spread * rows + 1], axis=1, keepdims=True)

    query = own_ref[0].astype(f32) + other_ref[0].astype(f32)
    query = query + down_ref[...].astype(f32) + up_ref[...].astype(f32)
    loads[0].wait()
    total = back(0, query)
    passage = jnp.zeros(terms_ref.shape[1:], f32)
    for k in range(groups):
        loads[k + 1].wait()
        for n in range(k * each, (k + 1) * each):
            passage = passage + terms[n].astype(f32)
    total = total + back(1, passage)
    total_ref[...] = total * (1.0 / count)
    stores = []
    for k in range(steps):
        part = pl.ds(k * chunk, chunk)
        loads[k + 1 + groups].wait()
        outs[:, part] = lax.dot_general(raw[...], weights[part, :], NT, preferred_element_type=f32)
        for n, out_ref in enumerate((query_ref, passage_ref)):
            source = outs.at[pl.ds(n * rows, rows), part]
            store = pltpu.make_async_copy(source, out_ref.at[:, part], out_sems.at[2 * k + n])
            store.start()
            stores.append(store)
    for store in stores:
        store.wait()


def final(count, own, other, down, up, proj, state, terms):
    rows = state.shape[0] // 2
    depth, width = proj.shape
    steps, groups = 8, 4
    block = pl.BlockSpec((1, *own.shape[1:]), lambda i: (0, 0, 0))
    return pl.pallas_call(
        functools.partial(final_kernel, count),
        grid=(1,),
        in_specs=[block] * 2 + [fixed(down.shape)] * 2 + [HBM] * 3,
        out_specs=[fixed((1, 1)), HBM, HBM],
        out_shape=[sds((1, 1), f32)] + [pltpu.HBM((rows, depth), f32)] * 2,
        scratch_shapes=[
            pltpu.VMEM(proj.shape, bf16),
            pltpu.VMEM(state.shape, f32),
            pltpu.VMEM(terms.shape, bf16),
            pltpu.VMEM((2 * rows, width), bf16),
            pltpu.VMEM((2 * rows, depth), f32),
            pltpu.SemaphoreType.DMA((1 + groups + steps,)),
            pltpu.SemaphoreType.DMA((2 * steps,)),
        ],
        compiler_params=params,
        name="final",
    )(own, other, down, up, *map(in_hbm, (proj, state, terms)))


def gather_queries(message):
    pieces = {0: message}
    down = up = message
    for k in range(1, NZ // 2 + 1):
        down = shift(down, "z", NZ, -1)
        pieces[k] = down
        if k < NZ // 2:
            up = shift(up, "z", NZ, 1)
            pieces[NZ - k] = up
    own = [pieces[k] for k in range(NZ)]
    return own + [swap(piece, "c", NC, 1) for piece in own]


def body(query_pool, passage_pool, proj, positive):
    message, copies, state = embed(query_pool, passage_pool, proj, positive[None])
    passage_tile = lax.all_to_all(copies, QR, 0, 0, tiled=True)
    pieces = gather_queries(message)
    shifted, query_tile, row_sum, column_sum = tile_logits(pieces, passage_tile)
    for pc_step, qr_step in zip(pc_steps, qr_steps):
        row_sum = row_sum + swap(row_sum, *pc_step)
        column_sum = column_sum + swap(column_sum, *qr_step)
    partial, own, other = tile_grads(shifted, row_sum, column_sum, query_tile, passage_tile)
    terms = lax.all_to_all(partial, QR, 0, 0, tiled=True)
    other = swap(other, "c", NC, 1)
    (down,) = ring_step(own, other, [(4, None)])
    came = shift(down, "z", NZ, -1)
    down, up = ring_step(own, other, [(5, came), (3, None)])
    for k in (2, 1):
        came = shift(down, "z", NZ, -1), shift(up, "z", NZ, 1)
        down, up = ring_step(own, other, [(NZ - k, came[0]), (k, came[1])])
    down, up = shift(down, "z", NZ, -1), shift(up, "z", NZ, 1)
    count = 2.0 * column_sum.shape[1] * NZ * NC
    total, grad_query_pool, grad_passage_pool = final(
        count, own, other, down, up, proj, state, terms
    )
    return (total.reshape(()), grad_query_pool, grad_passage_pool)


def solution(mesh):
    fine = Mesh(mesh.devices.reshape(NY, NX, NZ, NC), ("y", "x", "z", "c"))
    in_specs = (
        P(("y", "x", "z", "c"), None),
        P(("z", "c", "y", "x"), None),
        P(),
        P(("y", "x", "z", "c")),
    )
    out_specs = (P(), P(("y", "x", "z", "c"), None), P(("z", "c", "y", "x"), None))
    return jax.shard_map(
        body, mesh=fine, in_specs=in_specs, out_specs=out_specs, check_vma=False
    )
```

time: 149 us -> 125 us (0.84)
  local copies, waits for them, and re-layouts: 16.5 us -> 2.37 us
  starting transfers between devices: 62.6 us -> 57.4 us
  Pallas kernels: 27.7 us -> 24.5 us
    unnamed x24 -> x34, local copies, waits for them, and re-layouts: 16.5 us -> 2.37 us
    ppermute x21 -> x17, waiting for transfers between devices: 23.4 us -> 11.4 us  [swap(): return lax.ppermute(value, axis, [(i, i ^ bit) for i in range(size)])]
    ppermute x14, waiting for transfers between devices: 17.5 us -> 28.4 us  [shift(): lax.ppermute(value, axis, [(i, (i + step) % size) for i in range(size)])]
    ppermute x21 -> x17, starting transfers between devices: 22.9 us -> 17.3 us  [swap(): return lax.ppermute(value, axis, [(i, i ^ bit) for i in range(size)])]
    pallas_call x4, Pallas kernels: 27.4 us -> 24 us  [the longest x1 7.37 us: final(): pl.pallas_call(functools.partial(final_kernel, count), grid=(1,), in_spec...]
  transfers between devices with their start and end apart: 37 -> 33, of which waited for: 18 -> 17; matrix products, arithmetic and copies ran while one was open for 0% -> 0% of each run, Pallas kernels for 0% -> 0%
where the time goes in v3:
time: 125 us
  starting transfers between devices  57.4 us (46%)
  waiting for transfers between devices  39.8 us (32%)
  Pallas kernels  24.5 us (20%)
  local copies, waits for them, and re-layouts  2.37 us (2%)
    ppermute x14, waiting for transfers between devices, shift(): lax.ppermute(value, axis, [(i, (i + step) % size) for i in range(size)])  28.4 us
    ppermute x14, starting transfers between devices, shift(): lax.ppermute(value, axis, [(i, (i + step) % size) for i in range(size)])  25.5 us
    ppermute x17, starting transfers between devices, swap(): return lax.ppermute(value, axis, [(i, i ^ bit) for i in range(size)])  17.3 us
    ppermute x17, waiting for transfers between devices, swap(): return lax.ppermute(value, axis, [(i, i ^ bit) for i in range(size)])  11.4 us
    all_to_all x1, starting transfers between devices, body(): passage_tile = lax.all_to_all(copies, QR, 0, 0, tiled=True)  7.49 us
    pallas_call x1, Pallas kernels, final(): pl.pallas_call(functools.partial(final_kernel, count), grid=(1,), in_spec...  7.37 us
    all_to_all x1, starting transfers between devices, body(): terms = lax.all_to_all(partial, QR, 0, 0, tiled=True)  7.11 us
    pallas_call x1, Pallas kernels, embed(): pl.pallas_call(embed_kernel, in_specs=[HBM] * 4, out_specs=[VMEM, HBM, HB...  5.89 us
  transfers between devices with their start and end apart: 33, of which 17 were waited for; matrix products, arithmetic and copies ran while one was open for 0% of the time, Pallas kernels for 0%

profile of v3, /device:TPU:2, one launch (start us, length us, event | category | flops | bytes accessed | tf_op | source)
XLA Modules:
  0.0 125.2 jit_solution(17715213089755955555)
XLA Ops:
  0.6 5.9 %embed.1 = (bf16[64,1152]{1,0:T(8,128)(2,1)S(1)}, bf16[1024,1024]{1,0:T(8,128)(2,1)}, f32[128,1152]{1,0:T(8,128)}) custom-call(bf16[64,4096]{1,0:T(8,128)(2,1)} %query_ref.1, bf16[64,4096]{1,0:T(8,128)(2,1)} %passage_ref.1, bf16[4096,1024]{1,0:T(8,128)(2,1)} %proj_ref.3, s32[1,64]{1,0:T(1,128)} %bitcast.7), custom_call_target="tpu_custom_call" | custom-call | tf_op jit(solution)/shard_map/embed/pallas_call | solution.py:127
  6.5 7.5 %all-to-all-start = ((bf16[16,64,1024]{2,1,0:T(8,128)(2,1)}), bf16[16,64,1024]{2,1,0:T(8,128)(2,1)S(1)}, u32[]{:S(2)}, u32[]{:S(2)}) async-start(bf16[16,64,1024]{2,1,0:T(8,128)(2,1)} %bitcast.6), calls=%async_computation | async-start | bytes 4194304 | tf_op jit(solution)/shard_map/all_to_all | solution.py:477
  14.0 5.9 %collective-permute-start = (bf16[64,1152]{1,0:T(8,128)(2,1)S(1)}, bf16[64,1152]{1,0:T(8,128)(2,1)S(1)}, u32[]{:S(2)}, u32[]{:S(2)}) collective-permute-start(bf16[64,1152]{1,0:T(8,128)(2,1)S(1)} %get-tuple-element.22.refs_0_), channel_id=1, source_target_pairs={{0,14},{2,0},{4,2},{6,4},{8,6},{10,8},{12,10},{14,12},{1,15},{3,1}... | collective-permute-start | bytes 442376 | tf_op jit(solution)/shard_map/ppermute | solution.py:30
  19.9 2.7 %collective-permute-done.refs_1_ = bf16[64,1152]{1,0:T(8,128)(2,1)S(1)} collective-permute-done((bf16[64,1152]{1,0:T(8,128)(2,1)S(1)}, bf16[64,1152]{1,0:T(8,128)(2,1)S(1)}, u32[]{:S(2)}, u32[]{:S(2)}) %collective-permute-start) | collective-permute-done | bytes 147488 | tf_op jit(solution)/shard_map/ppermute | solution.py:30
  22.6 3.7 %collective-permute-start.1 = (bf16[64,1152]{1,0:T(8,128)(2,1)S(1)}, bf16[64,1152]{1,0:T(8,128)(2,1)S(1)}, u32[]{:S(2)}, u32[]{:S(2)}) collective-permute-start(bf16[64,1152]{1,0:T(8,128)(2,1)S(1)} %collective-permute-done.refs_1_), channel_id=1, source_target_pairs={{0,14},{2,0},{4,2},{6,4},{8,6},{10,8},{12,10},{14,12},{1,15},{3,1}... | collective-permute-start | bytes 442376 | tf_op jit(solution)/shard_map/ppermute | solution.py:30
  26.2 2.7 %collective-permute-done.1.refs_2_ = bf16[64,1152]{1,0:T(8,128)(2,1)S(1)} collective-permute-done((bf16[64,1152]{1,0:T(8,128)(2,1)S(1)}, bf16[64,1152]{1,0:T(8,128)(2,1)S(1)}, u32[]{:S(2)}, u32[]{:S(2)}) %collective-permute-start.1) | collective-permute-done | bytes 147488 | tf_op jit(solution)/shard_map/ppermute | solution.py:30
  28.9 3.7 %collective-permute-start.2 = (bf16[64,1152]{1,0:T(8,128)(2,1)S(1)}, bf16[64,1152]{1,0:T(8,128)(2,1)S(1)}, u32[]{:S(2)}, u32[]{:S(2)}) collective-permute-start(bf16[64,1152]{1,0:T(8,128)(2,1)S(1)} %collective-permute-done.1.refs_2_), channel_id=1, source_target_pairs={{0,14},{2,0},{4,2},{6,4},{8,6},{10,8},{12,10},{14,12},{1,15},{3,1}... | collective-permute-start | bytes 442376 | tf_op jit(solution)/shard_map/ppermute | solution.py:30
  33.2 2.1 %collective-permute-done.2.refs_3_ = bf16[64,1152]{1,0:T(8,128)(2,1)S(1)} collective-permute-done((bf16[64,1152]{1,0:T(8,128)(2,1)S(1)}, bf16[64,1152]{1,0:T(8,128)(2,1)S(1)}, u32[]{:S(2)}, u32[]{:S(2)}) %collective-permute-start.2) | collective-permute-done | bytes 147488 | tf_op jit(solution)/shard_map/ppermute | solution.py:30
  35.3 3.7 %collective-permute-start.3 = (bf16[64,1152]{1,0:T(8,128)(2,1)S(1)}, bf16[64,1152]{1,0:T(8,128)(2,1)S(1)}, u32[]{:S(2)}, u32[]{:S(2)}) collective-permute-start(bf16[64,1152]{1,0:T(8,128)(2,1)S(1)} %collective-permute-done.2.refs_3_), channel_id=1, source_target_pairs={{0,14},{2,0},{4,2},{6,4},{8,6},{10,8},{12,10},{14,12},{1,15},{3,1}... | collective-permute-start | bytes 442376 | tf_op jit(solution)/shard_map/ppermute | solution.py:30
  40.6 1.0 collective-permute-done.3.refs_4_
  43.4 4.9 %logits.1 = (f32[1024,1024]{1,0:T(8,128)S(1)}, bf16[1024,1152]{1,0:T(8,128)(2,1)S(1)}, f32[16,128]{1,0:T(8,128)S(1)}, f32[1,1024]{1,0:T(1,128)S(1)}) custom-call(bf16[64,1152]{1,0:T(8,128)(2,1)} %copy-done, bf16[64,1152]{1,0:T(8,128)(2,1)} %copy-done.3, bf16[64,1152]{1,0:T(8,128)(2,1)} %copy-done.5, bf16[64,1152]{1,0:T(8,128)(2,1)} %copy-done.7, ...), custom_call_target="tpu_custom_call" | custom-call | tf_op jit(solution)/shard_map/logits/pallas_call | solution.py:210
  49.5 4.4 %collective-permute-start.19 = (f32[1,1024]{1,0:T(1,128)S(1)}, f32[1,1024]{1,0:T(1,128)S(1)}, u32[]{:S(2)}, u32[]{:S(2)}) collective-permute-start(f32[1,1024]{1,0:T(1,128)S(1)} %get-tuple-element.26), channel_id=1, source_target_pairs={{0,16},{16,0},{32,48},{48,32},{1,17},{17,1},{33,49},{49,33},{2,18}... | collective-permute-start | bytes 12296 | tf_op jit(solution)/shard_map/ppermute | solution.py:34
  53.9 3.3 %collective-permute-start.17 = (f32[16,128]{1,0:T(8,128)S(1)}, f32[16,128]{1,0:T(8,128)S(1)}, u32[]{:S(2)}, u32[]{:S(2)}) collective-permute-start(f32[16,128]{1,0:T(8,128)S(1)} %add.25), channel_id=1, source_target_pairs={{0,4},{2,6},{4,0},{6,2},{8,12},{10,14},{12,8},{14,10},{1,5},{3,7},... | collective-permute-start | bytes 24584 | tf_op jit(solution)/shard_map/ppermute | solution.py:34
  57.6 4.8 %collective-permute-done.20 = f32[1,1024]{1,0:T(1,128)S(1)} collective-permute-done((f32[1,1024]{1,0:T(1,128)S(1)}, f32[1,1024]{1,0:T(1,128)S(1)}, u32[]{:S(2)}, u32[]{:S(2)}) %collective-permute-start.20) | collective-permute-done | bytes 4128 | tf_op jit(solution)/shard_map/ppermute | solution.py:34
  63.1 4.5 %collective-permute-start.18 = (f32[16,128]{1,0:T(8,128)S(1)}, f32[16,128]{1,0:T(8,128)S(1)}, u32[]{:S(2)}, u32[]{:S(2)}) collective-permute-start(f32[16,128]{1,0:T(8,128)S(1)} %add.26), channel_id=1, source_target_pairs={{0,8},{2,10},{4,12},{6,14},{8,0},{10,2},{12,4},{14,6},{1,9},{3,11}... | collective-permute-start | bytes 24584 | tf_op jit(solution)/shard_map/ppermute | solution.py:34
  67.6 2.5 %collective-permute-start.22 = (f32[1,1024]{1,0:T(1,128)S(1)}, f32[1,1024]{1,0:T(1,128)S(1)}, u32[]{:S(2)}, u32[]{:S(2)}) collective-permute-start(f32[1,1024]{1,0:T(1,128)S(1)} %add.30), channel_id=1, source_target_pairs={{0,128},{64,192},{128,0},{192,64},{1,129},{65,193},{129,1},{193,65... | collective-permute-start | bytes 12296 | tf_op jit(solution)/shard_map/ppermute | solution.py:34
  70.2 2.7 %collective-permute-done.22 = f32[1,1024]{1,0:T(1,128)S(1)} collective-permute-done((f32[1,1024]{1,0:T(1,128)S(1)}, f32[1,1024]{1,0:T(1,128)S(1)}, u32[]{:S(2)}, u32[]{:S(2)}) %collective-permute-start.22) | collective-permute-done | bytes 4128 | tf_op jit(solution)/shard_map/ppermute | solution.py:34
  72.9 5.8 %grads.1 = (bf16[16,528,128]{2,1,0:T(8,128)(2,1)}, bf16[8,528,128]{2,1,0:T(8,128)(2,1)S(1)}, bf16[8,528,128]{2,1,0:T(8,128)(2,1)S(1)}) custom-call(f32[1024,1024]{1,0:T(8,128)S(1)} %get-tuple-element.24.exp_ref, f32[16,128]{1,0:T(8,128)S(1)} %add.27.row_ref, f32[1,1024]{1,0:T(1,128)S(1)} %add.31.col_ref, bf16[1024,1152]{1,0:T(8,128)(2,1)S(1)} %get-tuple-element.27.query_ref, ...), custom_call_target="tpu_custom_call" | custom-call | tf_op jit(solution)/shard_map/grads/pallas_call | solution.py:309
  79.7 7.1 %all-to-all-start.1 = ((bf16[16,528,128]{2,1,0:T(8,128)(2,1)}), bf16[16,528,128]{2,1,0:T(8,128)(2,1)}, u32[]{:S(2)}, u32[]{:S(2)}) async-start(bf16[16,528,128]{2,1,0:T(8,128)(2,1)} %get-tuple-element.37), calls=%async_computation.1 | async-start | bytes 4325376 | tf_op jit(solution)/shard_map/all_to_all | solution.py:484
  86.9 2.7 %collective-permute-done.23.refs_1_.refs_4_.other_ref = bf16[8,528,128]{2,1,0:T(8,128)(2,1)S(1)} collective-permute-done((bf16[8,528,128]{2,1,0:T(8,128)(2,1)S(1)}, bf16[8,528,128]{2,1,0:T(8,128)(2,1)S(1)}, u32[]{:S(2)}, u32[]{:S(2)}) %collective-permute-start.23) | collective-permute-done | bytes 1081376 | tf_op jit(solution)/shard_map/ppermute | solution.py:34
  89.7 1.6 %collective-permute-start.24 = (bf16[528,128]{1,0:T(8,128)(2,1)S(1)}, bf16[528,128]{1,0:T(8,128)(2,1)S(1)}, u32[]{:S(2)}, u32[]{:S(2)}) collective-permute-start(bf16[528,128]{1,0:T(8,128)(2,1)S(1)} %ring.4), channel_id=1, source_target_pairs={{0,14},{2,0},{4,2},{6,4},{8,6},{10,8},{12,10},{14,12},{1,15},{3,1}... | collective-permute-start | bytes 405512 | tf_op jit(solution)/shard_map/ppermute | solution.py:30
  91.3 4.1 %collective-permute-done.24.refs_2_ = bf16[528,128]{1,0:T(8,128)(2,1)S(1)} collective-permute-done((bf16[528,128]{1,0:T(8,128)(2,1)S(1)}, bf16[528,128]{1,0:T(8,128)(2,1)S(1)}, u32[]{:S(2)}, u32[]{:S(2)}) %collective-permute-start.24) | collective-permute-done | bytes 135200 | tf_op jit(solution)/shard_map/ppermute | solution.py:30
  95.5 2.8 %collective-permute-start.25 = (bf16[528,128]{1,0:T(8,128)(2,1)S(1)}, bf16[528,128]{1,0:T(8,128)(2,1)S(1)}, u32[]{:S(2)}, u32[]{:S(2)}) collective-permute-start(bf16[528,128]{1,0:T(8,128)(2,1)S(1)} %get-tuple-element.30), channel_id=1, source_target_pairs={{0,14},{2,0},{4,2},{6,4},{8,6},{10,8},{12,10},{14,12},{1,15},{3,1}... | collective-permute-start | bytes 405512 | tf_op jit(solution)/shard_map/ppermute | solution.py:30
  98.3 2.6 %collective-permute-done.25.refs_2_ = bf16[528,128]{1,0:T(8,128)(2,1)S(1)} collective-permute-done((bf16[528,128]{1,0:T(8,128)(2,1)S(1)}, bf16[528,128]{1,0:T(8,128)(2,1)S(1)}, u32[]{:S(2)}, u32[]{:S(2)}) %collective-permute-start.25) | collective-permute-done | bytes 135200 | tf_op jit(solution)/shard_map/ppermute | solution.py:30
  100.9 3.7 %collective-permute-done.26.refs_5_ = bf16[528,128]{1,0:T(8,128)(2,1)S(1)} collective-permute-done((bf16[528,128]{1,0:T(8,128)(2,1)S(1)}, bf16[528,128]{1,0:T(8,128)(2,1)S(1)}, u32[]{:S(2)}, u32[]{:S(2)}) %collective-permute-start.26) | collective-permute-done | bytes 135200 | tf_op jit(solution)/shard_map/ppermute | solution.py:30
  104.8 2.0 %collective-permute-start.28 = (bf16[528,128]{1,0:T(8,128)(2,1)S(1)}, bf16[528,128]{1,0:T(8,128)(2,1)S(1)}, u32[]{:S(2)}, u32[]{:S(2)}) collective-permute-start(bf16[528,128]{1,0:T(8,128)(2,1)S(1)} %get-tuple-element.33), channel_id=1, source_target_pairs={{0,2},{2,4},{4,6},{6,8},{8,10},{10,12},{12,14},{14,0},{1,3},{3,5},... | collective-permute-start | bytes 405512 | tf_op jit(solution)/shard_map/ppermute | solution.py:30
  106.8 3.0 %collective-permute-done.27.refs_2_ = bf16[528,128]{1,0:T(8,128)(2,1)S(1)} collective-permute-done((bf16[528,128]{1,0:T(8,128)(2,1)S(1)}, bf16[528,128]{1,0:T(8,128)(2,1)S(1)}, u32[]{:S(2)}, u32[]{:S(2)}) %collective-permute-start.27) | collective-permute-done | bytes 135200 | tf_op jit(solution)/shard_map/ppermute | solution.py:30
  109.8 1.3 %collective-permute-done.28.refs_5_ = bf16[528,128]{1,0:T(8,128)(2,1)S(1)} collective-permute-done((bf16[528,128]{1,0:T(8,128)(2,1)S(1)}, bf16[528,128]{1,0:T(8,128)(2,1)S(1)}, u32[]{:S(2)}, u32[]{:S(2)}) %collective-permute-start.28) | collective-permute-done | bytes 135200 | tf_op jit(solution)/shard_map/ppermute | solution.py:30
  111.3 2.0 %collective-permute-start.30 = (bf16[528,128]{1,0:T(8,128)(2,1)S(1)}, bf16[528,128]{1,0:T(8,128)(2,1)S(1)}, u32[]{:S(2)}, u32[]{:S(2)}) collective-permute-start(bf16[528,128]{1,0:T(8,128)(2,1)S(1)} %get-tuple-element.35), channel_id=1, source_target_pairs={{0,2},{2,4},{4,6},{6,8},{8,10},{10,12},{12,14},{14,0},{1,3},{3,5},... | collective-permute-start | bytes 405512 | tf_op jit(solution)/shard_map/ppermute | solution.py:30
  113.3 3.0 %collective-permute-done.29.down_ref = bf16[528,128]{1,0:T(8,128)(2,1)S(1)} collective-permute-done((bf16[528,128]{1,0:T(8,128)(2,1)S(1)}, bf16[528,128]{1,0:T(8,128)(2,1)S(1)}, u32[]{:S(2)}, u32[]{:S(2)}) %collective-permute-start.29) | collective-permute-done | bytes 135200 | tf_op jit(solution)/shard_map/ppermute | solution.py:30
  116.3 1.3 %collective-permute-done.30.up_ref = bf16[528,128]{1,0:T(8,128)(2,1)S(1)} collective-permute-done((bf16[528,128]{1,0:T(8,128)(2,1)S(1)}, bf16[528,128]{1,0:T(8,128)(2,1)S(1)}, u32[]{:S(2)}, u32[]{:S(2)}) %collective-permute-start.30) | collective-permute-done | bytes 135200 | tf_op jit(solution)/shard_map/ppermute | solution.py:30
  117.6 7.4 %final.1 = (f32[1,1]{1,0:T(1,128)}, f32[64,4096]{1,0:T(8,128)}, f32[64,4096]{1,0:T(8,128)}) custom-call(bf16[8,528,128]{2,1,0:T(8,128)(2,1)S(1)} %get-tuple-element.28.refs_0_.refs_3_.own_ref, bf16[8,528,128]{2,1,0:T(8,128)(2,1)S(1)} %collective-permute-done.23.refs_1_.refs_4_.other_ref, bf16[528,128]{1,0:T(8,128)(2,1)S(1)} %collective-permute-done.29.down_ref, ...), custom_call_target="tpu_custom_call" | custom-call | tf_op jit(solution)/shard_map/final/pallas_call | solution.py:442
  (84 shorter events, 8.0 us)
Async XLA Ops:
  6.5 36.8 %all-to-all-start = ((bf16[16,64,1024]{2,1,0:T(8,128)(2,1)}), bf16[16,64,1024]{2,1,0:T(8,128)(2,1)S(1)}, u32[]{:S(2)}, u32[]{:S(2)}) async-start(bf16[16,64,1024]{2,1,0:T(8,128)(2,1)} %bitcast.6), calls=%async_computation | async-start | bytes 4194304 | tf_op jit(solution)/shard_map/all_to_all | solution.py:477
  14.0 8.5 %collective-permute-start = (bf16[64,1152]{1,0:T(8,128)(2,1)S(1)}, bf16[64,1152]{1,0:T(8,128)(2,1)S(1)}, u32[]{:S(2)}, u32[]{:S(2)}) collective-permute-start(bf16[64,1152]{1,0:T(8,128)(2,1)S(1)} %get-tuple-element.22.refs_0_), channel_id=1, source_target_pairs={{0,14},{2,0},{4,2},{6,4},{8,6},{10,8},{12,10},{14,12},{1,15},{3,1}... | collective-permute-start | bytes 442376 | tf_op jit(solution)/shard_map/ppermute | solution.py:30
  19.9 6.4 %collective-permute-start.4 = (bf16[64,1152]{1,0:T(8,128)(2,1)S(1)}, bf16[64,1152]{1,0:T(8,128)(2,1)S(1)}, u32[]{:S(2)}, u32[]{:S(2)}) collective-permute-start(bf16[64,1152]{1,0:T(8,128)(2,1)S(1)} %get-tuple-element.22.refs_0_), channel_id=1, source_target_pairs={{0,2},{2,4},{4,6},{6,8},{8,10},{10,12},{12,14},{14,0},{1,3},{3,5},... | collective-permute-start | bytes 442376 | tf_op jit(solution)/shard_map/ppermute | solution.py:30
  22.6 6.4 %collective-permute-start.1 = (bf16[64,1152]{1,0:T(8,128)(2,1)S(1)}, bf16[64,1152]{1,0:T(8,128)(2,1)S(1)}, u32[]{:S(2)}, u32[]{:S(2)}) collective-permute-start(bf16[64,1152]{1,0:T(8,128)(2,1)S(1)} %collective-permute-done.refs_1_), channel_id=1, source_target_pairs={{0,14},{2,0},{4,2},{6,4},{8,6},{10,8},{12,10},{14,12},{1,15},{3,1}... | collective-permute-start | bytes 442376 | tf_op jit(solution)/shard_map/ppermute | solution.py:30
  26.2 6.9 %collective-permute-start.5 = (bf16[64,1152]{1,0:T(8,128)(2,1)S(1)}, bf16[64,1152]{1,0:T(8,128)(2,1)S(1)}, u32[]{:S(2)}, u32[]{:S(2)}) collective-permute-start(bf16[64,1152]{1,0:T(8,128)(2,1)S(1)} %collective-permute-done.4.refs_7_), channel_id=1, source_target_pairs={{0,2},{2,4},{4,6},{6,8},{8,10},{10,12},{12,14},{14,0},{1,3},{3,5},... | collective-permute-start | bytes 442376 | tf_op jit(solution)/shard_map/ppermute | solution.py:30
  28.9 6.4 %collective-permute-start.2 = (bf16[64,1152]{1,0:T(8,128)(2,1)S(1)}, bf16[64,1152]{1,0:T(8,128)(2,1)S(1)}, u32[]{:S(2)}, u32[]{:S(2)}) collective-permute-start(bf16[64,1152]{1,0:T(8,128)(2,1)S(1)} %collective-permute-done.1.refs_2_), channel_id=1, source_target_pairs={{0,14},{2,0},{4,2},{6,4},{8,6},{10,8},{12,10},{14,12},{1,15},{3,1}... | collective-permute-start | bytes 442376 | tf_op jit(solution)/shard_map/ppermute | solution.py:30
  32.6 6.4 %collective-permute-start.7 = (bf16[64,1152]{1,0:T(8,128)(2,1)S(1)}, bf16[64,1152]{1,0:T(8,128)(2,1)S(1)}, u32[]{:S(2)}, u32[]{:S(2)}) collective-permute-start(bf16[64,1152]{1,0:T(8,128)(2,1)S(1)} %get-tuple-element.22.refs_0_), channel_id=1, source_target_pairs={{0,1},{1,0},{2,3},{3,2},{4,5},{5,4},{6,7},{7,6},{8,9},{9,8},{10,11... | collective-permute-start | bytes 442376 | tf_op jit(solution)/shard_map/ppermute | solution.py:34
  32.6 6.4 %collective-permute-start.14 = (bf16[64,1152]{1,0:T(8,128)(2,1)S(1)}, bf16[64,1152]{1,0:T(8,128)(2,1)S(1)}, u32[]{:S(2)}, u32[]{:S(2)}) collective-permute-start(bf16[64,1152]{1,0:T(8,128)(2,1)S(1)} %collective-permute-done.4.refs_7_), channel_id=1, source_target_pairs={{0,1},{1,0},{2,3},{3,2},{4,5},{5,4},{6,7},{7,6},{8,9},{9,8},{10,11... | collective-permute-start | bytes 442376 | tf_op jit(solution)/shard_map/ppermute | solution.py:34
  33.1 6.4 %collective-permute-start.8 = (bf16[64,1152]{1,0:T(8,128)(2,1)S(1)}, bf16[64,1152]{1,0:T(8,128)(2,1)S(1)}, u32[]{:S(2)}, u32[]{:S(2)}) collective-permute-start(bf16[64,1152]{1,0:T(8,128)(2,1)S(1)} %collective-permute-done.refs_1_), channel_id=1, source_target_pairs={{0,1},{1,0},{2,3},{3,2},{4,5},{5,4},{6,7},{7,6},{8,9},{9,8},{10,11... | collective-permute-start | bytes 442376 | tf_op jit(solution)/shard_map/ppermute | solution.py:34
  33.1 7.5 %collective-permute-start.6 = (bf16[64,1152]{1,0:T(8,128)(2,1)S(1)}, bf16[64,1152]{1,0:T(8,128)(2,1)S(1)}, u32[]{:S(2)}, u32[]{:S(2)}) collective-permute-start(bf16[64,1152]{1,0:T(8,128)(2,1)S(1)} %collective-permute-done.5.refs_6_), channel_id=1, source_target_pairs={{0,2},{2,4},{4,6},{6,8},{8,10},{10,12},{12,14},{14,0},{1,3},{3,5},... | collective-permute-start | bytes 442376 | tf_op jit(solution)/shard_map/ppermute | solution.py:30
  35.3 6.4 %collective-permute-start.3 = (bf16[64,1152]{1,0:T(8,128)(2,1)S(1)}, bf16[64,1152]{1,0:T(8,128)(2,1)S(1)}, u32[]{:S(2)}, u32[]{:S(2)}) collective-permute-start(bf16[64,1152]{1,0:T(8,128)(2,1)S(1)} %collective-permute-done.2.refs_3_), channel_id=1, source_target_pairs={{0,14},{2,0},{4,2},{6,4},{8,6},{10,8},{12,10},{14,12},{1,15},{3,1}... | collective-permute-start | bytes 442376 | tf_op jit(solution)/shard_map/ppermute | solution.py:30
  39.0 2.7 %collective-permute-start.13 = (bf16[64,1152]{1,0:T(8,128)(2,1)S(1)}, bf16[64,1152]{1,0:T(8,128)(2,1)S(1)}, u32[]{:S(2)}, u32[]{:S(2)}) collective-permute-start(bf16[64,1152]{1,0:T(8,128)(2,1)S(1)} %collective-permute-done.5.refs_6_), channel_id=1, source_target_pairs={{0,1},{1,0},{2,3},{3,2},{4,5},{5,4},{6,7},{7,6},{8,9},{9,8},{10,11... | collective-permute-start | bytes 442376 | tf_op jit(solution)/shard_map/ppermute | solution.py:34
  39.0 2.7 %collective-permute-start.9 = (bf16[64,1152]{1,0:T(8,128)(2,1)S(1)}, bf16[64,1152]{1,0:T(8,128)(2,1)S(1)}, u32[]{:S(2)}, u32[]{:S(2)}) collective-permute-start(bf16[64,1152]{1,0:T(8,128)(2,1)S(1)} %collective-permute-done.1.refs_2_), channel_id=1, source_target_pairs={{0,1},{1,0},{2,3},{3,2},{4,5},{5,4},{6,7},{7,6},{8,9},{9,8},{10,11... | collective-permute-start | bytes 442376 | tf_op jit(solution)/shard_map/ppermute | solution.py:34
  39.5 2.5 %collective-permute-start.10 = (bf16[64,1152]{1,0:T(8,128)(2,1)S(1)}, bf16[64,1152]{1,0:T(8,128)(2,1)S(1)}, u32[]{:S(2)}, u32[]{:S(2)}) collective-permute-start(bf16[64,1152]{1,0:T(8,128)(2,1)S(1)} %collective-permute-done.2.refs_3_), channel_id=1, source_target_pairs={{0,1},{1,0},{2,3},{3,2},{4,5},{5,4},{6,7},{7,6},{8,9},{9,8},{10,11... | collective-permute-start | bytes 442376 | tf_op jit(solution)/shard_map/ppermute | solution.py:34
  40.6 1.4 %collective-permute-start.12 = (bf16[64,1152]{1,0:T(8,128)(2,1)S(1)}, bf16[64,1152]{1,0:T(8,128)(2,1)S(1)}, u32[]{:S(2)}, u32[]{:S(2)}) collective-permute-start(bf16[64,1152]{1,0:T(8,128)(2,1)S(1)} %collective-permute-done.6.refs_5_), channel_id=1, source_target_pairs={{0,1},{1,0},{2,3},{3,2},{4,5},{5,4},{6,7},{7,6},{8,9},{9,8},{10,11... | collective-permute-start | bytes 442376 | tf_op jit(solution)/shard_map/ppermute | solution.py:34
  41.6 1.7 %collective-permute-start.11 = (bf16[64,1152]{1,0:T(8,128)(2,1)S(1)}, bf16[64,1152]{1,0:T(8,128)(2,1)}, u32[]{:S(2)}, u32[]{:S(2)}) collective-permute-start(bf16[64,1152]{1,0:T(8,128)(2,1)S(1)} %collective-permute-done.3.refs_4_), channel_id=1, source_target_pairs={{0,1},{1,0},{2,3},{3,2},{4,5},{5,4},{6,7},{7,6},{8,9},{9,8},{10,11... | collective-permute-start | bytes 442376 | tf_op jit(solution)/shard_map/ppermute | solution.py:34
  49.5 4.4 %collective-permute-start.16 = (f32[16,128]{1,0:T(8,128)S(1)}, f32[16,128]{1,0:T(8,128)S(1)}, u32[]{:S(2)}, u32[]{:S(2)}) collective-permute-start(f32[16,128]{1,0:T(8,128)S(1)} %add.24), channel_id=1, source_target_pairs={{0,2},{2,0},{4,6},{6,4},{8,10},{10,8},{12,14},{14,12},{1,3},{3,1},... | collective-permute-start | bytes 24584 | tf_op jit(solution)/shard_map/ppermute | solution.py:34
  49.5 7.7 %collective-permute-start.19 = (f32[1,1024]{1,0:T(1,128)S(1)}, f32[1,1024]{1,0:T(1,128)S(1)}, u32[]{:S(2)}, u32[]{:S(2)}) collective-permute-start(f32[1,1024]{1,0:T(1,128)S(1)} %get-tuple-element.26), channel_id=1, source_target_pairs={{0,16},{16,0},{32,48},{48,32},{1,17},{17,1},{33,49},{49,33},{2,18}... | collective-permute-start | bytes 12296 | tf_op jit(solution)/shard_map/ppermute | solution.py:34
  53.9 9.1 %collective-permute-start.17 = (f32[16,128]{1,0:T(8,128)S(1)}, f32[16,128]{1,0:T(8,128)S(1)}, u32[]{:S(2)}, u32[]{:S(2)}) collective-permute-start(f32[16,128]{1,0:T(8,128)S(1)} %add.25), channel_id=1, source_target_pairs={{0,4},{2,6},{4,0},{6,2},{8,12},{10,14},{12,8},{14,10},{1,5},{3,7},... | collective-permute-start | bytes 24584 | tf_op jit(solution)/shard_map/ppermute | solution.py:34
  57.2 5.2 %collective-permute-start.20 = (f32[1,1024]{1,0:T(1,128)S(1)}, f32[1,1024]{1,0:T(1,128)S(1)}, u32[]{:S(2)}, u32[]{:S(2)}) collective-permute-start(f32[1,1024]{1,0:T(1,128)S(1)} %add.28), channel_id=1, source_target_pairs={{0,32},{16,48},{32,0},{48,16},{1,33},{17,49},{33,1},{49,17},{2,34}... | collective-permute-start | bytes 12296 | tf_op jit(solution)/shard_map/ppermute | solution.py:34
  62.4 5.2 %collective-permute-start.21 = (f32[1,1024]{1,0:T(1,128)S(1)}, f32[1,1024]{1,0:T(1,128)S(1)}, u32[]{:S(2)}, u32[]{:S(2)}) collective-permute-start(f32[1,1024]{1,0:T(1,128)S(1)} %add.29), channel_id=1, source_target_pairs={{0,64},{64,0},{128,192},{192,128},{1,65},{65,1},{129,193},{193,129... | collective-permute-start | bytes 12296 | tf_op jit(solution)/shard_map/ppermute | solution.py:34
  63.1 9.8 %collective-permute-start.18 = (f32[16,128]{1,0:T(8,128)S(1)}, f32[16,128]{1,0:T(8,128)S(1)}, u32[]{:S(2)}, u32[]{:S(2)}) collective-permute-start(f32[16,128]{1,0:T(8,128)S(1)} %add.26), channel_id=1, source_target_pairs={{0,8},{2,10},{4,12},{6,14},{8,0},{10,2},{12,4},{14,6},{1,9},{3,11}... | collective-permute-start | bytes 24584 | tf_op jit(solution)/shard_map/ppermute | solution.py:34
  67.6 5.2 %collective-permute-start.22 = (f32[1,1024]{1,0:T(1,128)S(1)}, f32[1,1024]{1,0:T(1,128)S(1)}, u32[]{:S(2)}, u32[]{:S(2)}) collective-permute-start(f32[1,1024]{1,0:T(1,128)S(1)} %add.30), channel_id=1, source_target_pairs={{0,128},{64,192},{128,0},{192,64},{1,129},{65,193},{129,1},{193,65... | collective-permute-start | bytes 12296 | tf_op jit(solution)/shard_map/ppermute | solution.py:34
  79.7 37.9 %all-to-all-start.1 = ((bf16[16,528,128]{2,1,0:T(8,128)(2,1)}), bf16[16,528,128]{2,1,0:T(8,128)(2,1)}, u32[]{:S(2)}, u32[]{:S(2)}) async-start(bf16[16,528,128]{2,1,0:T(8,128)(2,1)} %get-tuple-element.37), calls=%async_computation.1 | async-start | bytes 4325376 | tf_op jit(solution)/shard_map/all_to_all | solution.py:484
  86.8 2.8 %collective-permute-start.23 = (bf16[8,528,128]{2,1,0:T(8,128)(2,1)S(1)}, bf16[8,528,128]{2,1,0:T(8,128)(2,1)S(1)}, u32[]{:S(2)}, u32[]{:S(2)}) collective-permute-start(bf16[8,528,128]{2,1,0:T(8,128)(2,1)S(1)} %copy-done.2), channel_id=1, source_target_pairs={{0,1},{1,0},{2,3},{3,2},{4,5},{5,4},{6,7},{7,6},{8,9},{9,8},{10,11... | collective-permute-start | bytes 3244040 | tf_op jit(solution)/shard_map/ppermute | solution.py:34
  89.7 5.7 %collective-permute-start.24 = (bf16[528,128]{1,0:T(8,128)(2,1)S(1)}, bf16[528,128]{1,0:T(8,128)(2,1)S(1)}, u32[]{:S(2)}, u32[]{:S(2)}) collective-permute-start(bf16[528,128]{1,0:T(8,128)(2,1)S(1)} %ring.4), channel_id=1, source_target_pairs={{0,14},{2,0},{4,2},{6,4},{8,6},{10,8},{12,10},{14,12},{1,15},{3,1}... | collective-permute-start | bytes 405512 | tf_op jit(solution)/shard_map/ppermute | solution.py:30
  95.5 5.4 %collective-permute-start.25 = (bf16[528,128]{1,0:T(8,128)(2,1)S(1)}, bf16[528,128]{1,0:T(8,128)(2,1)S(1)}, u32[]{:S(2)}, u32[]{:S(2)}) collective-permute-start(bf16[528,128]{1,0:T(8,128)(2,1)S(1)} %get-tuple-element.30), channel_id=1, source_target_pairs={{0,14},{2,0},{4,2},{6,4},{8,6},{10,8},{12,10},{14,12},{1,15},{3,1}... | collective-permute-start | bytes 405512 | tf_op jit(solution)/shard_map/ppermute | solution.py:30
  98.3 6.2 %collective-permute-start.26 = (bf16[528,128]{1,0:T(8,128)(2,1)S(1)}, bf16[528,128]{1,0:T(8,128)(2,1)S(1)}, u32[]{:S(2)}, u32[]{:S(2)}) collective-permute-start(bf16[528,128]{1,0:T(8,128)(2,1)S(1)} %get-tuple-element.31), channel_id=1, source_target_pairs={{0,2},{2,4},{4,6},{6,8},{8,10},{10,12},{12,14},{14,0},{1,3},{3,5},... | collective-permute-start | bytes 405512 | tf_op jit(solution)/shard_map/ppermute | solution.py:30
  104.7 5.1 %collective-permute-start.27 = (bf16[528,128]{1,0:T(8,128)(2,1)S(1)}, bf16[528,128]{1,0:T(8,128)(2,1)S(1)}, u32[]{:S(2)}, u32[]{:S(2)}) collective-permute-start(bf16[528,128]{1,0:T(8,128)(2,1)S(1)} %get-tuple-element.32), channel_id=1, source_target_pairs={{0,14},{2,0},{4,2},{6,4},{8,6},{10,8},{12,10},{14,12},{1,15},{3,1}... | collective-permute-start | bytes 405512 | tf_op jit(solution)/shard_map/ppermute | solution.py:30
  104.8 6.3 %collective-permute-start.28 = (bf16[528,128]{1,0:T(8,128)(2,1)S(1)}, bf16[528,128]{1,0:T(8,128)(2,1)S(1)}, u32[]{:S(2)}, u32[]{:S(2)}) collective-permute-start(bf16[528,128]{1,0:T(8,128)(2,1)S(1)} %get-tuple-element.33), channel_id=1, source_target_pairs={{0,2},{2,4},{4,6},{6,8},{8,10},{10,12},{12,14},{14,0},{1,3},{3,5},... | collective-permute-start | bytes 405512 | tf_op jit(solution)/shard_map/ppermute | solution.py:30
  111.2 5.1 %collective-permute-start.29 = (bf16[528,128]{1,0:T(8,128)(2,1)S(1)}, bf16[528,128]{1,0:T(8,128)(2,1)S(1)}, u32[]{:S(2)}, u32[]{:S(2)}) collective-permute-start(bf16[528,128]{1,0:T(8,128)(2,1)S(1)} %get-tuple-element.34), channel_id=1, source_target_pairs={{0,14},{2,0},{4,2},{6,4},{8,6},{10,8},{12,10},{14,12},{1,15},{3,1}... | collective-permute-start | bytes 405512 | tf_op jit(solution)/shard_map/ppermute | solution.py:30
  111.3 6.3 %collective-permute-start.30 = (bf16[528,128]{1,0:T(8,128)(2,1)S(1)}, bf16[528,128]{1,0:T(8,128)(2,1)S(1)}, u32[]{:S(2)}, u32[]{:S(2)}) collective-permute-start(bf16[528,128]{1,0:T(8,128)(2,1)S(1)} %get-tuple-element.35), channel_id=1, source_target_pairs={{0,2},{2,4},{4,6},{6,8},{8,10},{10,12},{12,14},{14,0},{1,3},{3,5},... | collective-permute-start | bytes 405512 | tf_op jit(solution)/shard_map/ppermute | solution.py:30
  (18 other events, 134.2 us)

commit v4 on v3

--- a/solution.py
+++ b/solution.py
@@ -32,10 +32,6 @@
 
 def swap(value, axis, size, bit):
     return lax.ppermute(value, axis, [(i, i ^ bit) for i in range(size)])
-
-
-pc_steps = (("c", NC, 1), ("z", NZ, 1), ("z", NZ, 2), ("z", NZ, 4))
-qr_steps = (("x", NX, 1), ("x", NX, 2), ("y", NY, 1), ("y", NY, 2))
 
 
 def sds(shape, dtype):
@@ -253,14 +249,13 @@
     other_ref,
     grad,
     row_scale,
+    query_parts,
     parts,
     sems,
 ):
     columns, width = passage_ref.shape
     rows = query_ref.shape[0]
     own = rows // (NZ * NC)
-    steps = sems.shape[0]
-    chunk = columns // steps
     half = 0.5 * grad_scale
     lane = lax.broadcasted_iota(jnp.int32, (1, LANES), 1)
     row_total = logit_scale * rows - 2.0 * row_ref[0:1, own : own + 1]
@@ -273,29 +268,39 @@
     col_total = jnp.sum(jnp.log(col_ref[...]), axis=1, keepdims=True) + logit_scale * columns
     row_extra = in_thirds(jnp.broadcast_to(row_total, (EXTRA, 1)), (EXTRA, LANES))
     col_extra = in_thirds(jnp.broadcast_to(col_total, (EXTRA, 1)), (EXTRA, LANES))
-    positive = positive_column(query_ref, pl.ds(0, rows), width, columns)
     stores = []
+
+    def send(blocks, first, count, out_ref, at):
+        source, target = blocks.at[pl.ds(first, count)], out_ref.at[pl.ds(at, count)]
+        stores.append(pltpu.make_async_copy(source, target, sems.at[len(stores)]))
+        stores[-1].start()
+
+    each = rows // 2
+    for k in (1, 0):
+        part = pl.ds(k * each, each)
+        positive = positive_column(query_ref, part, width, columns)
+        scale = jnp.concatenate([row_scale[part, :]] * (columns // LANES), axis=1)
+        column = lax.broadcasted_iota(jnp.int32, (each, columns), 1)
+        hit = jnp.where(column == positive, grad_scale, 0.0)
+        tile = (exp_ref[part, :] * (scale + half / col_ref[...]) - hit).astype(bf16)
+        grad[part, :] = tile
+        term = jnp.dot(tile, passage_ref[...], preferred_element_type=f32)
+        term = (logit_scale * term).astype(bf16)
+        for n in range(NZ):
+            as_tiles(query_parts.at[k * NZ + n], term[n * own : (n + 1) * own, :], col_extra)
+        send(query_parts, k * NZ, NZ, other_ref if k else own_ref, 0)
+    steps = 4
+    chunk = columns // steps
+    count = chunk // own
     for k in range(steps):
         part = pl.ds(k * chunk, chunk)
-        scale = jnp.concatenate([row_scale[...]] * (chunk // LANES), axis=1)
-        scale = scale + half / col_ref[:, part]
-        column = lax.broadcasted_iota(jnp.int32, (rows, chunk), 1) + k * chunk
-        hit = jnp.where(column == positive, grad_scale, 0.0)
-        tile = (exp_ref[:, part] * scale - hit).astype(bf16)
-        grad[:, part] = tile
-        term = lax.dot_general(tile, query_ref[:, :width], TN, preferred_element_type=f32)
+        term = lax.dot_general(
+            grad[:, part], query_ref[:, :width], TN, preferred_element_type=f32
+        )
         term = (logit_scale * term).astype(bf16)
-        blocks = pl.ds(k * chunk // own, chunk // own)
-        for n in range(chunk // own):
-            as_tiles(parts.at[k * chunk // own + n], term[n * own : (n + 1) * own, :], row_extra)
-        stores.append(pltpu.make_async_copy(parts.at[blocks], part_ref.at[blocks], sems.at[k]))
-        stores[-1].start()
-    for k, out_ref in enumerate((own_ref, other_ref)):
-        part = pl.ds(k * NZ * own, NZ * own)
-        term = jnp.dot(grad[part, :], passage_ref[...], preferred_element_type=f32)
-        term = (logit_scale * term).astype(bf16)
-        for n in range(NZ):
-            as_tiles(out_ref.at[n], term[n * own : (n + 1) * own, :], col_extra)
+        for n in range(count):
+            as_tiles(parts.at[k * count + n], term[n * own : (n + 1) * own, :], row_extra)
+        send(parts, k * count, count, part_ref, k * count)
     for store in stores:
         store.wait()
 
@@ -305,21 +310,21 @@
     columns, width = passage_tile.shape
     own = rows // (NZ * NC)
     block = (own * width // LANES + EXTRA, LANES)
-    steps = 4
     return pl.pallas_call(
         grads_kernel,
         in_specs=[VMEM] * 5,
-        out_specs=[HBM, VMEM, VMEM],
+        out_specs=[HBM] * 3,
         out_shape=[
             pltpu.HBM((columns // own, *block), bf16),
-            sds((NZ, *block), bf16),
-            sds((NZ, *block), bf16),
+            pltpu.HBM((NZ, *block), bf16),
+            pltpu.HBM((NZ, *block), bf16),
         ],
         scratch_shapes=[
             pltpu.VMEM((rows, columns), bf16),
             pltpu.VMEM((rows, LANES), f32),
+            pltpu.VMEM((NZ * NC, *block), bf16),
             pltpu.VMEM((columns // own, *block), bf16),
-            pltpu.SemaphoreType.DMA((steps,)),
+            pltpu.SemaphoreType.DMA((6,)),
         ],
         compiler_params=params,
         name="grads",
@@ -368,6 +373,7 @@
     other_ref,
     down_ref,
     up_ref,
+    across_ref,
     proj_ref,
     state_ref,
     terms_ref,
@@ -410,7 +416,8 @@
         return jnp.sum(tiles[spread * rows : spread * rows + 1], axis=1, keepdims=True)
 
     query = own_ref[0].astype(f32) + other_ref[0].astype(f32)
-    query = query + down_ref[...].astype(f32) + up_ref[...].astype(f32)
+    for ref in (down_ref, up_ref, across_ref):
+        query = query + ref[...].astype(f32)
     loads[0].wait()
     total = back(0, query)
     passage = jnp.zeros(terms_ref.shape[1:], f32)
@@ -434,7 +441,7 @@
         store.wait()
 
 
-def final(count, own, other, down, up, proj, state, terms):
+def final(count, own, other, down, up, across, proj, state, terms):
     rows = state.shape[0] // 2
     depth, width = proj.shape
     steps, groups = 8, 4
@@ -442,7 +449,7 @@
     return pl.pallas_call(
         functools.partial(final_kernel, count),
         grid=(1,),
-        in_specs=[block] * 2 + [fixed(down.shape)] * 2 + [HBM] * 3,
+        in_specs=[block] * 2 + [fixed(down.shape)] * 3 + [HBM] * 3,
         out_specs=[fixed((1, 1)), HBM, HBM],
         out_shape=[sds((1, 1), f32)] + [pltpu.HBM((rows, depth), f32)] * 2,
         scratch_shapes=[
@@ -456,7 +463,7 @@
         ],
         compiler_params=params,
         name="final",
-    )(own, other, down, up, *map(in_hbm, (proj, state, terms)))
+    )(own, other, down, up, across, *map(in_hbm, (proj, state, terms)))
 
 
 def gather_queries(message):
@@ -477,22 +484,26 @@
     passage_tile = lax.all_to_all(copies, QR, 0, 0, tiled=True)
     pieces = gather_queries(message)
     shifted, query_tile, row_sum, column_sum = tile_logits(pieces, passage_tile)
-    for pc_step, qr_step in zip(pc_steps, qr_steps):
-        row_sum = row_sum + swap(row_sum, *pc_step)
-        column_sum = column_sum + swap(column_sum, *qr_step)
+    row_sum = row_sum + swap(row_sum, "c", NC, 1)
+    column_sum = column_sum + sum(shift(column_sum, "x", NX, k) for k in range(1, NX))
+    before, after = shift(row_sum, "z", NZ, 1), shift(row_sum, "z", NZ, -1)
+    column_sum = column_sum + sum(shift(column_sum, "y", NY, k) for k in range(1, NY))
+    pair = row_sum + before
+    three = pair + after
+    row_sum = three + shift(three, "z", NZ, -3) + shift(pair, "z", NZ, 2)
     partial, own, other = tile_grads(shifted, row_sum, column_sum, query_tile, passage_tile)
     terms = lax.all_to_all(partial, QR, 0, 0, tiled=True)
     other = swap(other, "c", NC, 1)
-    (down,) = ring_step(own, other, [(4, None)])
-    came = shift(down, "z", NZ, -1)
-    down, up = ring_step(own, other, [(5, came), (3, None)])
-    for k in (2, 1):
+    far = NZ // 2
+    down, up, across = ring_step(own, other, [(far + 1, None), (far - 1, None), (far, None)])
+    across = shift(across, "z", NZ, far)
+    for k in range(far - 2, 0, -1):
         came = shift(down, "z", NZ, -1), shift(up, "z", NZ, 1)
         down, up = ring_step(own, other, [(NZ - k, came[0]), (k, came[1])])
     down, up = shift(down, "z", NZ, -1), shift(up, "z", NZ, 1)
     count = 2.0 * column_sum.shape[1] * NZ * NC
     total, grad_query_pool, grad_passage_pool = final(
-        count, own, other, down, up, proj, state, terms
+        count, own, other, down, up, across, proj, state, terms
     )
     return (total.reshape(()), grad_query_pool, grad_passage_pool)
 

time: 125 us -> 120 us (0.960)
  waiting for transfers between devices: 39.8 us -> 29.8 us
  starting transfers between devices: 57.4 us -> 63.4 us
    ppermute x14 -> x24, starting transfers between devices: 25.5 us -> 46.9 us  [shift(): lax.ppermute(value, axis, [(i, (i + step) % size) for i in range(size)])]
    ppermute x17 -> x10, starting transfers between devices: 17.3 us -> 1.48 us  [swap(): return lax.ppermute(value, axis, [(i, i ^ bit) for i in range(size)])]
    ppermute x17 -> x10, waiting for transfers between devices: 11.4 us -> 3.24 us  [swap(): return lax.ppermute(value, axis, [(i, i ^ bit) for i in range(size)])]
    ppermute x14 -> x24, waiting for transfers between devices: 28.4 us -> 26.5 us  [shift(): lax.ppermute(value, axis, [(i, (i + step) % size) for i in range(size)])]
  transfers between devices with their start and end apart: 33 -> 36, of which waited for: 17 -> 15; matrix products, arithmetic and copies ran while one was open for 0% -> 0% of each run, Pallas kernels for 0% -> 0%
where the time goes in v4:
time: 120 us
  starting transfers between devices  63.4 us (53%)
  waiting for transfers between devices  29.8 us (25%)
  Pallas kernels  24.4 us (20%)
  local copies, waits for them, and re-layouts  1.37 us (1%)
    ppermute x24, starting transfers between devices, shift(): lax.ppermute(value, axis, [(i, (i + step) % size) for i in range(size)])  46.9 us
    ppermute x24, waiting for transfers between devices, shift(): lax.ppermute(value, axis, [(i, (i + step) % size) for i in range(size)])  26.5 us
    all_to_all x1, starting transfers between devices, body(): terms = lax.all_to_all(partial, QR, 0, 0, tiled=True)  7.58 us
    all_to_all x1, starting transfers between devices, body(): passage_tile = lax.all_to_all(copies, QR, 0, 0, tiled=True)  7.49 us
    pallas_call x1, Pallas kernels, final(): pl.pallas_call(functools.partial(final_kernel, count), grid=(1,), in_spec...  7.37 us
    pallas_call x1, Pallas kernels, embed(): pl.pallas_call(embed_kernel, in_specs=[HBM] * 4, out_specs=[VMEM, HBM, HB...  5.92 us
    pallas_call x1, Pallas kernels, tile_grads(): pl.pallas_call(grads_kernel, in_specs=[VMEM] * 5, out_specs=[HBM] * 3, ou...  5.78 us
    pallas_call x1, Pallas kernels, tile_logits(): pl.pallas_call(logits_kernel, in_specs=[HBM] * len(pieces) + [VMEM], out_...  4.89 us
  transfers between devices with their start and end apart: 36, of which 15 were waited for; matrix products, arithmetic and copies ran while one was open for 0% of the time, Pallas kernels for 0%

profile of v4, /device:TPU:2, one launch (start us, length us, event | category | flops | bytes accessed | tf_op | source)
XLA Modules:
  0.0 120.1 jit_solution(11523461548291305481)
XLA Ops:
  0.6 5.9 %embed.1 = (bf16[64,1152]{1,0:T(8,128)(2,1)S(1)}, bf16[1024,1024]{1,0:T(8,128)(2,1)}, f32[128,1152]{1,0:T(8,128)}) custom-call(bf16[64,4096]{1,0:T(8,128)(2,1)} %query_ref.1, bf16[64,4096]{1,0:T(8,128)(2,1)} %passage_ref.1, bf16[4096,1024]{1,0:T(8,128)(2,1)} %proj_ref.3, s32[1,64]{1,0:T(1,128)} %bitcast.7), custom_call_target="tpu_custom_call" | custom-call | tf_op jit(solution)/shard_map/embed/pallas_call | solution.py:123
  6.6 7.5 %all-to-all-start = ((bf16[16,64,1024]{2,1,0:T(8,128)(2,1)}), bf16[16,64,1024]{2,1,0:T(8,128)(2,1)S(1)}, u32[]{:S(2)}, u32[]{:S(2)}) async-start(bf16[16,64,1024]{2,1,0:T(8,128)(2,1)} %bitcast.6), calls=%async_computation | async-start | bytes 4194304 | tf_op jit(solution)/shard_map/all_to_all | solution.py:484
  14.1 5.9 %collective-permute-start = (bf16[64,1152]{1,0:T(8,128)(2,1)S(1)}, bf16[64,1152]{1,0:T(8,128)(2,1)S(1)}, u32[]{:S(2)}, u32[]{:S(2)}) collective-permute-start(bf16[64,1152]{1,0:T(8,128)(2,1)S(1)} %get-tuple-element.23.refs_0_), channel_id=1, source_target_pairs={{0,14},{2,0},{4,2},{6,4},{8,6},{10,8},{12,10},{14,12},{1,15},{3,1}... | collective-permute-start | bytes 442376 | tf_op jit(solution)/shard_map/ppermute | solution.py:30
  19.9 2.7 %collective-permute-done.refs_1_ = bf16[64,1152]{1,0:T(8,128)(2,1)S(1)} collective-permute-done((bf16[64,1152]{1,0:T(8,128)(2,1)S(1)}, bf16[64,1152]{1,0:T(8,128)(2,1)S(1)}, u32[]{:S(2)}, u32[]{:S(2)}) %collective-permute-start) | collective-permute-done | bytes 147488 | tf_op jit(solution)/shard_map/ppermute | solution.py:30
  22.6 3.7 %collective-permute-start.1 = (bf16[64,1152]{1,0:T(8,128)(2,1)S(1)}, bf16[64,1152]{1,0:T(8,128)(2,1)S(1)}, u32[]{:S(2)}, u32[]{:S(2)}) collective-permute-start(bf16[64,1152]{1,0:T(8,128)(2,1)S(1)} %collective-permute-done.refs_1_), channel_id=1, source_target_pairs={{0,14},{2,0},{4,2},{6,4},{8,6},{10,8},{12,10},{14,12},{1,15},{3,1}... | collective-permute-start | bytes 442376 | tf_op jit(solution)/shard_map/ppermute | solution.py:30
  26.3 2.7 %collective-permute-done.1.refs_2_ = bf16[64,1152]{1,0:T(8,128)(2,1)S(1)} collective-permute-done((bf16[64,1152]{1,0:T(8,128)(2,1)S(1)}, bf16[64,1152]{1,0:T(8,128)(2,1)S(1)}, u32[]{:S(2)}, u32[]{:S(2)}) %collective-permute-start.1) | collective-permute-done | bytes 147488 | tf_op jit(solution)/shard_map/ppermute | solution.py:30
  29.0 3.7 %collective-permute-start.2 = (bf16[64,1152]{1,0:T(8,128)(2,1)S(1)}, bf16[64,1152]{1,0:T(8,128)(2,1)S(1)}, u32[]{:S(2)}, u32[]{:S(2)}) collective-permute-start(bf16[64,1152]{1,0:T(8,128)(2,1)S(1)} %collective-permute-done.1.refs_2_), channel_id=1, source_target_pairs={{0,14},{2,0},{4,2},{6,4},{8,6},{10,8},{12,10},{14,12},{1,15},{3,1}... | collective-permute-start | bytes 442376 | tf_op jit(solution)/shard_map/ppermute | solution.py:30
  33.2 2.1 %collective-permute-done.2.refs_3_ = bf16[64,1152]{1,0:T(8,128)(2,1)S(1)} collective-permute-done((bf16[64,1152]{1,0:T(8,128)(2,1)S(1)}, bf16[64,1152]{1,0:T(8,128)(2,1)S(1)}, u32[]{:S(2)}, u32[]{:S(2)}) %collective-permute-start.2) | collective-permute-done | bytes 147488 | tf_op jit(solution)/shard_map/ppermute | solution.py:30
  35.3 3.7 %collective-permute-start.3 = (bf16[64,1152]{1,0:T(8,128)(2,1)S(1)}, bf16[64,1152]{1,0:T(8,128)(2,1)S(1)}, u32[]{:S(2)}, u32[]{:S(2)}) collective-permute-start(bf16[64,1152]{1,0:T(8,128)(2,1)S(1)} %collective-permute-done.2.refs_3_), channel_id=1, source_target_pairs={{0,14},{2,0},{4,2},{6,4},{8,6},{10,8},{12,10},{14,12},{1,15},{3,1}... | collective-permute-start | bytes 442376 | tf_op jit(solution)/shard_map/ppermute | solution.py:30
  39.6 1.0 collective-permute-done.6.refs_5_
  40.6 1.0 collective-permute-done.3.refs_4_
  43.4 4.9 %logits.1 = (f32[1024,1024]{1,0:T(8,128)S(1)}, bf16[1024,1152]{1,0:T(8,128)(2,1)S(1)}, f32[16,128]{1,0:T(8,128)S(1)}, f32[1,1024]{1,0:T(1,128)S(1)}) custom-call(bf16[64,1152]{1,0:T(8,128)(2,1)} %copy-done.1, bf16[64,1152]{1,0:T(8,128)(2,1)} %copy-done.2, bf16[64,1152]{1,0:T(8,128)(2,1)} %copy-done.4, bf16[64,1152]{1,0:T(8,128)(2,1)} %copy-done.6, ...), custom_call_target="tpu_custom_call" | custom-call | tf_op jit(solution)/shard_map/logits/pallas_call | solution.py:206
  48.7 2.3 %collective-permute-start.22 = (f32[1,1024]{1,0:T(1,128)S(1)}, f32[1,1024]{1,0:T(1,128)S(1)}, u32[]{:S(2)}, u32[]{:S(2)}) collective-permute-start(f32[1,1024]{1,0:T(1,128)S(1)} %get-tuple-element.27), channel_id=1, source_target_pairs={{0,48},{16,0},{32,16},{48,32},{1,49},{17,1},{33,17},{49,33},{2,50}... | collective-permute-start | bytes 12296 | tf_op jit(solution)/shard_map/ppermute | solution.py:30
  51.6 1.8 %collective-permute-start.20 = (f32[1,1024]{1,0:T(1,128)S(1)}, f32[1,1024]{1,0:T(1,128)S(1)}, u32[]{:S(2)}, u32[]{:S(2)}) collective-permute-start(f32[1,1024]{1,0:T(1,128)S(1)} %get-tuple-element.27), channel_id=1, source_target_pairs={{0,16},{16,32},{32,48},{48,0},{1,17},{17,33},{33,49},{49,1},{2,18}... | collective-permute-start | bytes 12296 | tf_op jit(solution)/shard_map/ppermute | solution.py:30
  53.4 5.0 %collective-permute-start.17 = (f32[16,128]{1,0:T(8,128)S(1)}, f32[16,128]{1,0:T(8,128)S(1)}, u32[]{:S(2)}, u32[]{:S(2)}) collective-permute-start(f32[16,128]{1,0:T(8,128)S(1)} %add.33), channel_id=1, source_target_pairs={{0,14},{2,0},{4,2},{6,4},{8,6},{10,8},{12,10},{14,12},{1,15},{3,1}... | collective-permute-start | bytes 24584 | tf_op jit(solution)/shard_map/ppermute | solution.py:30
  58.4 1.7 %collective-permute-start.25 = (f32[1,1024]{1,0:T(1,128)S(1)}, f32[1,1024]{1,0:T(1,128)S(1)}, u32[]{:S(2)}, u32[]{:S(2)}) collective-permute-start(f32[1,1024]{1,0:T(1,128)S(1)} %add_add_fusion.2), channel_id=1, source_target_pairs={{0,192},{64,0},{128,64},{192,128},{1,193},{65,1},{129,65},{193,129... | collective-permute-start | bytes 12296 | tf_op jit(solution)/shard_map/ppermute | solution.py:30
  60.1 1.1 collective-permute-start.24
  61.2 1.3 %collective-permute-start.23 = (f32[1,1024]{1,0:T(1,128)S(1)}, f32[1,1024]{1,0:T(1,128)S(1)}, u32[]{:S(2)}, u32[]{:S(2)}) collective-permute-start(f32[1,1024]{1,0:T(1,128)S(1)} %add_add_fusion.2), channel_id=1, source_target_pairs={{0,64},{64,128},{128,192},{192,0},{1,65},{65,129},{129,193},{193,1... | collective-permute-start | bytes 12296 | tf_op jit(solution)/shard_map/ppermute | solution.py:30
  63.3 5.0 %collective-permute-start.18 = (f32[16,128]{1,0:T(8,128)S(1)}, f32[16,128]{1,0:T(8,128)S(1)}, u32[]{:S(2)}, u32[]{:S(2)}) collective-permute-start(f32[16,128]{1,0:T(8,128)S(1)} %get-tuple-element.43), channel_id=1, source_target_pairs={{0,10},{2,12},{4,14},{6,0},{8,2},{10,4},{12,6},{14,8},{1,11},{3,13... | collective-permute-start | bytes 24584 | tf_op jit(solution)/shard_map/ppermute | solution.py:30
  68.3 0.8 collective-permute-done.19
  69.6 5.8 %grads.1 = (bf16[16,528,128]{2,1,0:T(8,128)(2,1)}, bf16[8,528,128]{2,1,0:T(8,128)(2,1)}, bf16[8,528,128]{2,1,0:T(8,128)(2,1)}) custom-call(f32[1024,1024]{1,0:T(8,128)S(1)} %get-tuple-element.25.exp_ref, f32[16,128]{1,0:T(8,128)S(1)} %add_add_fusion.row_ref, f32[1,1024]{1,0:T(1,128)S(1)} %add_add_fusion.1.col_ref, ...), custom_call_target="tpu_custom_call" | custom-call | tf_op jit(solution)/shard_map/grads/pallas_call | solution.py:313
  75.4 7.6 %all-to-all-start.1 = ((bf16[16,528,128]{2,1,0:T(8,128)(2,1)}), bf16[16,528,128]{2,1,0:T(8,128)(2,1)}, u32[]{:S(2)}, u32[]{:S(2)}) async-start(bf16[16,528,128]{2,1,0:T(8,128)(2,1)} %get-tuple-element.39), calls=%async_computation.1 | async-start | bytes 4325376 | tf_op jit(solution)/shard_map/all_to_all | solution.py:495
  83.0 2.9 %collective-permute-done.26.refs_1_.refs_3_.refs_5_.refs_4_.other_ref = bf16[8,528,128]{2,1,0:T(8,128)(2,1)S(1)} collective-permute-done((bf16[8,528,128]{2,1,0:T(8,128)(2,1)}, bf16[8,528,128]{2,1,0:T(8,128)(2,1)S(1)}, u32[]{:S(2)}, u32[]{:S(2)}) %collective-permute-start.26) | collective-permute-done | bytes 1081376 | tf_op jit(solution)/shard_map/ppermute | solution.py:34
  86.1 3.3 %collective-permute-start.27 = (bf16[528,128]{1,0:T(8,128)(2,1)S(1)}, bf16[528,128]{1,0:T(8,128)(2,1)S(1)}, u32[]{:S(2)}, u32[]{:S(2)}) collective-permute-start(bf16[528,128]{1,0:T(8,128)(2,1)S(1)} %get-tuple-element.31), channel_id=1, source_target_pairs={{0,14},{2,0},{4,2},{6,4},{8,6},{10,8},{12,10},{14,12},{1,15},{3,1}... | collective-permute-start | bytes 405512 | tf_op jit(solution)/shard_map/ppermute | solution.py:30
  89.4 3.1 %collective-permute-done.27.refs_2_ = bf16[528,128]{1,0:T(8,128)(2,1)S(1)} collective-permute-done((bf16[528,128]{1,0:T(8,128)(2,1)S(1)}, bf16[528,128]{1,0:T(8,128)(2,1)S(1)}, u32[]{:S(2)}, u32[]{:S(2)}) %collective-permute-start.27) | collective-permute-done | bytes 135200 | tf_op jit(solution)/shard_map/ppermute | solution.py:30
  92.5 3.4 %collective-permute-done.28.refs_5_ = bf16[528,128]{1,0:T(8,128)(2,1)S(1)} collective-permute-done((bf16[528,128]{1,0:T(8,128)(2,1)S(1)}, bf16[528,128]{1,0:T(8,128)(2,1)S(1)}, u32[]{:S(2)}, u32[]{:S(2)}) %collective-permute-start.28) | collective-permute-done | bytes 135200 | tf_op jit(solution)/shard_map/ppermute | solution.py:30
  96.4 1.7 %collective-permute-start.30 = (bf16[528,128]{1,0:T(8,128)(2,1)S(1)}, bf16[528,128]{1,0:T(8,128)(2,1)S(1)}, u32[]{:S(2)}, u32[]{:S(2)}) collective-permute-start(bf16[528,128]{1,0:T(8,128)(2,1)S(1)} %get-tuple-element.34), channel_id=1, source_target_pairs={{0,2},{2,4},{4,6},{6,8},{8,10},{10,12},{12,14},{14,0},{1,3},{3,5},... | collective-permute-start | bytes 405512 | tf_op jit(solution)/shard_map/ppermute | solution.py:30
  98.2 3.6 %collective-permute-start.33 = (bf16[528,128]{1,0:T(8,128)(2,1)S(1)}, bf16[528,128]{1,0:T(8,128)(2,1)S(1)}, u32[]{:S(2)}, u32[]{:S(2)}) collective-permute-start(bf16[528,128]{1,0:T(8,128)(2,1)S(1)} %get-tuple-element.37), channel_id=1, source_target_pairs={{0,8},{2,10},{4,12},{6,14},{8,0},{10,2},{12,4},{14,6},{1,9},{3,11}... | collective-permute-start | bytes 405512 | tf_op jit(solution)/shard_map/ppermute | solution.py:30
  101.8 3.2 %collective-permute-done.30.refs_5_ = bf16[528,128]{1,0:T(8,128)(2,1)S(1)} collective-permute-done((bf16[528,128]{1,0:T(8,128)(2,1)S(1)}, bf16[528,128]{1,0:T(8,128)(2,1)S(1)}, u32[]{:S(2)}, u32[]{:S(2)}) %collective-permute-start.30) | collective-permute-done | bytes 135200 | tf_op jit(solution)/shard_map/ppermute | solution.py:30
  105.2 2.0 %collective-permute-start.32 = (bf16[528,128]{1,0:T(8,128)(2,1)S(1)}, bf16[528,128]{1,0:T(8,128)(2,1)S(1)}, u32[]{:S(2)}, u32[]{:S(2)}) collective-permute-start(bf16[528,128]{1,0:T(8,128)(2,1)S(1)} %get-tuple-element.36), channel_id=1, source_target_pairs={{0,2},{2,4},{4,6},{6,8},{8,10},{10,12},{12,14},{14,0},{1,3},{3,5},... | collective-permute-start | bytes 405512 | tf_op jit(solution)/shard_map/ppermute | solution.py:30
  107.2 4.7 %collective-permute-done.33.across_ref = bf16[528,128]{1,0:T(8,128)(2,1)S(1)} collective-permute-done((bf16[528,128]{1,0:T(8,128)(2,1)S(1)}, bf16[528,128]{1,0:T(8,128)(2,1)S(1)}, u32[]{:S(2)}, u32[]{:S(2)}) %collective-permute-start.33) | collective-permute-done | bytes 135200 | tf_op jit(solution)/shard_map/ppermute | solution.py:30
  112.5 7.4 %final.1 = (f32[1,1]{1,0:T(1,128)}, f32[64,4096]{1,0:T(8,128)}, f32[64,4096]{1,0:T(8,128)}) custom-call(bf16[8,528,128]{2,1,0:T(8,128)(2,1)S(1)} %copy-done, bf16[8,528,128]{2,1,0:T(8,128)(2,1)S(1)} %collective-permute-done.26.refs_1_.refs_3_.refs_5_.refs_4_.other_ref, bf16[528,128]{1,0:T(8,128)(2,1)S(1)} %collective-permute-done.31.down_ref, ...), custom_call_target="tpu_custom_call" | custom-call | tf_op jit(solution)/shard_map/final/pallas_call | solution.py:449
  (84 shorter events, 6.7 us)
Async XLA Ops:
  6.6 36.8 %all-to-all-start = ((bf16[16,64,1024]{2,1,0:T(8,128)(2,1)}), bf16[16,64,1024]{2,1,0:T(8,128)(2,1)S(1)}, u32[]{:S(2)}, u32[]{:S(2)}) async-start(bf16[16,64,1024]{2,1,0:T(8,128)(2,1)} %bitcast.6), calls=%async_computation | async-start | bytes 4194304 | tf_op jit(solution)/shard_map/all_to_all | solution.py:484
  14.1 8.5 %collective-permute-start = (bf16[64,1152]{1,0:T(8,128)(2,1)S(1)}, bf16[64,1152]{1,0:T(8,128)(2,1)S(1)}, u32[]{:S(2)}, u32[]{:S(2)}) collective-permute-start(bf16[64,1152]{1,0:T(8,128)(2,1)S(1)} %get-tuple-element.23.refs_0_), channel_id=1, source_target_pairs={{0,14},{2,0},{4,2},{6,4},{8,6},{10,8},{12,10},{14,12},{1,15},{3,1}... | collective-permute-start | bytes 442376 | tf_op jit(solution)/shard_map/ppermute | solution.py:30
  19.9 6.4 %collective-permute-start.4 = (bf16[64,1152]{1,0:T(8,128)(2,1)S(1)}, bf16[64,1152]{1,0:T(8,128)(2,1)S(1)}, u32[]{:S(2)}, u32[]{:S(2)}) collective-permute-start(bf16[64,1152]{1,0:T(8,128)(2,1)S(1)} %get-tuple-element.23.refs_0_), channel_id=1, source_target_pairs={{0,2},{2,4},{4,6},{6,8},{8,10},{10,12},{12,14},{14,0},{1,3},{3,5},... | collective-permute-start | bytes 442376 | tf_op jit(solution)/shard_map/ppermute | solution.py:30
  22.6 6.4 %collective-permute-start.1 = (bf16[64,1152]{1,0:T(8,128)(2,1)S(1)}, bf16[64,1152]{1,0:T(8,128)(2,1)S(1)}, u32[]{:S(2)}, u32[]{:S(2)}) collective-permute-start(bf16[64,1152]{1,0:T(8,128)(2,1)S(1)} %collective-permute-done.refs_1_), channel_id=1, source_target_pairs={{0,14},{2,0},{4,2},{6,4},{8,6},{10,8},{12,10},{14,12},{1,15},{3,1}... | collective-permute-start | bytes 442376 | tf_op jit(solution)/shard_map/ppermute | solution.py:30
  26.3 6.9 %collective-permute-start.5 = (bf16[64,1152]{1,0:T(8,128)(2,1)S(1)}, bf16[64,1152]{1,0:T(8,128)(2,1)S(1)}, u32[]{:S(2)}, u32[]{:S(2)}) collective-permute-start(bf16[64,1152]{1,0:T(8,128)(2,1)S(1)} %collective-permute-done.4.refs_7_), channel_id=1, source_target_pairs={{0,2},{2,4},{4,6},{6,8},{8,10},{10,12},{12,14},{14,0},{1,3},{3,5},... | collective-permute-start | bytes 442376 | tf_op jit(solution)/shard_map/ppermute | solution.py:30
  29.0 6.4 %collective-permute-start.2 = (bf16[64,1152]{1,0:T(8,128)(2,1)S(1)}, bf16[64,1152]{1,0:T(8,128)(2,1)S(1)}, u32[]{:S(2)}, u32[]{:S(2)}) collective-permute-start(bf16[64,1152]{1,0:T(8,128)(2,1)S(1)} %collective-permute-done.1.refs_2_), channel_id=1, source_target_pairs={{0,14},{2,0},{4,2},{6,4},{8,6},{10,8},{12,10},{14,12},{1,15},{3,1}... | collective-permute-start | bytes 442376 | tf_op jit(solution)/shard_map/ppermute | solution.py:30
  32.6 6.4 %collective-permute-start.7 = (bf16[64,1152]{1,0:T(8,128)(2,1)S(1)}, bf16[64,1152]{1,0:T(8,128)(2,1)S(1)}, u32[]{:S(2)}, u32[]{:S(2)}) collective-permute-start(bf16[64,1152]{1,0:T(8,128)(2,1)S(1)} %get-tuple-element.23.refs_0_), channel_id=1, source_target_pairs={{0,1},{1,0},{2,3},{3,2},{4,5},{5,4},{6,7},{7,6},{8,9},{9,8},{10,11... | collective-permute-start | bytes 442376 | tf_op jit(solution)/shard_map/ppermute | solution.py:34
  32.6 6.4 %collective-permute-start.14 = (bf16[64,1152]{1,0:T(8,128)(2,1)S(1)}, bf16[64,1152]{1,0:T(8,128)(2,1)S(1)}, u32[]{:S(2)}, u32[]{:S(2)}) collective-permute-start(bf16[64,1152]{1,0:T(8,128)(2,1)S(1)} %collective-permute-done.4.refs_7_), channel_id=1, source_target_pairs={{0,1},{1,0},{2,3},{3,2},{4,5},{5,4},{6,7},{7,6},{8,9},{9,8},{10,11... | collective-permute-start | bytes 442376 | tf_op jit(solution)/shard_map/ppermute | solution.py:34
  33.1 6.4 %collective-permute-start.8 = (bf16[64,1152]{1,0:T(8,128)(2,1)S(1)}, bf16[64,1152]{1,0:T(8,128)(2,1)S(1)}, u32[]{:S(2)}, u32[]{:S(2)}) collective-permute-start(bf16[64,1152]{1,0:T(8,128)(2,1)S(1)} %collective-permute-done.refs_1_), channel_id=1, source_target_pairs={{0,1},{1,0},{2,3},{3,2},{4,5},{5,4},{6,7},{7,6},{8,9},{9,8},{10,11... | collective-permute-start | bytes 442376 | tf_op jit(solution)/shard_map/ppermute | solution.py:34
  33.2 7.5 %collective-permute-start.6 = (bf16[64,1152]{1,0:T(8,128)(2,1)S(1)}, bf16[64,1152]{1,0:T(8,128)(2,1)S(1)}, u32[]{:S(2)}, u32[]{:S(2)}) collective-permute-start(bf16[64,1152]{1,0:T(8,128)(2,1)S(1)} %collective-permute-done.5.refs_6_), channel_id=1, source_target_pairs={{0,2},{2,4},{4,6},{6,8},{8,10},{10,12},{12,14},{14,0},{1,3},{3,5},... | collective-permute-start | bytes 442376 | tf_op jit(solution)/shard_map/ppermute | solution.py:30
  35.3 6.4 %collective-permute-start.3 = (bf16[64,1152]{1,0:T(8,128)(2,1)S(1)}, bf16[64,1152]{1,0:T(8,128)(2,1)S(1)}, u32[]{:S(2)}, u32[]{:S(2)}) collective-permute-start(bf16[64,1152]{1,0:T(8,128)(2,1)S(1)} %collective-permute-done.2.refs_3_), channel_id=1, source_target_pairs={{0,14},{2,0},{4,2},{6,4},{8,6},{10,8},{12,10},{14,12},{1,15},{3,1}... | collective-permute-start | bytes 442376 | tf_op jit(solution)/shard_map/ppermute | solution.py:30
  39.0 2.7 %collective-permute-start.13 = (bf16[64,1152]{1,0:T(8,128)(2,1)S(1)}, bf16[64,1152]{1,0:T(8,128)(2,1)S(1)}, u32[]{:S(2)}, u32[]{:S(2)}) collective-permute-start(bf16[64,1152]{1,0:T(8,128)(2,1)S(1)} %collective-permute-done.5.refs_6_), channel_id=1, source_target_pairs={{0,1},{1,0},{2,3},{3,2},{4,5},{5,4},{6,7},{7,6},{8,9},{9,8},{10,11... | collective-permute-start | bytes 442376 | tf_op jit(solution)/shard_map/ppermute | solution.py:34
  48.3 5.1 %collective-permute-start.15 = (f32[16,128]{1,0:T(8,128)S(1)}, f32[16,128]{1,0:T(8,128)S(1)}, u32[]{:S(2)}, u32[]{:S(2)}) collective-permute-start(f32[16,128]{1,0:T(8,128)S(1)} %get-tuple-element.26), channel_id=1, source_target_pairs={{0,1},{1,0},{2,3},{3,2},{4,5},{5,4},{6,7},{7,6},{8,9},{9,8},{10,11... | collective-permute-start | bytes 24584 | tf_op jit(solution)/shard_map/ppermute | solution.py:34
  48.7 9.7 %collective-permute-start.22 = (f32[1,1024]{1,0:T(1,128)S(1)}, f32[1,1024]{1,0:T(1,128)S(1)}, u32[]{:S(2)}, u32[]{:S(2)}) collective-permute-start(f32[1,1024]{1,0:T(1,128)S(1)} %get-tuple-element.27), channel_id=1, source_target_pairs={{0,48},{16,0},{32,16},{48,32},{1,49},{17,1},{33,17},{49,33},{2,50}... | collective-permute-start | bytes 12296 | tf_op jit(solution)/shard_map/ppermute | solution.py:30
  51.0 7.4 %collective-permute-start.21 = (f32[1,1024]{1,0:T(1,128)S(1)}, f32[1,1024]{1,0:T(1,128)S(1)}, u32[]{:S(2)}, u32[]{:S(2)}) collective-permute-start(f32[1,1024]{1,0:T(1,128)S(1)} %get-tuple-element.27), channel_id=1, source_target_pairs={{0,32},{16,48},{32,0},{48,16},{1,33},{17,49},{33,1},{49,17},{2,34}... | collective-permute-start | bytes 12296 | tf_op jit(solution)/shard_map/ppermute | solution.py:30
  51.6 6.8 %collective-permute-start.20 = (f32[1,1024]{1,0:T(1,128)S(1)}, f32[1,1024]{1,0:T(1,128)S(1)}, u32[]{:S(2)}, u32[]{:S(2)}) collective-permute-start(f32[1,1024]{1,0:T(1,128)S(1)} %get-tuple-element.27), channel_id=1, source_target_pairs={{0,16},{16,32},{32,48},{48,0},{1,17},{17,33},{33,49},{49,1},{2,18}... | collective-permute-start | bytes 12296 | tf_op jit(solution)/shard_map/ppermute | solution.py:30
  53.4 9.2 %collective-permute-start.17 = (f32[16,128]{1,0:T(8,128)S(1)}, f32[16,128]{1,0:T(8,128)S(1)}, u32[]{:S(2)}, u32[]{:S(2)}) collective-permute-start(f32[16,128]{1,0:T(8,128)S(1)} %add.33), channel_id=1, source_target_pairs={{0,14},{2,0},{4,2},{6,4},{8,6},{10,8},{12,10},{14,12},{1,15},{3,1}... | collective-permute-start | bytes 24584 | tf_op jit(solution)/shard_map/ppermute | solution.py:30
  58.4 4.9 %collective-permute-start.16 = (f32[16,128]{1,0:T(8,128)S(1)}, f32[16,128]{1,0:T(8,128)S(1)}, u32[]{:S(2)}, u32[]{:S(2)}) collective-permute-start(f32[16,128]{1,0:T(8,128)S(1)} %add.33), channel_id=1, source_target_pairs={{0,2},{2,4},{4,6},{6,8},{8,10},{10,12},{12,14},{14,0},{1,3},{3,5},... | collective-permute-start | bytes 24584 | tf_op jit(solution)/shard_map/ppermute | solution.py:30
  58.4 9.8 %collective-permute-start.25 = (f32[1,1024]{1,0:T(1,128)S(1)}, f32[1,1024]{1,0:T(1,128)S(1)}, u32[]{:S(2)}, u32[]{:S(2)}) collective-permute-start(f32[1,1024]{1,0:T(1,128)S(1)} %add_add_fusion.2), channel_id=1, source_target_pairs={{0,192},{64,0},{128,64},{192,128},{1,193},{65,1},{129,65},{193,129... | collective-permute-start | bytes 12296 | tf_op jit(solution)/shard_map/ppermute | solution.py:30
  60.1 8.1 %collective-permute-start.24 = (f32[1,1024]{1,0:T(1,128)S(1)}, f32[1,1024]{1,0:T(1,128)S(1)}, u32[]{:S(2)}, u32[]{:S(2)}) collective-permute-start(f32[1,1024]{1,0:T(1,128)S(1)} %add_add_fusion.2), channel_id=1, source_target_pairs={{0,128},{64,192},{128,0},{192,64},{1,129},{65,193},{129,1},{193,65... | collective-permute-start | bytes 12296 | tf_op jit(solution)/shard_map/ppermute | solution.py:30
  61.2 7.0 %collective-permute-start.23 = (f32[1,1024]{1,0:T(1,128)S(1)}, f32[1,1024]{1,0:T(1,128)S(1)}, u32[]{:S(2)}, u32[]{:S(2)}) collective-permute-start(f32[1,1024]{1,0:T(1,128)S(1)} %add_add_fusion.2), channel_id=1, source_target_pairs={{0,64},{64,128},{128,192},{192,0},{1,65},{65,129},{129,193},{193,1... | collective-permute-start | bytes 12296 | tf_op jit(solution)/shard_map/ppermute | solution.py:30
  63.3 5.8 %collective-permute-start.19 = (f32[16,128]{1,0:T(8,128)S(1)}, f32[16,128]{1,0:T(8,128)S(1)}, u32[]{:S(2)}, u32[]{:S(2)}) collective-permute-start(f32[16,128]{1,0:T(8,128)S(1)} %get-tuple-element.44), channel_id=1, source_target_pairs={{0,4},{2,6},{4,8},{6,10},{8,12},{10,14},{12,0},{14,2},{1,5},{3,7},... | collective-permute-start | bytes 24584 | tf_op jit(solution)/shard_map/ppermute | solution.py:30
  63.3 6.3 %collective-permute-start.18 = (f32[16,128]{1,0:T(8,128)S(1)}, f32[16,128]{1,0:T(8,128)S(1)}, u32[]{:S(2)}, u32[]{:S(2)}) collective-permute-start(f32[16,128]{1,0:T(8,128)S(1)} %get-tuple-element.43), channel_id=1, source_target_pairs={{0,10},{2,12},{4,14},{6,0},{8,2},{10,4},{12,6},{14,8},{1,11},{3,13... | collective-permute-start | bytes 24584 | tf_op jit(solution)/shard_map/ppermute | solution.py:30
  75.4 37.1 %all-to-all-start.1 = ((bf16[16,528,128]{2,1,0:T(8,128)(2,1)}), bf16[16,528,128]{2,1,0:T(8,128)(2,1)}, u32[]{:S(2)}, u32[]{:S(2)}) async-start(bf16[16,528,128]{2,1,0:T(8,128)(2,1)} %get-tuple-element.39), calls=%async_computation.1 | async-start | bytes 4325376 | tf_op jit(solution)/shard_map/all_to_all | solution.py:495
  83.0 2.9 %collective-permute-start.26 = (bf16[8,528,128]{2,1,0:T(8,128)(2,1)}, bf16[8,528,128]{2,1,0:T(8,128)(2,1)S(1)}, u32[]{:S(2)}, u32[]{:S(2)}) collective-permute-start(bf16[8,528,128]{2,1,0:T(8,128)(2,1)} %get-tuple-element.30), channel_id=1, source_target_pairs={{0,1},{1,0},{2,3},{3,2},{4,5},{5,4},{6,7},{7,6},{8,9},{9,8},{10,11... | collective-permute-start | bytes 3244040 | tf_op jit(solution)/shard_map/ppermute | solution.py:34
  86.1 6.5 %collective-permute-start.27 = (bf16[528,128]{1,0:T(8,128)(2,1)S(1)}, bf16[528,128]{1,0:T(8,128)(2,1)S(1)}, u32[]{:S(2)}, u32[]{:S(2)}) collective-permute-start(bf16[528,128]{1,0:T(8,128)(2,1)S(1)} %get-tuple-element.31), channel_id=1, source_target_pairs={{0,14},{2,0},{4,2},{6,4},{8,6},{10,8},{12,10},{14,12},{1,15},{3,1}... | collective-permute-start | bytes 405512 | tf_op jit(solution)/shard_map/ppermute | solution.py:30
  89.4 6.6 %collective-permute-start.28 = (bf16[528,128]{1,0:T(8,128)(2,1)S(1)}, bf16[528,128]{1,0:T(8,128)(2,1)S(1)}, u32[]{:S(2)}, u32[]{:S(2)}) collective-permute-start(bf16[528,128]{1,0:T(8,128)(2,1)S(1)} %get-tuple-element.32), channel_id=1, source_target_pairs={{0,2},{2,4},{4,6},{6,8},{8,10},{10,12},{12,14},{14,0},{1,3},{3,5},... | collective-permute-start | bytes 405512 | tf_op jit(solution)/shard_map/ppermute | solution.py:30
  96.1 5.7 %collective-permute-start.29 = (bf16[528,128]{1,0:T(8,128)(2,1)S(1)}, bf16[528,128]{1,0:T(8,128)(2,1)S(1)}, u32[]{:S(2)}, u32[]{:S(2)}) collective-permute-start(bf16[528,128]{1,0:T(8,128)(2,1)S(1)} %get-tuple-element.33), channel_id=1, source_target_pairs={{0,14},{2,0},{4,2},{6,4},{8,6},{10,8},{12,10},{14,12},{1,15},{3,1}... | collective-permute-start | bytes 405512 | tf_op jit(solution)/shard_map/ppermute | solution.py:30
  96.4 8.5 %collective-permute-start.30 = (bf16[528,128]{1,0:T(8,128)(2,1)S(1)}, bf16[528,128]{1,0:T(8,128)(2,1)S(1)}, u32[]{:S(2)}, u32[]{:S(2)}) collective-permute-start(bf16[528,128]{1,0:T(8,128)(2,1)S(1)} %get-tuple-element.34), channel_id=1, source_target_pairs={{0,2},{2,4},{4,6},{6,8},{8,10},{10,12},{12,14},{14,0},{1,3},{3,5},... | collective-permute-start | bytes 405512 | tf_op jit(solution)/shard_map/ppermute | solution.py:30
  98.2 13.7 %collective-permute-start.33 = (bf16[528,128]{1,0:T(8,128)(2,1)S(1)}, bf16[528,128]{1,0:T(8,128)(2,1)S(1)}, u32[]{:S(2)}, u32[]{:S(2)}) collective-permute-start(bf16[528,128]{1,0:T(8,128)(2,1)S(1)} %get-tuple-element.37), channel_id=1, source_target_pairs={{0,8},{2,10},{4,12},{6,14},{8,0},{10,2},{12,4},{14,6},{1,9},{3,11}... | collective-permute-start | bytes 405512 | tf_op jit(solution)/shard_map/ppermute | solution.py:30
  105.1 6.8 %collective-permute-start.31 = (bf16[528,128]{1,0:T(8,128)(2,1)S(1)}, bf16[528,128]{1,0:T(8,128)(2,1)S(1)}, u32[]{:S(2)}, u32[]{:S(2)}) collective-permute-start(bf16[528,128]{1,0:T(8,128)(2,1)S(1)} %get-tuple-element.35), channel_id=1, source_target_pairs={{0,14},{2,0},{4,2},{6,4},{8,6},{10,8},{12,10},{14,12},{1,15},{3,1}... | collective-permute-start | bytes 405512 | tf_op jit(solution)/shard_map/ppermute | solution.py:30
  105.2 7.3 %collective-permute-start.32 = (bf16[528,128]{1,0:T(8,128)(2,1)S(1)}, bf16[528,128]{1,0:T(8,128)(2,1)S(1)}, u32[]{:S(2)}, u32[]{:S(2)}) collective-permute-start(bf16[528,128]{1,0:T(8,128)(2,1)S(1)} %get-tuple-element.36), channel_id=1, source_target_pairs={{0,2},{2,4},{4,6},{6,8},{8,10},{10,12},{12,14},{14,0},{1,3},{3,5},... | collective-permute-start | bytes 405512 | tf_op jit(solution)/shard_map/ppermute | solution.py:30
  (20 other events, 143.7 us)

commit v5 on v4

--- a/solution.py
+++ b/solution.py
@@ -467,14 +467,12 @@
 
 
 def gather_queries(message):
-    pieces = {0: message}
+    far = NZ // 2
+    pieces = {0: message, far: shift(message, "z", NZ, far)}
     down = up = message
-    for k in range(1, NZ // 2 + 1):
-        down = shift(down, "z", NZ, -1)
-        pieces[k] = down
-        if k < NZ // 2:
-            up = shift(up, "z", NZ, 1)
-            pieces[NZ - k] = up
+    for k in range(1, far):
+        down, up = shift(down, "z", NZ, -1), shift(up, "z", NZ, 1)
+        pieces[k], pieces[NZ - k] = down, up
     own = [pieces[k] for k in range(NZ)]
     return own + [swap(piece, "c", NC, 1) for piece in own]
 

time: 120 us -> 120 us (level)
  starting transfers between devices: 63.4 us -> 64.9 us
  waiting for transfers between devices: 29.8 us -> 28.5 us
    ppermute x24, waiting for transfers between devices: 26.5 us -> 25.2 us  [shift(): lax.ppermute(value, axis, [(i, (i + step) % size) for i in range(size)])]
    ppermute x24, starting transfers between devices: 46.9 us -> 48.2 us  [shift(): lax.ppermute(value, axis, [(i, (i + step) % size) for i in range(size)])]
  transfers between devices with their start and end apart: 36 -> 36, of which waited for: 15 -> 14; matrix products, arithmetic and copies ran while one was open for 0% -> 0% of each run, Pallas kernels for 0% -> 0%
where the time goes in v5:
time: 120 us
  starting transfers between devices  64.9 us (54%)
  waiting for transfers between devices  28.5 us (24%)
  Pallas kernels  24.4 us (20%)
    ppermute x24, starting transfers between devices, shift(): lax.ppermute(value, axis, [(i, (i + step) % size) for i in range(size)])  48.2 us
    ppermute x24, waiting for transfers between devices, shift(): lax.ppermute(value, axis, [(i, (i + step) % size) for i in range(size)])  25.2 us
    all_to_all x1, starting transfers between devices, body(): terms = lax.all_to_all(partial, QR, 0, 0, tiled=True)  7.58 us
    all_to_all x1, starting transfers between devices, body(): passage_tile = lax.all_to_all(copies, QR, 0, 0, tiled=True)  7.49 us
    pallas_call x1, Pallas kernels, final(): pl.pallas_call(functools.partial(final_kernel, count), grid=(1,), in_spec...  7.37 us
    pallas_call x1, Pallas kernels, embed(): pl.pallas_call(embed_kernel, in_specs=[HBM] * 4, out_specs=[VMEM, HBM, HB...  5.92 us
    pallas_call x1, Pallas kernels, tile_grads(): pl.pallas_call(grads_kernel, in_specs=[VMEM] * 5, out_specs=[HBM] * 3, ou...  5.78 us
    pallas_call x1, Pallas kernels, tile_logits(): pl.pallas_call(logits_kernel, in_specs=[HBM] * len(pieces) + [VMEM], out_...  4.89 us
  transfers between devices with their start and end apart: 36, of which 14 were waited for; matrix products, arithmetic and copies ran while one was open for 0% of the time, Pallas kernels for 0%

profile of v5, /device:TPU:2, one launch (start us, length us, event | category | flops | bytes accessed | tf_op | source)
XLA Modules:
  0.0 120.1 jit_solution(5402509808810985910)
XLA Ops:
  0.6 5.9 %embed.1 = (bf16[64,1152]{1,0:T(8,128)(2,1)S(1)}, bf16[1024,1024]{1,0:T(8,128)(2,1)}, f32[128,1152]{1,0:T(8,128)}) custom-call(bf16[64,4096]{1,0:T(8,128)(2,1)} %query_ref.1, bf16[64,4096]{1,0:T(8,128)(2,1)} %passage_ref.1, bf16[4096,1024]{1,0:T(8,128)(2,1)} %proj_ref.3, s32[1,64]{1,0:T(1,128)} %bitcast.7), custom_call_target="tpu_custom_call" | custom-call | tf_op jit(solution)/shard_map/embed/pallas_call | solution.py:123
  6.6 7.5 %all-to-all-start = ((bf16[16,64,1024]{2,1,0:T(8,128)(2,1)}), bf16[16,64,1024]{2,1,0:T(8,128)(2,1)S(1)}, u32[]{:S(2)}, u32[]{:S(2)}) async-start(bf16[16,64,1024]{2,1,0:T(8,128)(2,1)} %bitcast.6), calls=%async_computation | async-start | bytes 4194304 | tf_op jit(solution)/shard_map/all_to_all | solution.py:482
  14.1 1.9 %collective-permute-start.4 = (bf16[64,1152]{1,0:T(8,128)(2,1)S(1)}, bf16[64,1152]{1,0:T(8,128)(2,1)S(1)}, u32[]{:S(2)}, u32[]{:S(2)}) collective-permute-start(bf16[64,1152]{1,0:T(8,128)(2,1)S(1)} %get-tuple-element.23.refs_0_), channel_id=1, source_target_pairs={{0,2},{2,4},{4,6},{6,8},{8,10},{10,12},{12,14},{14,0},{1,3},{3,5},... | collective-permute-start | bytes 442376 | tf_op jit(solution)/shard_map/ppermute | solution.py:30
  16.0 4.0 %collective-permute-start = (bf16[64,1152]{1,0:T(8,128)(2,1)S(1)}, bf16[64,1152]{1,0:T(8,128)(2,1)S(1)}, u32[]{:S(2)}, u32[]{:S(2)}) collective-permute-start(bf16[64,1152]{1,0:T(8,128)(2,1)S(1)} %get-tuple-element.23.refs_0_), channel_id=1, source_target_pairs={{0,14},{2,0},{4,2},{6,4},{8,6},{10,8},{12,10},{14,12},{1,15},{3,1}... | collective-permute-start | bytes 442376 | tf_op jit(solution)/shard_map/ppermute | solution.py:30
  20.0 4.5 %collective-permute-start.3 = (bf16[64,1152]{1,0:T(8,128)(2,1)S(1)}, bf16[64,1152]{1,0:T(8,128)(2,1)S(1)}, u32[]{:S(2)}, u32[]{:S(2)}) collective-permute-start(bf16[64,1152]{1,0:T(8,128)(2,1)S(1)} %get-tuple-element.23.refs_0_), channel_id=1, source_target_pairs={{0,8},{2,10},{4,12},{6,14},{8,0},{10,2},{12,4},{14,6},{1,9},{3,11}... | collective-permute-start | bytes 442376 | tf_op jit(solution)/shard_map/ppermute | solution.py:30
  24.5 3.9 %collective-permute-start.1 = (bf16[64,1152]{1,0:T(8,128)(2,1)S(1)}, bf16[64,1152]{1,0:T(8,128)(2,1)S(1)}, u32[]{:S(2)}, u32[]{:S(2)}) collective-permute-start(bf16[64,1152]{1,0:T(8,128)(2,1)S(1)} %collective-permute-done.refs_1_), channel_id=1, source_target_pairs={{0,14},{2,0},{4,2},{6,4},{8,6},{10,8},{12,10},{14,12},{1,15},{3,1}... | collective-permute-start | bytes 442376 | tf_op jit(solution)/shard_map/ppermute | solution.py:30
  28.9 3.6 %collective-permute-done.3.refs_4_ = bf16[64,1152]{1,0:T(8,128)(2,1)S(1)} collective-permute-done((bf16[64,1152]{1,0:T(8,128)(2,1)S(1)}, bf16[64,1152]{1,0:T(8,128)(2,1)S(1)}, u32[]{:S(2)}, u32[]{:S(2)}) %collective-permute-start.3) | collective-permute-done | bytes 147488 | tf_op jit(solution)/shard_map/ppermute | solution.py:30
  32.5 1.1 collective-permute-done.5.refs_6_
  33.6 1.4 %collective-permute-start.6 = (bf16[64,1152]{1,0:T(8,128)(2,1)S(1)}, bf16[64,1152]{1,0:T(8,128)(2,1)S(1)}, u32[]{:S(2)}, u32[]{:S(2)}) collective-permute-start(bf16[64,1152]{1,0:T(8,128)(2,1)S(1)} %collective-permute-done.5.refs_6_), channel_id=1, source_target_pairs={{0,2},{2,4},{4,6},{6,8},{8,10},{10,12},{12,14},{14,0},{1,3},{3,5},... | collective-permute-start | bytes 442376 | tf_op jit(solution)/shard_map/ppermute | solution.py:30
  35.0 1.8 %collective-permute-start.2 = (bf16[64,1152]{1,0:T(8,128)(2,1)S(1)}, bf16[64,1152]{1,0:T(8,128)(2,1)S(1)}, u32[]{:S(2)}, u32[]{:S(2)}) collective-permute-start(bf16[64,1152]{1,0:T(8,128)(2,1)S(1)} %collective-permute-done.1.refs_2_), channel_id=1, source_target_pairs={{0,14},{2,0},{4,2},{6,4},{8,6},{10,8},{12,10},{14,12},{1,15},{3,1}... | collective-permute-start | bytes 442376 | tf_op jit(solution)/shard_map/ppermute | solution.py:30
  37.5 2.5 %collective-permute-done.6.refs_5_ = bf16[64,1152]{1,0:T(8,128)(2,1)S(1)} collective-permute-done((bf16[64,1152]{1,0:T(8,128)(2,1)S(1)}, bf16[64,1152]{1,0:T(8,128)(2,1)S(1)}, u32[]{:S(2)}, u32[]{:S(2)}) %collective-permute-start.6) | collective-permute-done | bytes 147488 | tf_op jit(solution)/shard_map/ppermute | solution.py:30
  40.0 1.0 collective-permute-done.2.refs_3_
  42.5 4.9 %logits.1 = (f32[1024,1024]{1,0:T(8,128)S(1)}, bf16[1024,1152]{1,0:T(8,128)(2,1)S(1)}, f32[16,128]{1,0:T(8,128)S(1)}, f32[1,1024]{1,0:T(1,128)S(1)}) custom-call(bf16[64,1152]{1,0:T(8,128)(2,1)} %copy-done.1, bf16[64,1152]{1,0:T(8,128)(2,1)} %copy-done.3, bf16[64,1152]{1,0:T(8,128)(2,1)} %copy-done.6, bf16[64,1152]{1,0:T(8,128)(2,1)} %copy-done.11, ...), custom_call_target="tpu_custom_call" | custom-call | tf_op jit(solution)/shard_map/logits/pallas_call | solution.py:206
  48.0 3.0 %collective-permute-start.22 = (f32[1,1024]{1,0:T(1,128)S(1)}, f32[1,1024]{1,0:T(1,128)S(1)}, u32[]{:S(2)}, u32[]{:S(2)}) collective-permute-start(f32[1,1024]{1,0:T(1,128)S(1)} %get-tuple-element.27), channel_id=1, source_target_pairs={{0,48},{16,0},{32,16},{48,32},{1,49},{17,1},{33,17},{49,33},{2,50}... | collective-permute-start | bytes 12296 | tf_op jit(solution)/shard_map/ppermute | solution.py:30
  51.0 1.7 %collective-permute-start.20 = (f32[1,1024]{1,0:T(1,128)S(1)}, f32[1,1024]{1,0:T(1,128)S(1)}, u32[]{:S(2)}, u32[]{:S(2)}) collective-permute-start(f32[1,1024]{1,0:T(1,128)S(1)} %get-tuple-element.27), channel_id=1, source_target_pairs={{0,16},{16,32},{32,48},{48,0},{1,17},{17,33},{33,49},{49,1},{2,18}... | collective-permute-start | bytes 12296 | tf_op jit(solution)/shard_map/ppermute | solution.py:30
  52.7 5.7 %collective-permute-start.17 = (f32[16,128]{1,0:T(8,128)S(1)}, f32[16,128]{1,0:T(8,128)S(1)}, u32[]{:S(2)}, u32[]{:S(2)}) collective-permute-start(f32[16,128]{1,0:T(8,128)S(1)} %add.33), channel_id=1, source_target_pairs={{0,14},{2,0},{4,2},{6,4},{8,6},{10,8},{12,10},{14,12},{1,15},{3,1}... | collective-permute-start | bytes 24584 | tf_op jit(solution)/shard_map/ppermute | solution.py:30
  58.4 1.7 %collective-permute-start.25 = (f32[1,1024]{1,0:T(1,128)S(1)}, f32[1,1024]{1,0:T(1,128)S(1)}, u32[]{:S(2)}, u32[]{:S(2)}) collective-permute-start(f32[1,1024]{1,0:T(1,128)S(1)} %add_add_fusion.2), channel_id=1, source_target_pairs={{0,192},{64,0},{128,64},{192,128},{1,193},{65,1},{129,65},{193,129... | collective-permute-start | bytes 12296 | tf_op jit(solution)/shard_map/ppermute | solution.py:30
  60.1 1.1 collective-permute-start.24
  61.2 1.3 %collective-permute-start.23 = (f32[1,1024]{1,0:T(1,128)S(1)}, f32[1,1024]{1,0:T(1,128)S(1)}, u32[]{:S(2)}, u32[]{:S(2)}) collective-permute-start(f32[1,1024]{1,0:T(1,128)S(1)} %add_add_fusion.2), channel_id=1, source_target_pairs={{0,64},{64,128},{128,192},{192,0},{1,65},{65,129},{129,193},{193,1... | collective-permute-start | bytes 12296 | tf_op jit(solution)/shard_map/ppermute | solution.py:30
  63.3 5.0 %collective-permute-start.18 = (f32[16,128]{1,0:T(8,128)S(1)}, f32[16,128]{1,0:T(8,128)S(1)}, u32[]{:S(2)}, u32[]{:S(2)}) collective-permute-start(f32[16,128]{1,0:T(8,128)S(1)} %get-tuple-element.43), channel_id=1, source_target_pairs={{0,10},{2,12},{4,14},{6,0},{8,2},{10,4},{12,6},{14,8},{1,11},{3,13... | collective-permute-start | bytes 24584 | tf_op jit(solution)/shard_map/ppermute | solution.py:30
  69.6 5.8 %grads.1 = (bf16[16,528,128]{2,1,0:T(8,128)(2,1)}, bf16[8,528,128]{2,1,0:T(8,128)(2,1)}, bf16[8,528,128]{2,1,0:T(8,128)(2,1)}) custom-call(f32[1024,1024]{1,0:T(8,128)S(1)} %get-tuple-element.25.exp_ref, f32[16,128]{1,0:T(8,128)S(1)} %add_add_fusion.row_ref, f32[1,1024]{1,0:T(1,128)S(1)} %add_add_fusion.1.col_ref, ...), custom_call_target="tpu_custom_call" | custom-call | tf_op jit(solution)/shard_map/grads/pallas_call | solution.py:313
  75.4 7.6 %all-to-all-start.1 = ((bf16[16,528,128]{2,1,0:T(8,128)(2,1)}), bf16[16,528,128]{2,1,0:T(8,128)(2,1)}, u32[]{:S(2)}, u32[]{:S(2)}) async-start(bf16[16,528,128]{2,1,0:T(8,128)(2,1)} %get-tuple-element.39), calls=%async_computation.1 | async-start | bytes 4325376 | tf_op jit(solution)/shard_map/all_to_all | solution.py:493
  83.0 2.9 %collective-permute-done.26.refs_1_.refs_3_.refs_5_.refs_4_.other_ref = bf16[8,528,128]{2,1,0:T(8,128)(2,1)S(1)} collective-permute-done((bf16[8,528,128]{2,1,0:T(8,128)(2,1)}, bf16[8,528,128]{2,1,0:T(8,128)(2,1)S(1)}, u32[]{:S(2)}, u32[]{:S(2)}) %collective-permute-start.26) | collective-permute-done | bytes 1081376 | tf_op jit(solution)/shard_map/ppermute | solution.py:34
  86.1 3.3 %collective-permute-start.27 = (bf16[528,128]{1,0:T(8,128)(2,1)S(1)}, bf16[528,128]{1,0:T(8,128)(2,1)S(1)}, u32[]{:S(2)}, u32[]{:S(2)}) collective-permute-start(bf16[528,128]{1,0:T(8,128)(2,1)S(1)} %get-tuple-element.31), channel_id=1, source_target_pairs={{0,14},{2,0},{4,2},{6,4},{8,6},{10,8},{12,10},{14,12},{1,15},{3,1}... | collective-permute-start | bytes 405512 | tf_op jit(solution)/shard_map/ppermute | solution.py:30
  89.4 3.1 %collective-permute-done.27.refs_2_ = bf16[528,128]{1,0:T(8,128)(2,1)S(1)} collective-permute-done((bf16[528,128]{1,0:T(8,128)(2,1)S(1)}, bf16[528,128]{1,0:T(8,128)(2,1)S(1)}, u32[]{:S(2)}, u32[]{:S(2)}) %collective-permute-start.27) | collective-permute-done | bytes 135200 | tf_op jit(solution)/shard_map/ppermute | solution.py:30
  92.5 3.4 %collective-permute-done.28.refs_5_ = bf16[528,128]{1,0:T(8,128)(2,1)S(1)} collective-permute-done((bf16[528,128]{1,0:T(8,128)(2,1)S(1)}, bf16[528,128]{1,0:T(8,128)(2,1)S(1)}, u32[]{:S(2)}, u32[]{:S(2)}) %collective-permute-start.28) | collective-permute-done | bytes 135200 | tf_op jit(solution)/shard_map/ppermute | solution.py:30
  96.4 1.7 %collective-permute-start.30 = (bf16[528,128]{1,0:T(8,128)(2,1)S(1)}, bf16[528,128]{1,0:T(8,128)(2,1)S(1)}, u32[]{:S(2)}, u32[]{:S(2)}) collective-permute-start(bf16[528,128]{1,0:T(8,128)(2,1)S(1)} %get-tuple-element.34), channel_id=1, source_target_pairs={{0,2},{2,4},{4,6},{6,8},{8,10},{10,12},{12,14},{14,0},{1,3},{3,5},... | collective-permute-start | bytes 405512 | tf_op jit(solution)/shard_map/ppermute | solution.py:30
  98.2 3.6 %collective-permute-start.33 = (bf16[528,128]{1,0:T(8,128)(2,1)S(1)}, bf16[528,128]{1,0:T(8,128)(2,1)S(1)}, u32[]{:S(2)}, u32[]{:S(2)}) collective-permute-start(bf16[528,128]{1,0:T(8,128)(2,1)S(1)} %get-tuple-element.37), channel_id=1, source_target_pairs={{0,8},{2,10},{4,12},{6,14},{8,0},{10,2},{12,4},{14,6},{1,9},{3,11}... | collective-permute-start | bytes 405512 | tf_op jit(solution)/shard_map/ppermute | solution.py:30
  101.8 3.2 %collective-permute-done.30.refs_5_ = bf16[528,128]{1,0:T(8,128)(2,1)S(1)} collective-permute-done((bf16[528,128]{1,0:T(8,128)(2,1)S(1)}, bf16[528,128]{1,0:T(8,128)(2,1)S(1)}, u32[]{:S(2)}, u32[]{:S(2)}) %collective-permute-start.30) | collective-permute-done | bytes 135200 | tf_op jit(solution)/shard_map/ppermute | solution.py:30
  105.2 2.0 %collective-permute-start.32 = (bf16[528,128]{1,0:T(8,128)(2,1)S(1)}, bf16[528,128]{1,0:T(8,128)(2,1)S(1)}, u32[]{:S(2)}, u32[]{:S(2)}) collective-permute-start(bf16[528,128]{1,0:T(8,128)(2,1)S(1)} %get-tuple-element.36), channel_id=1, source_target_pairs={{0,2},{2,4},{4,6},{6,8},{8,10},{10,12},{12,14},{14,0},{1,3},{3,5},... | collective-permute-start | bytes 405512 | tf_op jit(solution)/shard_map/ppermute | solution.py:30
  107.2 4.7 %collective-permute-done.33.across_ref = bf16[528,128]{1,0:T(8,128)(2,1)S(1)} collective-permute-done((bf16[528,128]{1,0:T(8,128)(2,1)S(1)}, bf16[528,128]{1,0:T(8,128)(2,1)S(1)}, u32[]{:S(2)}, u32[]{:S(2)}) %collective-permute-start.33) | collective-permute-done | bytes 135200 | tf_op jit(solution)/shard_map/ppermute | solution.py:30
  112.5 7.4 %final.1 = (f32[1,1]{1,0:T(1,128)}, f32[64,4096]{1,0:T(8,128)}, f32[64,4096]{1,0:T(8,128)}) custom-call(bf16[8,528,128]{2,1,0:T(8,128)(2,1)S(1)} %copy-done, bf16[8,528,128]{2,1,0:T(8,128)(2,1)S(1)} %collective-permute-done.26.refs_1_.refs_3_.refs_5_.refs_4_.other_ref, bf16[528,128]{1,0:T(8,128)(2,1)S(1)} %collective-permute-done.31.down_ref, ...), custom_call_target="tpu_custom_call" | custom-call | tf_op jit(solution)/shard_map/final/pallas_call | solution.py:449
  (84 shorter events, 6.7 us)
Async XLA Ops:
  6.6 35.9 %all-to-all-start = ((bf16[16,64,1024]{2,1,0:T(8,128)(2,1)}), bf16[16,64,1024]{2,1,0:T(8,128)(2,1)S(1)}, u32[]{:S(2)}, u32[]{:S(2)}) async-start(bf16[16,64,1024]{2,1,0:T(8,128)(2,1)} %bitcast.6), calls=%async_computation | async-start | bytes 4194304 | tf_op jit(solution)/shard_map/all_to_all | solution.py:482
  14.1 10.4 %collective-permute-start.4 = (bf16[64,1152]{1,0:T(8,128)(2,1)S(1)}, bf16[64,1152]{1,0:T(8,128)(2,1)S(1)}, u32[]{:S(2)}, u32[]{:S(2)}) collective-permute-start(bf16[64,1152]{1,0:T(8,128)(2,1)S(1)} %get-tuple-element.23.refs_0_), channel_id=1, source_target_pairs={{0,2},{2,4},{4,6},{6,8},{8,10},{10,12},{12,14},{14,0},{1,3},{3,5},... | collective-permute-start | bytes 442376 | tf_op jit(solution)/shard_map/ppermute | solution.py:30
  16.0 8.5 %collective-permute-start = (bf16[64,1152]{1,0:T(8,128)(2,1)S(1)}, bf16[64,1152]{1,0:T(8,128)(2,1)S(1)}, u32[]{:S(2)}, u32[]{:S(2)}) collective-permute-start(bf16[64,1152]{1,0:T(8,128)(2,1)S(1)} %get-tuple-element.23.refs_0_), channel_id=1, source_target_pairs={{0,14},{2,0},{4,2},{6,4},{8,6},{10,8},{12,10},{14,12},{1,15},{3,1}... | collective-permute-start | bytes 442376 | tf_op jit(solution)/shard_map/ppermute | solution.py:30
  20.0 12.4 %collective-permute-start.3 = (bf16[64,1152]{1,0:T(8,128)(2,1)S(1)}, bf16[64,1152]{1,0:T(8,128)(2,1)S(1)}, u32[]{:S(2)}, u32[]{:S(2)}) collective-permute-start(bf16[64,1152]{1,0:T(8,128)(2,1)S(1)} %get-tuple-element.23.refs_0_), channel_id=1, source_target_pairs={{0,8},{2,10},{4,12},{6,14},{8,0},{10,2},{12,4},{14,6},{1,9},{3,11}... | collective-permute-start | bytes 442376 | tf_op jit(solution)/shard_map/ppermute | solution.py:30
  24.5 9.1 %collective-permute-start.5 = (bf16[64,1152]{1,0:T(8,128)(2,1)S(1)}, bf16[64,1152]{1,0:T(8,128)(2,1)S(1)}, u32[]{:S(2)}, u32[]{:S(2)}) collective-permute-start(bf16[64,1152]{1,0:T(8,128)(2,1)S(1)} %collective-permute-done.4.refs_7_), channel_id=1, source_target_pairs={{0,2},{2,4},{4,6},{6,8},{8,10},{10,12},{12,14},{14,0},{1,3},{3,5},... | collective-permute-start | bytes 442376 | tf_op jit(solution)/shard_map/ppermute | solution.py:30
  24.5 10.5 %collective-permute-start.1 = (bf16[64,1152]{1,0:T(8,128)(2,1)S(1)}, bf16[64,1152]{1,0:T(8,128)(2,1)S(1)}, u32[]{:S(2)}, u32[]{:S(2)}) collective-permute-start(bf16[64,1152]{1,0:T(8,128)(2,1)S(1)} %collective-permute-done.refs_1_), channel_id=1, source_target_pairs={{0,14},{2,0},{4,2},{6,4},{8,6},{10,8},{12,10},{14,12},{1,15},{3,1}... | collective-permute-start | bytes 442376 | tf_op jit(solution)/shard_map/ppermute | solution.py:30
  28.4 8.5 %collective-permute-start.7 = (bf16[64,1152]{1,0:T(8,128)(2,1)S(1)}, bf16[64,1152]{1,0:T(8,128)(2,1)S(1)}, u32[]{:S(2)}, u32[]{:S(2)}) collective-permute-start(bf16[64,1152]{1,0:T(8,128)(2,1)S(1)} %get-tuple-element.23.refs_0_), channel_id=1, source_target_pairs={{0,1},{1,0},{2,3},{3,2},{4,5},{5,4},{6,7},{7,6},{8,9},{9,8},{10,11... | collective-permute-start | bytes 442376 | tf_op jit(solution)/shard_map/ppermute | solution.py:34
  28.4 8.5 %collective-permute-start.14 = (bf16[64,1152]{1,0:T(8,128)(2,1)S(1)}, bf16[64,1152]{1,0:T(8,128)(2,1)S(1)}, u32[]{:S(2)}, u32[]{:S(2)}) collective-permute-start(bf16[64,1152]{1,0:T(8,128)(2,1)S(1)} %collective-permute-done.4.refs_7_), channel_id=1, source_target_pairs={{0,1},{1,0},{2,3},{3,2},{4,5},{5,4},{6,7},{7,6},{8,9},{9,8},{10,11... | collective-permute-start | bytes 442376 | tf_op jit(solution)/shard_map/ppermute | solution.py:34
  32.5 4.9 %collective-permute-start.11 = (bf16[64,1152]{1,0:T(8,128)(2,1)S(1)}, bf16[64,1152]{1,0:T(8,128)(2,1)S(1)}, u32[]{:S(2)}, u32[]{:S(2)}) collective-permute-start(bf16[64,1152]{1,0:T(8,128)(2,1)S(1)} %collective-permute-done.3.refs_4_), channel_id=1, source_target_pairs={{0,1},{1,0},{2,3},{3,2},{4,5},{5,4},{6,7},{7,6},{8,9},{9,8},{10,11... | collective-permute-start | bytes 442376 | tf_op jit(solution)/shard_map/ppermute | solution.py:34
  33.6 6.4 %collective-permute-start.6 = (bf16[64,1152]{1,0:T(8,128)(2,1)S(1)}, bf16[64,1152]{1,0:T(8,128)(2,1)S(1)}, u32[]{:S(2)}, u32[]{:S(2)}) collective-permute-start(bf16[64,1152]{1,0:T(8,128)(2,1)S(1)} %collective-permute-done.5.refs_6_), channel_id=1, source_target_pairs={{0,2},{2,4},{4,6},{6,8},{8,10},{10,12},{12,14},{14,0},{1,3},{3,5},... | collective-permute-start | bytes 442376 | tf_op jit(solution)/shard_map/ppermute | solution.py:30
  35.0 5.9 %collective-permute-start.2 = (bf16[64,1152]{1,0:T(8,128)(2,1)S(1)}, bf16[64,1152]{1,0:T(8,128)(2,1)S(1)}, u32[]{:S(2)}, u32[]{:S(2)}) collective-permute-start(bf16[64,1152]{1,0:T(8,128)(2,1)S(1)} %collective-permute-done.1.refs_2_), channel_id=1, source_target_pairs={{0,14},{2,0},{4,2},{6,4},{8,6},{10,8},{12,10},{14,12},{1,15},{3,1}... | collective-permute-start | bytes 442376 | tf_op jit(solution)/shard_map/ppermute | solution.py:30
  36.8 4.1 %collective-permute-start.8 = (bf16[64,1152]{1,0:T(8,128)(2,1)S(1)}, bf16[64,1152]{1,0:T(8,128)(2,1)S(1)}, u32[]{:S(2)}, u32[]{:S(2)}) collective-permute-start(bf16[64,1152]{1,0:T(8,128)(2,1)S(1)} %collective-permute-done.refs_1_), channel_id=1, source_target_pairs={{0,1},{1,0},{2,3},{3,2},{4,5},{5,4},{6,7},{7,6},{8,9},{9,8},{10,11... | collective-permute-start | bytes 442376 | tf_op jit(solution)/shard_map/ppermute | solution.py:34
  36.9 4.1 %collective-permute-start.13 = (bf16[64,1152]{1,0:T(8,128)(2,1)S(1)}, bf16[64,1152]{1,0:T(8,128)(2,1)S(1)}, u32[]{:S(2)}, u32[]{:S(2)}) collective-permute-start(bf16[64,1152]{1,0:T(8,128)(2,1)S(1)} %collective-permute-done.5.refs_6_), channel_id=1, source_target_pairs={{0,1},{1,0},{2,3},{3,2},{4,5},{5,4},{6,7},{7,6},{8,9},{9,8},{10,11... | collective-permute-start | bytes 442376 | tf_op jit(solution)/shard_map/ppermute | solution.py:34
  47.4 5.2 %collective-permute-start.15 = (f32[16,128]{1,0:T(8,128)S(1)}, f32[16,128]{1,0:T(8,128)S(1)}, u32[]{:S(2)}, u32[]{:S(2)}) collective-permute-start(f32[16,128]{1,0:T(8,128)S(1)} %get-tuple-element.26), channel_id=1, source_target_pairs={{0,1},{1,0},{2,3},{3,2},{4,5},{5,4},{6,7},{7,6},{8,9},{9,8},{10,11... | collective-permute-start | bytes 24584 | tf_op jit(solution)/shard_map/ppermute | solution.py:34
  48.0 10.4 %collective-permute-start.22 = (f32[1,1024]{1,0:T(1,128)S(1)}, f32[1,1024]{1,0:T(1,128)S(1)}, u32[]{:S(2)}, u32[]{:S(2)}) collective-permute-start(f32[1,1024]{1,0:T(1,128)S(1)} %get-tuple-element.27), channel_id=1, source_target_pairs={{0,48},{16,0},{32,16},{48,32},{1,49},{17,1},{33,17},{49,33},{2,50}... | collective-permute-start | bytes 12296 | tf_op jit(solution)/shard_map/ppermute | solution.py:30
  51.0 7.4 %collective-permute-start.21 = (f32[1,1024]{1,0:T(1,128)S(1)}, f32[1,1024]{1,0:T(1,128)S(1)}, u32[]{:S(2)}, u32[]{:S(2)}) collective-permute-start(f32[1,1024]{1,0:T(1,128)S(1)} %get-tuple-element.27), channel_id=1, source_target_pairs={{0,32},{16,48},{32,0},{48,16},{1,33},{17,49},{33,1},{49,17},{2,34}... | collective-permute-start | bytes 12296 | tf_op jit(solution)/shard_map/ppermute | solution.py:30
  51.0 7.4 %collective-permute-start.20 = (f32[1,1024]{1,0:T(1,128)S(1)}, f32[1,1024]{1,0:T(1,128)S(1)}, u32[]{:S(2)}, u32[]{:S(2)}) collective-permute-start(f32[1,1024]{1,0:T(1,128)S(1)} %get-tuple-element.27), channel_id=1, source_target_pairs={{0,16},{16,32},{32,48},{48,0},{1,17},{17,33},{33,49},{49,1},{2,18}... | collective-permute-start | bytes 12296 | tf_op jit(solution)/shard_map/ppermute | solution.py:30
  52.7 9.9 %collective-permute-start.17 = (f32[16,128]{1,0:T(8,128)S(1)}, f32[16,128]{1,0:T(8,128)S(1)}, u32[]{:S(2)}, u32[]{:S(2)}) collective-permute-start(f32[16,128]{1,0:T(8,128)S(1)} %add.33), channel_id=1, source_target_pairs={{0,14},{2,0},{4,2},{6,4},{8,6},{10,8},{12,10},{14,12},{1,15},{3,1}... | collective-permute-start | bytes 24584 | tf_op jit(solution)/shard_map/ppermute | solution.py:30
  58.4 4.9 %collective-permute-start.16 = (f32[16,128]{1,0:T(8,128)S(1)}, f32[16,128]{1,0:T(8,128)S(1)}, u32[]{:S(2)}, u32[]{:S(2)}) collective-permute-start(f32[16,128]{1,0:T(8,128)S(1)} %add.33), channel_id=1, source_target_pairs={{0,2},{2,4},{4,6},{6,8},{8,10},{10,12},{12,14},{14,0},{1,3},{3,5},... | collective-permute-start | bytes 24584 | tf_op jit(solution)/shard_map/ppermute | solution.py:30
  58.4 9.8 %collective-permute-start.25 = (f32[1,1024]{1,0:T(1,128)S(1)}, f32[1,1024]{1,0:T(1,128)S(1)}, u32[]{:S(2)}, u32[]{:S(2)}) collective-permute-start(f32[1,1024]{1,0:T(1,128)S(1)} %add_add_fusion.2), channel_id=1, source_target_pairs={{0,192},{64,0},{128,64},{192,128},{1,193},{65,1},{129,65},{193,129... | collective-permute-start | bytes 12296 | tf_op jit(solution)/shard_map/ppermute | solution.py:30
  60.1 8.1 %collective-permute-start.24 = (f32[1,1024]{1,0:T(1,128)S(1)}, f32[1,1024]{1,0:T(1,128)S(1)}, u32[]{:S(2)}, u32[]{:S(2)}) collective-permute-start(f32[1,1024]{1,0:T(1,128)S(1)} %add_add_fusion.2), channel_id=1, source_target_pairs={{0,128},{64,192},{128,0},{192,64},{1,129},{65,193},{129,1},{193,65... | collective-permute-start | bytes 12296 | tf_op jit(solution)/shard_map/ppermute | solution.py:30
  61.2 7.0 %collective-permute-start.23 = (f32[1,1024]{1,0:T(1,128)S(1)}, f32[1,1024]{1,0:T(1,128)S(1)}, u32[]{:S(2)}, u32[]{:S(2)}) collective-permute-start(f32[1,1024]{1,0:T(1,128)S(1)} %add_add_fusion.2), channel_id=1, source_target_pairs={{0,64},{64,128},{128,192},{192,0},{1,65},{65,129},{129,193},{193,1... | collective-permute-start | bytes 12296 | tf_op jit(solution)/shard_map/ppermute | solution.py:30
  63.3 5.8 %collective-permute-start.19 = (f32[16,128]{1,0:T(8,128)S(1)}, f32[16,128]{1,0:T(8,128)S(1)}, u32[]{:S(2)}, u32[]{:S(2)}) collective-permute-start(f32[16,128]{1,0:T(8,128)S(1)} %get-tuple-element.44), channel_id=1, source_target_pairs={{0,4},{2,6},{4,8},{6,10},{8,12},{10,14},{12,0},{14,2},{1,5},{3,7},... | collective-permute-start | bytes 24584 | tf_op jit(solution)/shard_map/ppermute | solution.py:30
  63.3 6.3 %collective-permute-start.18 = (f32[16,128]{1,0:T(8,128)S(1)}, f32[16,128]{1,0:T(8,128)S(1)}, u32[]{:S(2)}, u32[]{:S(2)}) collective-permute-start(f32[16,128]{1,0:T(8,128)S(1)} %get-tuple-element.43), channel_id=1, source_target_pairs={{0,10},{2,12},{4,14},{6,0},{8,2},{10,4},{12,6},{14,8},{1,11},{3,13... | collective-permute-start | bytes 24584 | tf_op jit(solution)/shard_map/ppermute | solution.py:30
  75.4 37.1 %all-to-all-start.1 = ((bf16[16,528,128]{2,1,0:T(8,128)(2,1)}), bf16[16,528,128]{2,1,0:T(8,128)(2,1)}, u32[]{:S(2)}, u32[]{:S(2)}) async-start(bf16[16,528,128]{2,1,0:T(8,128)(2,1)} %get-tuple-element.39), calls=%async_computation.1 | async-start | bytes 4325376 | tf_op jit(solution)/shard_map/all_to_all | solution.py:493
  86.1 6.5 %collective-permute-start.27 = (bf16[528,128]{1,0:T(8,128)(2,1)S(1)}, bf16[528,128]{1,0:T(8,128)(2,1)S(1)}, u32[]{:S(2)}, u32[]{:S(2)}) collective-permute-start(bf16[528,128]{1,0:T(8,128)(2,1)S(1)} %get-tuple-element.31), channel_id=1, source_target_pairs={{0,14},{2,0},{4,2},{6,4},{8,6},{10,8},{12,10},{14,12},{1,15},{3,1}... | collective-permute-start | bytes 405512 | tf_op jit(solution)/shard_map/ppermute | solution.py:30
  89.4 6.6 %collective-permute-start.28 = (bf16[528,128]{1,0:T(8,128)(2,1)S(1)}, bf16[528,128]{1,0:T(8,128)(2,1)S(1)}, u32[]{:S(2)}, u32[]{:S(2)}) collective-permute-start(bf16[528,128]{1,0:T(8,128)(2,1)S(1)} %get-tuple-element.32), channel_id=1, source_target_pairs={{0,2},{2,4},{4,6},{6,8},{8,10},{10,12},{12,14},{14,0},{1,3},{3,5},... | collective-permute-start | bytes 405512 | tf_op jit(solution)/shard_map/ppermute | solution.py:30
  96.1 5.7 %collective-permute-start.29 = (bf16[528,128]{1,0:T(8,128)(2,1)S(1)}, bf16[528,128]{1,0:T(8,128)(2,1)S(1)}, u32[]{:S(2)}, u32[]{:S(2)}) collective-permute-start(bf16[528,128]{1,0:T(8,128)(2,1)S(1)} %get-tuple-element.33), channel_id=1, source_target_pairs={{0,14},{2,0},{4,2},{6,4},{8,6},{10,8},{12,10},{14,12},{1,15},{3,1}... | collective-permute-start | bytes 405512 | tf_op jit(solution)/shard_map/ppermute | solution.py:30
  96.4 8.5 %collective-permute-start.30 = (bf16[528,128]{1,0:T(8,128)(2,1)S(1)}, bf16[528,128]{1,0:T(8,128)(2,1)S(1)}, u32[]{:S(2)}, u32[]{:S(2)}) collective-permute-start(bf16[528,128]{1,0:T(8,128)(2,1)S(1)} %get-tuple-element.34), channel_id=1, source_target_pairs={{0,2},{2,4},{4,6},{6,8},{8,10},{10,12},{12,14},{14,0},{1,3},{3,5},... | collective-permute-start | bytes 405512 | tf_op jit(solution)/shard_map/ppermute | solution.py:30
  98.2 13.7 %collective-permute-start.33 = (bf16[528,128]{1,0:T(8,128)(2,1)S(1)}, bf16[528,128]{1,0:T(8,128)(2,1)S(1)}, u32[]{:S(2)}, u32[]{:S(2)}) collective-permute-start(bf16[528,128]{1,0:T(8,128)(2,1)S(1)} %get-tuple-element.37), channel_id=1, source_target_pairs={{0,8},{2,10},{4,12},{6,14},{8,0},{10,2},{12,4},{14,6},{1,9},{3,11}... | collective-permute-start | bytes 405512 | tf_op jit(solution)/shard_map/ppermute | solution.py:30
  105.1 6.8 %collective-permute-start.31 = (bf16[528,128]{1,0:T(8,128)(2,1)S(1)}, bf16[528,128]{1,0:T(8,128)(2,1)S(1)}, u32[]{:S(2)}, u32[]{:S(2)}) collective-permute-start(bf16[528,128]{1,0:T(8,128)(2,1)S(1)} %get-tuple-element.35), channel_id=1, source_target_pairs={{0,14},{2,0},{4,2},{6,4},{8,6},{10,8},{12,10},{14,12},{1,15},{3,1}... | collective-permute-start | bytes 405512 | tf_op jit(solution)/shard_map/ppermute | solution.py:30
  105.2 7.3 %collective-permute-start.32 = (bf16[528,128]{1,0:T(8,128)(2,1)S(1)}, bf16[528,128]{1,0:T(8,128)(2,1)S(1)}, u32[]{:S(2)}, u32[]{:S(2)}) collective-permute-start(bf16[528,128]{1,0:T(8,128)(2,1)S(1)} %get-tuple-element.36), channel_id=1, source_target_pairs={{0,2},{2,4},{4,6},{6,8},{8,10},{10,12},{12,14},{14,0},{1,3},{3,5},... | collective-permute-start | bytes 405512 | tf_op jit(solution)/shard_map/ppermute | solution.py:30
  (20 other events, 139.6 us)
